TPU v7x, 32 devices: a whole 2x2x4 slice. The times are simulated.
32 devices in a mesh: seq: 4 (over y, x), dp: 8 (over z, core).
Axes of the slice: x: 2, y: 2, z: 4, core: 2. Of those that a mesh axis runs over, the one named last changes fastest.
Arguments:
- tokens_in: bfloat16 [8, 2048, 1024], P('dp', 'seq'), may hold values from -8 to 8, as said below
- out_grad: bfloat16 [8, 2048, 1024], P('dp', 'seq'), may hold values from -6 to 6
- first_gain: bfloat16 [1024], P(('seq', 'dp')), may hold values from 0.25 to 1.75
- first_shift: bfloat16 [1024], P(('seq', 'dp')), may hold values from -1.75 to 1.75
- input_weight: bfloat16 [1024, 3072], P(('seq', 'dp')), may hold values from -0.1875 to 0.1875
- input_bias: bfloat16 [2048], P(('seq', 'dp')), may hold values from -3 to 3
- output_weight: bfloat16 [1024, 1024], P(('seq', 'dp')), may hold values from -0.75 to 0.75
- output_bias: bfloat16 [1024], P(('seq', 'dp')), may hold values from -3 to 3
- second_gain: bfloat16 [1024], P(('seq', 'dp')), may hold values from 0.25 to 1.75
- second_shift: bfloat16 [1024], P(('seq', 'dp')), may hold values from -1.75 to 1.75
- up_weight: bfloat16 [1024, 4096], P(('seq', 'dp')), may hold values from -0.1875 to 0.1875
- up_bias: bfloat16 [4096], P(('seq', 'dp')), may hold values from -3 to 3
- down_weight: bfloat16 [4096, 1024], P(('seq', 'dp')), may hold values from -0.09375 to 0.09375
- down_bias: bfloat16 [1024], P(('seq', 'dp')), may hold values from -3 to 3
Outputs:
- layer_out: bfloat16 [8, 2048, 1024], P('dp', 'seq')
- tokens_grad: float32 [8, 2048, 1024], P('dp', 'seq')
- grad_first_gain: float32 [1024], P(('seq', 'dp'))
- grad_first_shift: float32 [1024], P(('seq', 'dp'))
- grad_input_weight: float32 [1024, 3072], P(('seq', 'dp'))
- grad_input_bias: float32 [2048], P(('seq', 'dp'))
- grad_output_weight: float32 [1024, 1024], P(('seq', 'dp'))
- grad_output_bias: float32 [1024], P(('seq', 'dp'))
- grad_second_gain: float32 [1024], P(('seq', 'dp'))
- grad_second_shift: float32 [1024], P(('seq', 'dp'))
- grad_up_weight: float32 [1024, 4096], P(('seq', 'dp'))
- grad_up_bias: float32 [4096], P(('seq', 'dp'))
- grad_down_weight: float32 [4096, 1024], P(('seq', 'dp'))
- grad_down_bias: float32 [1024], P(('seq', 'dp'))
Inputs may be any that keep to these rules, and one draw needn't show every extreme that they name: `tokens_in`: the block's.
All inputs are finite; a program needn't handle non-finite values.
Results may differ from a plain program's by a relative error of at most 0.0082.
Values may be sent and summed in bfloat16 or wider, within the bound.
No kernel may reach another device: no remote copies, remote signals or barrier semaphores. Data moves between devices by JAX's collectives and lax.ppermute only.
A program may use at most 192 MiB of HBM per device.

v0:
```python
import jax
import jax.numpy as jnp
from jax import lax
from jax.sharding import PartitionSpec as P

HEADS = 16
HEAD = 64


EPSILON = 1e-05


def layer_norm(values, norm_gain, norm_shift):
    centre = values - jnp.mean(values, axis=-1, keepdims=True)
    spread = jnp.mean(centre * centre, axis=-1, keepdims=True)
    return centre * lax.rsqrt(spread + EPSILON) * norm_gain + norm_shift


def tanh_gelu(upper_in):
    return jax.nn.gelu(upper_in, approximate=True)


def head_slopes(first_head, head_count, head_total):
    head_ids = (first_head + jnp.arange(head_count, dtype=jnp.int32)).astype(jnp.float32)
    return jnp.exp2(-8.0 * (head_ids + 1.0) / head_total)


def block_scores(query_rows, key_heads, row_start, slopes, score_scale):
    raw_scores = jnp.einsum(
        "sqhe,skhe->shqk", query_rows, key_heads, preferred_element_type=jnp.float32
    )
    row_place = row_start + jnp.arange(query_rows.shape[1], dtype=jnp.int32)
    col_place = jnp.arange(key_heads.shape[1], dtype=jnp.int32)
    offset = (row_place[:, None] - col_place[None, :]).astype(jnp.float32)
    scores = raw_scores * score_scale - slopes[:, None, None] * offset
    return jnp.where(offset >= 0, scores, -jnp.inf)


def body(
    tokens_in,
    out_grad,
    first_gain,
    first_shift,
    input_weight,
    input_bias,
    output_weight,
    output_bias,
    second_gain,
    second_shift,
    up_weight,
    up_bias,
    down_weight,
    down_bias,
):
    gathered = (
        lax.all_gather(first_gain, ("seq", "dp"), axis=0, tiled=True),
        lax.all_gather(first_shift, ("seq", "dp"), axis=0, tiled=True),
        lax.all_gather(input_weight, ("seq", "dp"), axis=0, tiled=True),
        lax.all_gather(input_bias, ("seq", "dp"), axis=0, tiled=True),
        lax.all_gather(output_weight, ("seq", "dp"), axis=0, tiled=True),
        lax.all_gather(output_bias, ("seq", "dp"), axis=0, tiled=True),
        lax.all_gather(second_gain, ("seq", "dp"), axis=0, tiled=True),
        lax.all_gather(second_shift, ("seq", "dp"), axis=0, tiled=True),
        lax.all_gather(up_weight, ("seq", "dp"), axis=0, tiled=True),
        lax.all_gather(up_bias, ("seq", "dp"), axis=0, tiled=True),
        lax.all_gather(down_weight, ("seq", "dp"), axis=0, tiled=True),
        lax.all_gather(down_bias, ("seq", "dp"), axis=0, tiled=True),
    )
    gain_first = gathered[0].astype(jnp.float32)
    shift_first = gathered[1].astype(jnp.float32)
    weight_input = gathered[2]
    bias_input = gathered[3].astype(jnp.float32)
    weight_output = gathered[4]
    bias_output = gathered[5].astype(jnp.float32)
    gain_second = gathered[6].astype(jnp.float32)
    shift_second = gathered[7].astype(jnp.float32)
    weight_up = gathered[8]
    bias_up = gathered[9].astype(jnp.float32)
    weight_down = gathered[10]
    bias_down = gathered[11].astype(jnp.float32)
    model_width = tokens_in.shape[-1]
    inputs = tokens_in.astype(jnp.float32)
    normed_float, first_back = jax.vjp(layer_norm, inputs, gain_first, shift_first)
    normed = normed_float.astype(jnp.bfloat16)
    projected = jnp.dot(normed, weight_input, preferred_element_type=jnp.float32)
    query_tokens = (projected[..., :model_width] + bias_input[:model_width]).astype(jnp.bfloat16)
    key_tokens = projected[..., model_width : 2 * model_width].astype(jnp.bfloat16)
    value_tokens = (projected[..., 2 * model_width :] + bias_input[model_width:]).astype(
        jnp.bfloat16
    )
    query_split, key_split, value_split = (
        lax.all_to_all(query_tokens, "seq", split_axis=2, concat_axis=1, tiled=True),
        lax.all_to_all(key_tokens, "seq", split_axis=2, concat_axis=1, tiled=True),
        lax.all_to_all(value_tokens, "seq", split_axis=2, concat_axis=1, tiled=True),
    )
    seq_count, full_length, head_width = query_split.shape
    head_group = head_width // HEAD
    query_heads = query_split.reshape(seq_count, full_length, head_group, HEAD)
    key_heads = key_split.reshape(seq_count, full_length, head_group, HEAD)
    value_heads = value_split.reshape(seq_count, full_length, head_group, HEAD)
    slopes = head_slopes(lax.axis_index("seq") * head_group, head_group, HEADS)
    score_scale = HEAD ** (-0.5)
    block_rows = min(512, full_length)
    block_count = full_length // block_rows

    def forward_block(block_index):
        row_start = block_index * block_rows
        query_rows = lax.dynamic_slice_in_dim(query_heads, row_start, block_rows, 1)
        scores = block_scores(query_rows, key_heads, row_start, slopes, score_scale)
        row_peak = jnp.max(scores, axis=-1, keepdims=True)
        exponent = jnp.exp(scores - row_peak)
        row_total = jnp.sum(exponent, axis=-1, keepdims=True)
        probs_low = (exponent / row_total).astype(jnp.bfloat16)
        context_rows = jnp.einsum(
            "shqk,skhe->sqhe", probs_low, value_heads, preferred_element_type=jnp.float32
        )
        return (context_rows.astype(jnp.bfloat16), (row_peak + jnp.log(row_total))[..., 0])

    context_blocks, log_totals = lax.map(forward_block, jnp.arange(block_count, dtype=jnp.int32))
    context_split = jnp.moveaxis(context_blocks, 0, 1).reshape(seq_count, full_length, head_width)
    context = lax.all_to_all(context_split, "seq", split_axis=1, concat_axis=2, tiled=True)
    branch = jnp.dot(context, weight_output, preferred_element_type=jnp.float32) + bias_output
    residual = inputs + branch
    normed_two_float, second_back = jax.vjp(layer_norm, residual, gain_second, shift_second)
    normed_two = normed_two_float.astype(jnp.bfloat16)
    upper = jnp.dot(normed_two, weight_up, preferred_element_type=jnp.float32) + bias_up
    activated, gelu_back = jax.vjp(tanh_gelu, upper)
    hidden = activated.astype(jnp.bfloat16)
    layer_out = (
        residual + jnp.dot(hidden, weight_down, preferred_element_type=jnp.float32) + bias_down
    ).astype(jnp.bfloat16)
    upstream = out_grad.astype(jnp.float32)
    grad_down_weight = jnp.einsum(
        "std,ste->de", hidden, out_grad, preferred_element_type=jnp.float32
    )
    grad_down_bias = jnp.sum(upstream, axis=(0, 1))
    grad_hidden = jnp.einsum(
        "ste,de->std", out_grad, weight_down, preferred_element_type=jnp.float32
    )
    grad_upper = gelu_back(grad_hidden)[0]
    upper_low = grad_upper.astype(jnp.bfloat16)
    grad_up_weight = jnp.einsum(
        "std,stf->df", normed_two, upper_low, preferred_element_type=jnp.float32
    )
    grad_up_bias = jnp.sum(grad_upper, axis=(0, 1))
    grad_normed_two = jnp.einsum(
        "stf,df->std", upper_low, weight_up, preferred_element_type=jnp.float32
    )
    grad_through, grad_second_gain, grad_second_shift = second_back(grad_normed_two)
    grad_residual = upstream + grad_through
    branch_low = grad_residual.astype(jnp.bfloat16)
    grad_output_weight = jnp.einsum(
        "std,ste->de", context, branch_low, preferred_element_type=jnp.float32
    )
    grad_output_bias = jnp.sum(grad_residual, axis=(0, 1))
    context_grad = jnp.einsum(
        "ste,de->std", branch_low, weight_output, preferred_element_type=jnp.float32
    ).astype(jnp.bfloat16)
    grad_split = lax.all_to_all(context_grad, "seq", split_axis=2, concat_axis=1, tiled=True)
    grad_heads = grad_split.reshape(seq_count, full_length, head_group, HEAD)

    def backward_block(carried, block_index):
        key_sum, value_sum = carried
        row_start = block_index * block_rows
        query_rows = lax.dynamic_slice_in_dim(query_heads, row_start, block_rows, 1)
        grad_rows = lax.dynamic_slice_in_dim(grad_heads, row_start, block_rows, 1)
        scores = block_scores(query_rows, key_heads, row_start, slopes, score_scale)
        soft_probs = jnp.exp(scores - log_totals[block_index][..., None])
        value_sum = value_sum + jnp.einsum(
            "shqk,sqhe->skhe",
            soft_probs.astype(jnp.bfloat16),
            grad_rows,
            preferred_element_type=jnp.float32,
        )
        prob_grad = jnp.einsum(
            "sqhe,skhe->shqk", grad_rows, value_heads, preferred_element_type=jnp.float32
        )
        inner_sum = jnp.sum(soft_probs * prob_grad, axis=-1, keepdims=True)
        score_grad = (soft_probs * (prob_grad - inner_sum) * score_scale).astype(jnp.bfloat16)
        query_rows_grad = jnp.einsum(
            "shqk,skhe->sqhe", score_grad, key_heads, preferred_element_type=jnp.float32
        )
        key_sum = key_sum + jnp.einsum(
            "shqk,sqhe->skhe", score_grad, query_rows, preferred_element_type=jnp.float32
        )
        return ((key_sum, value_sum), query_rows_grad.astype(jnp.bfloat16))

    empty_grad = jnp.zeros(key_heads.shape, jnp.float32)
    (key_total, value_total), query_blocks = lax.scan(
        backward_block, (empty_grad, empty_grad), jnp.arange(block_count, dtype=jnp.int32)
    )
    query_grad_split = jnp.moveaxis(query_blocks, 0, 1).reshape(seq_count, full_length, head_width)
    key_grad_split = key_total.reshape(seq_count, full_length, head_width).astype(jnp.bfloat16)
    value_grad_split = value_total.reshape(seq_count, full_length, head_width).astype(jnp.bfloat16)
    query_grad, key_grad, value_grad = (
        lax.all_to_all(query_grad_split, "seq", split_axis=1, concat_axis=2, tiled=True),
        lax.all_to_all(key_grad_split, "seq", split_axis=1, concat_axis=2, tiled=True),
        lax.all_to_all(value_grad_split, "seq", split_axis=1, concat_axis=2, tiled=True),
    )
    grad_projected = jnp.concatenate((query_grad, key_grad, value_grad), axis=-1)
    grad_input_weight = jnp.einsum(
        "std,ste->de", normed, grad_projected, preferred_element_type=jnp.float32
    )
    grad_input_bias = jnp.concatenate(
        (
            jnp.sum(query_grad.astype(jnp.float32), axis=(0, 1)),
            jnp.sum(value_grad.astype(jnp.float32), axis=(0, 1)),
        )
    )
    grad_normed = jnp.einsum(
        "ste,de->std", grad_projected, weight_input, preferred_element_type=jnp.float32
    )
    grad_entry, grad_first_gain, grad_first_shift = first_back(grad_normed)
    tokens_grad = grad_residual + grad_entry
    owned = (
        lax.psum_scatter(grad_first_gain, ("seq", "dp"), scatter_dimension=0, tiled=True),
        lax.psum_scatter(grad_first_shift, ("seq", "dp"), scatter_dimension=0, tiled=True),
        lax.psum_scatter(grad_input_weight, ("seq", "dp"), scatter_dimension=0, tiled=True),
        lax.psum_scatter(grad_input_bias, ("seq", "dp"), scatter_dimension=0, tiled=True),
        lax.psum_scatter(grad_output_weight, ("seq", "dp"), scatter_dimension=0, tiled=True),
        lax.psum_scatter(grad_output_bias, ("seq", "dp"), scatter_dimension=0, tiled=True),
        lax.psum_scatter(grad_second_gain, ("seq", "dp"), scatter_dimension=0, tiled=True),
        lax.psum_scatter(grad_second_shift, ("seq", "dp"), scatter_dimension=0, tiled=True),
        lax.psum_scatter(grad_up_weight, ("seq", "dp"), scatter_dimension=0, tiled=True),
        lax.psum_scatter(grad_up_bias, ("seq", "dp"), scatter_dimension=0, tiled=True),
        lax.psum_scatter(grad_down_weight, ("seq", "dp"), scatter_dimension=0, tiled=True),
        lax.psum_scatter(grad_down_bias, ("seq", "dp"), scatter_dimension=0, tiled=True),
    )
    return (
        layer_out,
        tokens_grad,
        owned[0],
        owned[1],
        owned[2],
        owned[3],
        owned[4],
        owned[5],
        owned[6],
        owned[7],
        owned[8],
        owned[9],
        owned[10],
        owned[11],
    )


def solution(mesh):
    placed = (
        P("dp", "seq", None),
        P("dp", "seq", None),
        P(("seq", "dp")),
        P(("seq", "dp")),
        P(("seq", "dp"), None),
        P(("seq", "dp")),
        P(("seq", "dp"), None),
        P(("seq", "dp")),
        P(("seq", "dp")),
        P(("seq", "dp")),
        P(("seq", "dp"), None),
        P(("seq", "dp")),
        P(("seq", "dp"), None),
        P(("seq", "dp")),
    )
    return jax.shard_map(
        body,
        mesh=mesh,
        in_specs=placed,
        out_specs=(
            P("dp", "seq", None),
            P("dp", "seq", None),
            P(("seq", "dp")),
            P(("seq", "dp")),
            P(("seq", "dp"), None),
            P(("seq", "dp")),
            P(("seq", "dp"), None),
            P(("seq", "dp")),
            P(("seq", "dp")),
            P(("seq", "dp")),
            P(("seq", "dp"), None),
            P(("seq", "dp")),
            P(("seq", "dp"), None),
            P(("seq", "dp")),
        ),
        check_vma=False,
    )
```

profile of v0, /device:TPU:0, one launch (start us, length us, event | category | flops | bytes accessed | tf_op | source)
XLA Modules:
  0.0 1357.1 jit_solution(16838269105665266919)
XLA Ops:
  15.3 42.5 %all-reduce.16 = (bf16[1024]{0:T(1024)(128)(2,1)S(1)}, bf16[1024]{0:T(1024)(128)(2,1)S(1)}, bf16[2048]{0:T(1024)(128)(2,1)S(1)}, bf16[1024]{0:T(1024)(128)(2,1)}...) all-reduce(bf16[1024]{0:T(1024)(128)(2,1)S(1)} %dynamic-update-slic, ...), channel_id=1, replica_groups=mesh['seq'=4,'dp'=8] {'seq','dp'}, use_global_device_ids=true, to_apply=%add.1 | all-reduce | flops 8192 | bytes 32768
  61.6 21.9 %all-gather.6.cloned.1.call-done = bf16[1024,3072]{1,0:T(8,128)(2,1)} async-done(((bf16[32,3072]{1,0:T(8,128)(2,1)}), bf16[1024,3072]{1,0:T(8,128)(2,1)}) %all-gather.6.cloned.1.call-update) | async-done | bytes 6291472 | tf_op jit(solution)/shard_map/all_gather | solution.py:58
  83.5 6.1 convolution_bitcast_fusion
  95.0 7.0 reduce.26
  110.5 4.6 copy.96
  115.2 8.0 reduce.25
  126.9 4.7 all-to-all-start.1
  131.6 4.6 copy.94
  136.3 8.0 reduce.24
  164.1 4.5 all-to-all-done
  177.9 92.3 %while.28 = (s32[]{:T(128)}, bf16[4,1,512,4,64]{2,4,3,1,0:T(8,128)(2,1)}, f32[4,1,4,512]{3,2,1,0:T(4,128)S(1)}, s32[4]{0:T(128)S(1)}, bf16[1,2048,4,64]{1,3,2,0:...) while((s32[]{:T(128)}, ...), condition=%wide.region_5.6_spmd.clone, body=%wide.region_2.5_spmd.clone.sunk | while | flops 1154611712 | bytes 94968136 | solution.py:119
  180.6 6.3 fusion.160
  186.9 5.8 fusion.161
  192.7 8.3 fusion.162
  203.6 6.3 fusion.160
  210.0 5.8 fusion.161
  215.8 8.3 fusion.162
  226.6 6.3 fusion.160
  233.0 5.8 fusion.161
  238.8 8.4 fusion.162
  249.7 6.3 fusion.160
  256.1 5.8 fusion.161
  261.8 8.3 fusion.162
  274.5 8.3 reshape.490
  282.8 12.1 reduce.27
  300.9 40.3 %all-gather = bf16[32,1,128]{2,1,0:T(2,128)(2,1)S(1)} all-gather(bf16[1,1,128]{2,1,0:T(2,128)(2,1)S(1)} %bitcast.285), channel_id=1, replica_groups=mesh['seq'=4,'dp'=8] {'seq','dp'}, dimensions={0}, use_global_device_ids=true | all-gather | bytes 8448 | tf_op jit(solution)/shard_map/all_gather | solution.py:65
  351.1 10.6 fusion.122
  361.8 14.0 %fusion.128 = (f32[4096]{0:T(1024)}, bf16[512,4096]{1,0:T(8,128)(2,1)S(1)}) fusion(f32[512,4096]{1,0:T(8,128)} %fusion.122, f32[4096]{0:T(1024)S(1)} %bitcast.280, bf16[4096,1024]{1,0:T(8,128)(2,1)} %all-gather.12.cloned.1.call-done, bf16[1,512,1024]{2,1,0:T(8,128)(2,1)S(1)} %copy-done.16), kind=kOutput, calls=%fused_computation.149 | convolution fusion | flops 4341100544 | bytes 22052864 | tf_op jit(solution)/shard_map/ste,de->std/dot_general | solution.py:137
  375.8 5.4 fusion.90
  389.1 8.1 reduce.28
  405.2 5.3 fusion.103
  410.5 9.1 all-to-all-done.4
  431.1 286.8 %while.29 = (s32[]{:T(128)}, f32[1,2048,4,64]{1,3,2,0:T(8,128)}, f32[1,2048,4,64]{1,3,2,0:T(8,128)S(1)}, bf16[4,1,512,4,64]{2,4,3,1,0:T(8,128)(2,1)}, s32[4]{0:T...) while((s32[]{:T(128)}, f32[1,2048,4,64]{1,3,2,0:T(8,128)}, ...), condition=%wide.region_12.13_spmd.clone, body=%wide.region_10.12_spmd.clone.sunk | while | flops 2758943232 | bytes 279214464 | solution.py:189
  435.9 6.8 subtract_exponential_fusion.3
  448.4 8.1 fusion.173
  456.5 22.9 %fusion.176 = bf16[4,1,512,4,64]{2,4,3,1,0:T(8,128)(2,1)} fusion(bf16[4,1,512,4,64]{2,4,3,1,0:T(8,128)(2,1)} %get-tuple-element.431, s32[]{:T(128)S(6)} %copy.149, f32[4,512,2048]{2,1,0:T(8,128)} %copy-done, f32[4,512,2048]{2,1,0:T(8,128)} %fusion.173, bf16[1,2048,4,64]{1,3,2,0:T(8,128)(2,1)} %get-tuple-element.450), kind=kOutput, calls=%fused_computation.41.clone.1 | convolution fusion | flops 557977600 | bytes 68419584 | tf_op jit(solution)/shard_map/while/body/eval_jaxpr/shqk,skhe->sqhe/dot_general | solution.py:180
  479.4 23.5 %fusion.174 = f32[1,2048,4,64]{1,3,2,0:T(8,128)} fusion(f32[4,512,2048]{2,1,0:T(8,128)} %copy-done, f32[4,512,2048]{2,1,0:T(8,128)} %fusion.173, f32[1,2048,4,64]{1,3,2,0:T(8,128)} %get-tuple-element.429, pred[]{:T(512)S(6)} %compare.3, bf16[1,2048,4,64]{1,3,2,0:T(8,128)(2,1)} %get-tuple-element.449, s32[]{:T(128)S(6)} %select_n.52), kind=kOutput, calls=%fused_computation.36.clone.1 | convolution fusion | flops 558895104 | bytes 71565320 | tf_op jit(solution)/shard_map/while/body/eval_jaxpr/shqk,sqhe->skhe/dot_general | solution.py:183
  507.3 6.8 subtract_exponential_fusion.3
  519.9 8.1 fusion.173
  527.9 22.8 %fusion.176 = bf16[4,1,512,4,64]{2,4,3,1,0:T(8,128)(2,1)} fusion(bf16[4,1,512,4,64]{2,4,3,1,0:T(8,128)(2,1)} %get-tuple-element.431, s32[]{:T(128)S(6)} %copy.149, f32[4,512,2048]{2,1,0:T(8,128)} %copy-done, f32[4,512,2048]{2,1,0:T(8,128)} %fusion.173, bf16[1,2048,4,64]{1,3,2,0:T(8,128)(2,1)} %get-tuple-element.450), kind=kOutput, calls=%fused_computation.41.clone.1 | convolution fusion | flops 557977600 | bytes 68419584 | tf_op jit(solution)/shard_map/while/body/eval_jaxpr/shqk,skhe->sqhe/dot_general | solution.py:180
  550.8 23.9 %fusion.174 = f32[1,2048,4,64]{1,3,2,0:T(8,128)} fusion(f32[4,512,2048]{2,1,0:T(8,128)} %copy-done, f32[4,512,2048]{2,1,0:T(8,128)} %fusion.173, f32[1,2048,4,64]{1,3,2,0:T(8,128)} %get-tuple-element.429, pred[]{:T(512)S(6)} %compare.3, bf16[1,2048,4,64]{1,3,2,0:T(8,128)(2,1)} %get-tuple-element.449, s32[]{:T(128)S(6)} %select_n.52), kind=kOutput, calls=%fused_computation.36.clone.1 | convolution fusion | flops 558895104 | bytes 71565320 | tf_op jit(solution)/shard_map/while/body/eval_jaxpr/shqk,sqhe->skhe/dot_general | solution.py:183
  579.1 6.8 subtract_exponential_fusion.3
  591.6 8.1 fusion.173
  599.7 22.6 %fusion.176 = bf16[4,1,512,4,64]{2,4,3,1,0:T(8,128)(2,1)} fusion(bf16[4,1,512,4,64]{2,4,3,1,0:T(8,128)(2,1)} %get-tuple-element.431, s32[]{:T(128)S(6)} %copy.149, f32[4,512,2048]{2,1,0:T(8,128)} %copy-done, f32[4,512,2048]{2,1,0:T(8,128)} %fusion.173, bf16[1,2048,4,64]{1,3,2,0:T(8,128)(2,1)} %get-tuple-element.450), kind=kOutput, calls=%fused_computation.41.clone.1 | convolution fusion | flops 557977600 | bytes 68419584 | tf_op jit(solution)/shard_map/while/body/eval_jaxpr/shqk,skhe->sqhe/dot_general | solution.py:180
  622.3 23.9 %fusion.174 = f32[1,2048,4,64]{1,3,2,0:T(8,128)} fusion(f32[4,512,2048]{2,1,0:T(8,128)} %copy-done, f32[4,512,2048]{2,1,0:T(8,128)} %fusion.173, f32[1,2048,4,64]{1,3,2,0:T(8,128)} %get-tuple-element.429, pred[]{:T(512)S(6)} %compare.3, bf16[1,2048,4,64]{1,3,2,0:T(8,128)(2,1)} %get-tuple-element.449, s32[]{:T(128)S(6)} %select_n.52), kind=kOutput, calls=%fused_computation.36.clone.1 | convolution fusion | flops 558895104 | bytes 71565320 | tf_op jit(solution)/shard_map/while/body/eval_jaxpr/shqk,sqhe->skhe/dot_general | solution.py:183
  650.6 6.8 subtract_exponential_fusion.3
  663.1 8.1 fusion.173
  671.2 22.6 %fusion.176 = bf16[4,1,512,4,64]{2,4,3,1,0:T(8,128)(2,1)} fusion(bf16[4,1,512,4,64]{2,4,3,1,0:T(8,128)(2,1)} %get-tuple-element.431, s32[]{:T(128)S(6)} %copy.149, f32[4,512,2048]{2,1,0:T(8,128)} %copy-done, f32[4,512,2048]{2,1,0:T(8,128)} %fusion.173, bf16[1,2048,4,64]{1,3,2,0:T(8,128)(2,1)} %get-tuple-element.450), kind=kOutput, calls=%fused_computation.41.clone.1 | convolution fusion | flops 557977600 | bytes 68419584 | tf_op jit(solution)/shard_map/while/body/eval_jaxpr/shqk,skhe->sqhe/dot_general | solution.py:180
  693.8 23.9 %fusion.174 = f32[1,2048,4,64]{1,3,2,0:T(8,128)} fusion(f32[4,512,2048]{2,1,0:T(8,128)} %copy-done, f32[4,512,2048]{2,1,0:T(8,128)} %fusion.173, f32[1,2048,4,64]{1,3,2,0:T(8,128)} %get-tuple-element.429, pred[]{:T(512)S(6)} %compare.3, bf16[1,2048,4,64]{1,3,2,0:T(8,128)(2,1)} %get-tuple-element.449, s32[]{:T(128)S(6)} %select_n.52), kind=kOutput, calls=%fused_computation.36.clone.1 | convolution fusion | flops 558895104 | bytes 71565320 | tf_op jit(solution)/shard_map/while/body/eval_jaxpr/shqk,sqhe->skhe/dot_general | solution.py:183
  721.9 8.2 reshape.491
  730.2 11.6 reduce.31
  743.5 4.3 all-to-all-start.5
  753.2 11.6 reduce.30
  772.6 10.6 reduce.29
  784.9 4.3 all-to-all-start.7
  809.9 9.8 fusion.99
  820.9 16.7 %fusion.106 = f32[4096,1024]{1,0:T(8,128)} fusion(bf16[1,512,1024]{2,1,0:T(8,128)(2,1)S(1)} %copy-done.17, f32[512,4096]{1,0:T(8,128)} %fusion.122, f32[4096]{0:T(1024)S(1)} %bitcast.281), kind=kOutput, calls=%fused_computation.124 | convolution fusion | flops 4315938816 | bytes 26230784 | tf_op jit(solution)/shard_map/std,ste->de/dot_general | solution.py:133
  839.3 11.5 fusion.94
  853.5 13.2 fusion.93
  867.1 6.6 fusion.87
  878.5 40.6 %all-reduce.15 = (f32[1024]{0:T(1024)S(1)}, f32[1024]{0:T(1024)S(1)}, f32[2048]{0:T(1024)S(1)}, f32[1024]{0:T(1024)S(1)}, f32[1024]{0:T(1024)S(1)}, /*index=5*/f...) all-reduce(f32[1024]{0:T(1024)S(1)} %get-tuple-element.181, ...), channel_id=2, replica_groups=mesh['seq'=4,'dp'=8] {'seq','dp'}, use_global_device_ids=true, to_apply=%region_16.17.clone | all-reduce | flops 12288 | bytes 98304
  923.8 49.9 %reduce-scatter.5.cloned.1.call-done = f32[32,3072]{1,0:T(8,128)} async-done(((f32[1024,3072]{1,0:T(8,128)}), f32[32,3072]{1,0:T(8,128)}) %reduce-scatter.5.cloned.1.call-update) | async-done | bytes 393232 | tf_op jit(solution)/shard_map/reduce_scatter | solution.py:218
  973.7 188.8 %reduce-scatter.11.cloned.1.call-done = f32[128,1024]{1,0:T(8,128)} async-done(((f32[4096,1024]{1,0:T(8,128)}), f32[128,1024]{1,0:T(8,128)}) %reduce-scatter.11.cloned.1.call-update) | async-done | bytes 524304 | tf_op jit(solution)/shard_map/reduce_scatter | solution.py:226
  1162.4 187.3 %reduce-scatter.9.cloned.1.call-done = f32[32,4096]{1,0:T(8,128)} async-done(((f32[1024,4096]{1,0:T(8,128)}), f32[32,4096]{1,0:T(8,128)}) %reduce-scatter.9.cloned.1.call-update) | async-done | bytes 524304 | tf_op jit(solution)/shard_map/reduce_scatter | solution.py:224
  (324 shorter events, 199.7 us)
Async XLA Ops:
  7.2 76.3 %all-gather.6.cloned.1.call-start = ((), (), s32[]{:S(2)}) async-start(), calls=%async_computation.12 | async-start | bytes 6488064 | tf_op jit(solution)/shard_map/all_gather | solution.py:58
  7.9 339.5 %all-gather.8.cloned.1.call-start = ((), (), s32[]{:S(2)}) async-start(), calls=%async_computation.13 | async-start | bytes 2162688 | tf_op jit(solution)/shard_map/all_gather | solution.py:60
  8.7 342.5 %all-gather.10.cloned.1.call-start = ((), (), s32[]{:S(2)}) async-start(), calls=%async_computation.14 | async-start | bytes 8650752 | tf_op jit(solution)/shard_map/all_gather | solution.py:64
  57.8 31.8 %copy-start.44 = (f32[1024]{0:T(1024)}, f32[1024]{0:T(1024)S(1)}, u32[]{:S(2)}) copy-start(f32[1024]{0:T(1024)S(1)} %convert_element_type.158) | copy-start | bytes 12292
  57.8 31.8 %copy-start.24 = (f32[1024]{0:T(1024)}, f32[1024]{0:T(1024)S(1)}, u32[]{:S(2)}) copy-start(f32[1024]{0:T(1024)S(1)} %convert_element_type.157) | copy-start | bytes 12292
  59.3 30.3 %copy-start.28 = (f32[512]{0:T(512)}, f32[512]{0:T(512)S(1)}, u32[]{:S(2)}) copy-start(f32[512]{0:T(512)S(1)} %broadcast_multiply_fusion.1) | copy-start | bytes 6148
  61.6 28.0 %copy-start.26 = (f32[512]{0:T(512)}, f32[512]{0:T(512)S(1)}, u32[]{:S(2)}) copy-start(f32[512]{0:T(512)S(1)} %fusion.114) | copy-start | bytes 6148
  104.1 22.9 %all-to-all-start.2 = ((bf16[4,2,65536]{2,1,0:T(2,128)(2,1)}), bf16[4,2,65536]{2,1,0:T(2,128)(2,1)S(1)}, u32[]{:S(2)}, u32[]{:S(2)}) async-start(bf16[4,2,65536]{2,1,0:T(2,128)(2,1)} %reshape.496), calls=%async_computation.2 | async-start | bytes 2097152 | tf_op jit(solution)/shard_map/all_to_all | solution.py:94
  126.9 21.1 %all-to-all-start.1 = ((bf16[4,2,65536]{2,1,0:T(2,128)(2,1)}), bf16[4,2,65536]{2,1,0:T(2,128)(2,1)}, u32[]{:S(2)}, u32[]{:S(2)}) async-start(bf16[4,2,65536]{2,1,0:T(2,128)(2,1)} %reshape.494), calls=%async_computation.1 | async-start | bytes 2097152 | tf_op jit(solution)/shard_map/all_to_all | solution.py:93
  148.0 20.6 %all-to-all-start = ((bf16[4,2,65536]{2,1,0:T(2,128)(2,1)}), bf16[4,2,65536]{2,1,0:T(2,128)(2,1)}, u32[]{:S(2)}, u32[]{:S(2)}) async-start(bf16[4,2,65536]{2,1,0:T(2,128)(2,1)} %reshape.492), calls=%async_computation | async-start | bytes 2097152 | tf_op jit(solution)/shard_map/all_to_all | solution.py:92
  152.3 209.5 %all-gather.12.cloned.1.call-start = ((), (), s32[]{:S(2)}) async-start(), calls=%async_computation.15 | async-start | bytes 8650752 | tf_op jit(solution)/shard_map/all_gather | solution.py:66
  180.6 6.3 copy-start.1
  203.6 6.3 copy-start.1
  226.6 6.3 copy-start.1
  249.7 6.3 copy-start.1
  270.2 24.7 %copy-start.2 = (bf16[1,2048,4,64]{1,3,2,0:T(8,128)(2,1)}, bf16[1,2048,4,64]{1,3,2,0:T(8,128)(2,1)S(1)}, u32[]{:S(2)}) copy-start(bf16[1,2048,4,64]{1,3,2,0:T(8,128)(2,1)S(1)} %get-tuple-element.468) | copy-start | bytes 3145732
  282.8 18.0 %copy-start.51 = (bf16[1024]{0:T(1024)(128)(2,1)S(1)}, bf16[1024]{0:T(1024)(128)(2,1)}, u32[]{:S(2)}) copy-start(bf16[1024]{0:T(1024)(128)(2,1)} %get-tuple-element.237) | copy-start | bytes 6148
  282.8 18.0 %copy-start.50 = (bf16[1024]{0:T(1024)(128)(2,1)S(1)}, bf16[1024]{0:T(1024)(128)(2,1)}, u32[]{:S(2)}) copy-start(bf16[1024]{0:T(1024)(128)(2,1)} %get-tuple-element.236) | copy-start | bytes 6148
  282.8 18.1 %copy-start.49 = (bf16[1024]{0:T(1024)(128)(2,1)S(1)}, bf16[1024]{0:T(1024)(128)(2,1)}, u32[]{:S(2)}) copy-start(bf16[1024]{0:T(1024)(128)(2,1)} %get-tuple-element.234) | copy-start | bytes 6148
  282.8 18.1 %copy-start.52 = (bf16[128]{0:T(256)(128)(2,1)S(1)}, bf16[128]{0:T(256)(128)(2,1)}, u32[]{:S(2)}) copy-start(bf16[128]{0:T(256)(128)(2,1)} %param.29) | copy-start | bytes 772
  296.5 44.7 %all-to-all-start.3 = ((bf16[4,2,65536]{2,1,0:T(2,128)(2,1)}), bf16[4,2,65536]{2,1,0:T(2,128)(2,1)}, u32[]{:S(2)}, u32[]{:S(2)}) async-start(bf16[4,2,65536]{2,1,0:T(2,128)(2,1)} %reshape.498), calls=%async_computation.3 | async-start | bytes 2097152 | tf_op jit(solution)/shard_map/all_to_all | solution.py:121
  300.8 80.4 %copy-start.39 = (f32[1024]{0:T(1024)}, f32[1024]{0:T(1024)S(1)}, u32[]{:S(2)}) copy-start(f32[1024]{0:T(1024)S(1)} %convert_element_type.165) | copy-start | bytes 12292
  300.8 50.3 %copy-start.46 = (f32[1024]{0:T(1024)}, f32[1024]{0:T(1024)S(1)}, u32[]{:S(2)}) copy-start(f32[1024]{0:T(1024)S(1)} %convert_element_type.166) | copy-start | bytes 12292
  341.2 20.6 %copy-start.37 = (f32[32,1,128]{2,1,0:T(1,128)}, f32[32,1,128]{2,1,0:T(1,128)S(1)}, u32[]{:S(2)}) copy-start(f32[32,1,128]{2,1,0:T(1,128)S(1)} %convert_element_type.183) | copy-start | bytes 49156
  341.2 6.2 copy-start.4
  350.7 30.5 %copy-start.6 = (f32[1,512,1024]{2,1,0:T(8,128)}, f32[1,512,1024]{2,1,0:T(8,128)S(1)}, u32[]{:S(2)}) copy-start(f32[1,512,1024]{2,1,0:T(8,128)S(1)} %get-tuple-element.248) | copy-start | bytes 6291460
  350.7 30.5 %copy-start.34 = (f32[512]{0:T(512)}, f32[512]{0:T(512)S(1)}, u32[]{:S(2)}) copy-start(f32[512]{0:T(512)S(1)} %broadcast_multiply_fusion) | copy-start | bytes 6148
  351.1 30.2 %copy-start.41 = (f32[512]{0:T(512)}, f32[512]{0:T(512)S(1)}, u32[]{:S(2)}) copy-start(f32[512]{0:T(512)S(1)} %fusion.115) | copy-start | bytes 6148
  351.1 10.7 copy-start.16
  361.8 14.0 %copy-start.53 = (bf16[1024,4096]{1,0:T(8,128)(2,1)S(1)}, bf16[1024,4096]{1,0:T(8,128)(2,1)}, u32[]{:S(2)}) copy-start(bf16[1024,4096]{1,0:T(8,128)(2,1)} %all-gather.10.cloned.1.call-done) | copy-start | bytes 25165828
  375.8 5.4 copy-start.54
  383.3 21.9 %copy-start.30 = (f32[512]{0:T(512)}, f32[512]{0:T(512)S(1)}, u32[]{:S(2)}) copy-start(f32[512]{0:T(512)S(1)} %negate_multiply_fusion.1) | copy-start | bytes 6148
  389.1 16.2 %copy-start.9 = (bf16[1,512,4,256]{1,3,2,0:T(8,128)(2,1)S(1)}, bf16[1,512,4,256]{1,3,2,0:T(8,128)(2,1)}, u32[]{:S(2)}) copy-start(bf16[1,512,4,256]{1,3,2,0:T(8,128)(2,1)} %copy.102) | copy-start | bytes 3145732
  400.9 18.7 %all-to-all-start.4 = ((bf16[4,2,65536]{2,1,0:T(2,128)(2,1)}), bf16[4,2,65536]{2,1,0:T(2,128)(2,1)}, u32[]{:S(2)}, u32[]{:S(2)}) async-start(bf16[4,2,65536]{2,1,0:T(2,128)(2,1)} %reshape.500), calls=%async_computation.4 | async-start | bytes 2097152 | tf_op jit(solution)/shard_map/all_to_all | solution.py:159
  405.2 518.6 %reduce-scatter.7.cloned.1.call-start = ((), (), s32[]{:S(2)}) async-start(), calls=%async_computation.17 | async-start | bytes 4325376 | tf_op jit(solution)/shard_map/reduce_scatter | solution.py:220
  423.6 7.4 copy-start.3
  435.9 6.8 copy-start.8
  442.7 5.7 copy-start
  507.3 6.8 copy-start.8
  514.1 5.7 copy-start
  579.1 6.8 copy-start.8
  585.9 5.7 copy-start
  650.6 6.8 copy-start.8
  657.4 5.7 copy-start
  743.5 23.1 %all-to-all-start.5 = ((bf16[4,2,65536]{2,1,0:T(2,128)(2,1)}), bf16[4,2,65536]{2,1,0:T(2,128)(2,1)}, u32[]{:S(2)}, u32[]{:S(2)}) async-start(bf16[4,2,65536]{2,1,0:T(2,128)(2,1)} %reshape.506), calls=%async_computation.5 | async-start | bytes 2097152 | tf_op jit(solution)/shard_map/all_to_all | solution.py:196
  766.5 18.3 %all-to-all-start.6 = ((bf16[4,2,65536]{2,1,0:T(2,128)(2,1)}), bf16[4,2,65536]{2,1,0:T(2,128)(2,1)}, u32[]{:S(2)}, u32[]{:S(2)}) async-start(bf16[4,2,65536]{2,1,0:T(2,128)(2,1)} %reshape.504), calls=%async_computation.6 | async-start | bytes 2097152 | tf_op jit(solution)/shard_map/all_to_all | solution.py:197
  784.9 17.9 %all-to-all-start.7 = ((bf16[4,2,65536]{2,1,0:T(2,128)(2,1)}), bf16[4,2,65536]{2,1,0:T(2,128)(2,1)}, u32[]{:S(2)}, u32[]{:S(2)}) async-start(bf16[4,2,65536]{2,1,0:T(2,128)(2,1)} %reshape.502), calls=%async_computation.7 | async-start | bytes 2097152 | tf_op jit(solution)/shard_map/all_to_all | solution.py:198
  789.1 184.5 %reduce-scatter.5.cloned.1.call-start = ((), (), s32[]{:S(2)}) async-start(), calls=%async_computation.16 | async-start | bytes 12976128 | tf_op jit(solution)/shard_map/reduce_scatter | solution.py:218
  792.2 5.1 copy-start.10
  799.6 10.2 copy-start.5
  799.6 10.2 copy-start.20
  799.6 10.2 copy-start.25
  799.7 10.2 copy-start.27
  799.7 10.2 copy-start.29
  799.7 10.2 copy-start.45
  808.5 11.2 copy-start.12
  819.7 342.7 %reduce-scatter.11.cloned.1.call-start = ((), (), s32[]{:S(2)}) async-start(), calls=%async_computation.19 | async-start | bytes 17301504 | tf_op jit(solution)/shard_map/reduce_scatter | solution.py:226
  837.6 512.2 %reduce-scatter.9.cloned.1.call-start = ((), (), s32[]{:S(2)}) async-start(), calls=%async_computation.18 | async-start | bytes 17301504 | tf_op jit(solution)/shard_map/reduce_scatter | solution.py:224
  853.4 13.3 copy-start.11
  853.4 13.4 copy-start.13
  853.4 13.6 %copy-start.21 = (bf16[1,512,4,256]{1,3,2,0:T(8,128)(2,1)S(1)}, bf16[1,512,4,256]{1,3,2,0:T(8,128)(2,1)}, u32[]{:S(2)}) copy-start(bf16[1,512,4,256]{1,3,2,0:T(8,128)(2,1)} %copy.107) | copy-start | bytes 3145732
  853.4 13.6 %copy-start.22 = (bf16[1,512,4,256]{1,3,2,0:T(8,128)(2,1)S(1)}, bf16[1,512,4,256]{1,3,2,0:T(8,128)(2,1)}, u32[]{:S(2)}) copy-start(bf16[1,512,4,256]{1,3,2,0:T(8,128)(2,1)} %copy.109) | copy-start | bytes 3145732
  853.5 13.6 %copy-start.23 = (bf16[1,512,4,256]{1,3,2,0:T(8,128)(2,1)S(1)}, bf16[1,512,4,256]{1,3,2,0:T(8,128)(2,1)}, u32[]{:S(2)}) copy-start(bf16[1,512,4,256]{1,3,2,0:T(8,128)(2,1)} %copy.111) | copy-start | bytes 3145732
  867.1 6.8 copy-start.33
  (19 other events, 34.0 us)
Sparse Core Ops, SparseCore 0:
  11.0 72.4 all-gather.5
  86.5 62.3 all-gather.7
  151.8 78.8 all-gather.9
  233.6 75.9 all-gather.11
  410.7 141.3 reduce-scatter.6
  819.9 153.7 reduce-scatter.4
  976.6 185.7 reduce-scatter.10
  1165.4 184.3 reduce-scatter.8
where the time goes:
time: 1370 us; the launch traced here: 1360 us
  waiting for transfers between devices  467 us (34%)
  matrix products  417 us (30%)
  local copies, waits for them, and re-layouts  159 us (12%)
  other arithmetic  127 us (9%)
  blocking collectives  123 us (9%)
  starting transfers between devices  34.2 us (2%)
  between operations  15.5 us (1%)
  loops' own time  14.3 us (1%)
    reduce_scatter x1, waiting for transfers between devices, body(): lax.psum_scatter(grad_down_weight, ('seq', 'dp'), scatter_dimension=0, ti...  189 us
    reduce_scatter x1, waiting for transfers between devices, body(): lax.psum_scatter(grad_up_weight, ('seq', 'dp'), scatter_dimension=0, tile...  187 us
    dot_general x4, matrix products, backward_block(): jnp.einsum('shqk,sqhe->skhe', score_grad, query_rows, preferred_element_t...  95.1 us
    dot_general x4, matrix products, backward_block(): jnp.einsum('shqk,skhe->sqhe', score_grad, key_heads, preferred_element_ty...  91 us
    unnamed x2, blocking collectives  83.1 us
    unnamed x10, other arithmetic  77.1 us
    unnamed x151, local copies, waits for them, and re-layouts  72.5 us
    dot_general x8, matrix products, block_scores(): jnp.einsum('sqhe,skhe->shqk', query_rows, key_heads, preferred_element_ty...  52.3 us
  transfers between devices with their start and end apart: 16, of which 7 were waited for; matrix products, arithmetic and copies ran while one was open for 47% of the time, Pallas kernels for 0%

commit v1 on v0

v1 whole, which is shorter than its diff:
```python
import functools
import math

import jax
import jax.numpy as jnp
from jax import lax
from jax.experimental import pallas as pl
from jax.experimental.pallas import tpu as pltpu
from jax.sharding import Mesh
from jax.sharding import PartitionSpec as P

HEADS = 16
HEAD = 64
EPSILON = 1e-05
LOG2E = math.log2(math.e)
TILE = 256
VMEM_BYTES = 60 * 1024 * 1024
CORES = 2
CHIPS = ("seq", "ring")
WORLD = ("seq", "ring", "core")

def _dot(a, b):
    return jnp.dot(a, b, preferred_element_type=jnp.float32)

def _bias_tile(slope):
    return lax.broadcasted_iota(jnp.int32, (TILE, TILE), 0).astype(jnp.float32) * slope

def _keep():
    return lax.broadcasted_iota(jnp.int32, (TILE, TILE), 0) <= lax.broadcasted_iota(jnp.int32, (TILE, TILE), 1)

def _row_mask(shape, axis, half):
    ids = lax.broadcasted_iota(jnp.int32, shape, axis)
    return (ids >= HEAD) == (half == 1)

def forward_kernel(slope_ref, q_ref, k_ref, v_ref, ctx_ref, wide_ref, log_ref, q_turn, v_turn, scores):
    head = pl.program_id(0)
    half = lax.rem(head, 2)
    length = q_ref.shape[0]
    tiles = length // TILE

    @pl.when(half == 0)
    def _():
        q_turn[...] = q_ref[...].T
        v_turn[...] = v_ref[...].T

    slope = slope_ref[head] * LOG2E
    scale = HEAD ** -0.5 * LOG2E
    rows = pl.ds(pl.multiple_of(half * HEAD, HEAD), HEAD)
    bias = _bias_tile(slope)
    for i in range(tiles):
        cols = slice(i * TILE, (i + 1) * TILE)
        q_block = q_turn[:, cols]
        q_block = jnp.where(_row_mask(q_block.shape, 0, half), q_block, jnp.zeros_like(q_block))
        peak = None
        for c in range(i + 1):
            part = _dot(k_ref[c * TILE:(c + 1) * TILE, :], q_block) * scale + bias
            if c == i:
                part = jnp.where(_keep(), part, -jnp.inf)
            scores[i % 2, c] = part
            top = jnp.max(part, axis=0, keepdims=True) + slope * ((c - i) * TILE)
            peak = top if peak is None else jnp.maximum(peak, top)
        total = jnp.zeros((1, TILE), jnp.float32)
        out = jnp.zeros((HEAD, TILE), jnp.float32)
        for c in range(i + 1):
            probs = jnp.exp2(scores[i % 2, c] - (peak - slope * ((c - i) * TILE)))
            total = total + jnp.sum(probs, axis=0, keepdims=True)
            out = out + _dot(v_turn[rows, c * TILE:(c + 1) * TILE], probs.astype(jnp.bfloat16))
        wide_ref[rows, cols] = out / total
        log_ref[:, cols] = jnp.broadcast_to(peak + jnp.log2(total), (8, TILE))

    @pl.when(half == 1)
    def _():
        ctx_ref[...] = wide_ref[...].T.astype(jnp.bfloat16)

def attend_forward(slopes, qkv):
    length, triple = qkv.shape
    heads = triple // (3 * HEAD)
    pairs = heads // 2
    spec = lambda part: pl.BlockSpec((length, 2 * HEAD), lambda h, part=part: (0, part * pairs + h // 2))
    return pl.pallas_call(
        forward_kernel,
        grid=(heads,),
        in_specs=[pl.BlockSpec(memory_space=pltpu.SMEM), spec(0), spec(1), spec(2)],
        out_specs=[
            pl.BlockSpec((length, 2 * HEAD), lambda h: (0, h // 2)),
            pl.BlockSpec((2 * HEAD, length), lambda h: (h // 2, 0)),
            pl.BlockSpec((8, length), lambda h: (h, 0)),
        ],
        out_shape=[
            jax.ShapeDtypeStruct((length, heads * HEAD), jnp.bfloat16),
            jax.ShapeDtypeStruct((heads * HEAD, length), jnp.float32),
            jax.ShapeDtypeStruct((heads * 8, length), jnp.float32),
        ],
        scratch_shapes=[
            pltpu.VMEM((2 * HEAD, length), jnp.bfloat16),
            pltpu.VMEM((2 * HEAD, length), jnp.bfloat16),
            pltpu.VMEM((2, length // TILE, TILE, TILE), jnp.float32),
        ],
        compiler_params=pltpu.CompilerParams(vmem_limit_bytes=VMEM_BYTES),
        name="attend_forward",
    )(slopes, qkv, qkv, qkv)

def backward_kernel(slope_ref, q_ref, k_ref, v_ref, g_ref, wide_ref, log_ref, out_ref, q_turn, k_turn, g_turn, dq_turn, dk_sum, dv_sum):
    head = pl.program_id(0)
    half = lax.rem(head, 2)
    length = q_ref.shape[0]
    tiles = length // TILE
    heads = out_ref.shape[1] // (3 * HEAD)
    wide = heads * HEAD

    @pl.when(half == 0)
    def _():
        q_turn[...] = q_ref[...].T
        k_turn[...] = k_ref[...].T
        g_turn[...] = g_ref[...].T

    slope = slope_ref[head] * LOG2E
    scale = HEAD ** -0.5 * LOG2E
    rows = pl.ds(pl.multiple_of(half * HEAD, HEAD), HEAD)
    bias = _bias_tile(slope)
    inner = jnp.sum(wide_ref[rows, :] * g_turn[rows, :].astype(jnp.float32), axis=0, keepdims=True)
    for c in range(tiles):
        span = slice(c * TILE, (c + 1) * TILE)
        dk = jnp.zeros((TILE, 2 * HEAD), jnp.float32)
        dv = jnp.zeros((TILE, 2 * HEAD), jnp.float32)
        for i in range(c, tiles):
            cols = slice(i * TILE, (i + 1) * TILE)
            q_cols = q_turn[:, cols]
            q_cols = jnp.where(_row_mask(q_cols.shape, 0, half), q_cols, jnp.zeros_like(q_cols))
            g_cols = g_turn[:, cols]
            g_cols = jnp.where(_row_mask(g_cols.shape, 0, half), g_cols, jnp.zeros_like(g_cols))
            q_rows = q_ref[cols, :]
            q_rows = jnp.where(_row_mask(q_rows.shape, 1, half), q_rows, jnp.zeros_like(q_rows))
            g_rows = g_ref[cols, :]
            g_rows = jnp.where(_row_mask(g_rows.shape, 1, half), g_rows, jnp.zeros_like(g_rows))
            part = _dot(k_ref[span, :], q_cols) * scale + bias
            if c == i:
                part = jnp.where(_keep(), part, -jnp.inf)
            probs = jnp.exp2(part - (log_ref[0:1, cols] - slope * ((c - i) * TILE)))
            grad = (probs * (_dot(v_ref[span, :], g_cols) - inner[:, cols])).astype(jnp.bfloat16)
            dv = dv + _dot(probs.astype(jnp.bfloat16), g_rows)
            dk = dk + _dot(grad, q_rows)
            dq = _dot(k_turn[rows, span], grad)
            if c == 0:
                dq_turn[rows, cols] = dq
            else:
                dq_turn[rows, cols] += dq

        @pl.when(half == 0)
        def _():
            dk_sum[span, :] = dk
            dv_sum[span, :] = dv

        @pl.when(half == 1)
        def _():
            lane = pl.multiple_of((head // 2) * 2 * HEAD, 2 * HEAD)
            out_ref[span, pl.ds(wide + lane, 2 * HEAD)] = ((dk_sum[span, :] + dk) * HEAD ** -0.5).astype(jnp.bfloat16)
            out_ref[span, pl.ds(2 * wide + lane, 2 * HEAD)] = (dv_sum[span, :] + dv).astype(jnp.bfloat16)

    @pl.when(half == 1)
    def _():
        lane = pl.multiple_of((head // 2) * 2 * HEAD, 2 * HEAD)
        out_ref[:, pl.ds(lane, 2 * HEAD)] = (dq_turn[...] * HEAD ** -0.5).T.astype(jnp.bfloat16)

def attend_backward(slopes, qkv, grad, wide, log):
    length, triple = qkv.shape
    heads = triple // (3 * HEAD)
    pairs = heads // 2
    spec = lambda part: pl.BlockSpec((length, 2 * HEAD), lambda h, part=part: (0, part * pairs + h // 2))
    return pl.pallas_call(
        backward_kernel,
        grid=(heads,),
        in_specs=[
            pl.BlockSpec(memory_space=pltpu.SMEM), spec(0), spec(1), spec(2),
            pl.BlockSpec((length, 2 * HEAD), lambda h: (0, h // 2)),
            pl.BlockSpec((2 * HEAD, length), lambda h: (h // 2, 0)),
            pl.BlockSpec((8, length), lambda h: (h, 0)),
        ],
        out_specs=pl.BlockSpec((length, triple), lambda h: (0, 0)),
        out_shape=jax.ShapeDtypeStruct((length, triple), jnp.bfloat16),
        scratch_shapes=[
            pltpu.VMEM((2 * HEAD, length), jnp.bfloat16),
            pltpu.VMEM((2 * HEAD, length), jnp.bfloat16),
            pltpu.VMEM((2 * HEAD, length), jnp.bfloat16),
            pltpu.VMEM((2 * HEAD, length), jnp.float32),
            pltpu.VMEM((length, 2 * HEAD), jnp.float32),
            pltpu.VMEM((length, 2 * HEAD), jnp.float32),
        ],
        compiler_params=pltpu.CompilerParams(vmem_limit_bytes=VMEM_BYTES),
        name="attend_backward",
    )(slopes, qkv, qkv, qkv, grad, wide, log)

def layer_norm(values, norm_gain, norm_shift):
    centre = values - jnp.mean(values, axis=-1, keepdims=True)
    spread = jnp.mean(centre * centre, axis=-1, keepdims=True)
    return centre * lax.rsqrt(spread + EPSILON) * norm_gain + norm_shift


def tanh_gelu(upper_in):
    return jax.nn.gelu(upper_in, approximate=True)


def gather_small(parts):
    sizes = [part.shape[0] for part in parts]
    width = -(-sum(sizes) // 512) * 512
    packed = jnp.concatenate(list(parts) + [jnp.zeros((width - sum(sizes),), parts[0].dtype)])
    whole = lax.all_gather(packed.reshape(4, width // 4), WORLD, axis=0, tiled=False)
    whole = whole.reshape(-1, width).astype(jnp.float32)
    out, start = [], 0
    for size in sizes:
        out.append(whole[:, start : start + size].reshape(-1))
        start += size
    return out


def scatter_small(parts, world):
    rows = [part.reshape(world, -1) for part in parts]
    sizes = [row.shape[1] for row in rows]
    width = -(-sum(sizes) // 128) * 128
    packed = jnp.concatenate(rows + [jnp.zeros((world, width - sum(sizes)), jnp.float32)], axis=1)
    owned = lax.psum_scatter(packed, WORLD, scatter_dimension=0, tiled=True)[0]
    out, start = [], 0
    for size in sizes:
        out.append(owned[start : start + size])
        start += size
    return out


def other_core(value):
    return lax.ppermute(value, "core", [(0, 1), (1, 0)])


def gather_weight(shard):
    mine = lax.all_gather(shard, CHIPS, axis=0, tiled=False)
    theirs = other_core(mine)
    first = lax.axis_index("core") == 0
    pair = jnp.stack((jnp.where(first, mine, theirs), jnp.where(first, theirs, mine)), axis=1)
    return pair.reshape(-1, shard.shape[-1])


def pick_rows(columns, chips, core):
    tokens, width = columns.shape
    parts = columns.reshape(tokens, chips, CORES, width // (chips * CORES))
    return lax.dynamic_index_in_dim(parts, core, 2, keepdims=False).reshape(tokens, width // CORES)


def contract_tokens(left, right):
    return lax.dot_general(left, right, (((0,), (0,)), ((), ())), preferred_element_type=jnp.float32)


def scatter_weight_grad(left, right, chips):
    core = lax.axis_index("core")
    sent = contract_tokens(pick_rows(left, chips, 1 - core), right).astype(jnp.bfloat16)
    came = other_core(sent).astype(jnp.float32)
    both = (contract_tokens(pick_rows(left, chips, core), right) + came).astype(jnp.bfloat16)
    return lax.psum_scatter(both, CHIPS, scatter_dimension=0, tiled=True).astype(jnp.float32)


def body(
    tokens_in,
    out_grad,
    first_gain,
    first_shift,
    input_weight,
    input_bias,
    output_weight,
    output_bias,
    second_gain,
    second_shift,
    up_weight,
    up_bias,
    down_weight,
    down_bias,
):
    ways = lax.axis_size("seq")
    rings = lax.axis_size("ring")
    chips = ways * rings
    model_width = tokens_in.shape[-1]
    group_width = model_width // ways
    head_group = group_width // HEAD
    rows_in = tokens_in.reshape(-1, model_width)
    local = rows_in.shape[0]
    length = local * ways
    upstream = out_grad.reshape(local, model_width)

    (
        gain_first,
        shift_first,
        bias_input,
        bias_output,
        gain_second,
        shift_second,
        bias_up,
        bias_down,
    ) = gather_small(
        (first_gain, first_shift, input_bias, output_bias, second_gain, second_shift, up_bias, down_bias)
    )
    seq_index = lax.axis_index("seq")

    all_rows = lax.all_gather(rows_in, "seq", axis=0, tiled=True)
    owned_rows = input_weight.shape[0]
    by_group = input_weight.reshape(owned_rows, 3, ways, group_width)
    by_group = jnp.moveaxis(by_group, 2, 0).reshape(ways, owned_rows, 3 * group_width)
    columns = lax.all_to_all(by_group, "seq", split_axis=0, concat_axis=0, tiled=True)
    columns = lax.all_gather(columns, ("ring", "core"), axis=0, tiled=False)
    weight_input = jnp.moveaxis(columns, 0, 1).reshape(model_width, 3 * group_width)

    weight_output = gather_weight(output_weight)
    weight_up = gather_weight(up_weight)
    weight_down = gather_weight(down_weight)

    normed = layer_norm(all_rows.astype(jnp.float32), gain_first, shift_first).astype(jnp.bfloat16)
    start = seq_index * group_width
    bias_group = jnp.concatenate(
        (
            lax.dynamic_slice_in_dim(bias_input, start, group_width),
            jnp.zeros((group_width,), jnp.float32),
            lax.dynamic_slice_in_dim(bias_input, model_width + start, group_width),
        )
    )
    qkv = (jnp.dot(normed, weight_input, preferred_element_type=jnp.float32) + bias_group).astype(
        jnp.bfloat16
    )
    head_ids = (seq_index * head_group + jnp.arange(head_group, dtype=jnp.int32)).astype(jnp.float32)
    slopes = jnp.exp2(-8.0 * (head_ids + 1.0) / HEADS)
    context_split, wide, log_totals = attend_forward(slopes, qkv)
    context = lax.all_to_all(
        context_split.reshape(ways, local, group_width), "seq", split_axis=0, concat_axis=0, tiled=True
    )
    context = jnp.moveaxis(context, 0, 1).reshape(local, model_width)

    inputs = rows_in.astype(jnp.float32)
    branch = jnp.dot(context, weight_output, preferred_element_type=jnp.float32) + bias_output
    residual = inputs + branch
    normed_two_float, second_back = jax.vjp(layer_norm, residual, gain_second, shift_second)
    normed_two = normed_two_float.astype(jnp.bfloat16)
    upper = jnp.dot(normed_two, weight_up, preferred_element_type=jnp.float32) + bias_up
    activated, gelu_back = jax.vjp(tanh_gelu, upper)
    hidden = activated.astype(jnp.bfloat16)
    layer_out = (
        residual + jnp.dot(hidden, weight_down, preferred_element_type=jnp.float32) + bias_down
    ).astype(jnp.bfloat16)
    grad_hidden = lax.dot_general(
        upstream, weight_down, (((1,), (1,)), ((), ())), preferred_element_type=jnp.float32
    )
    grad_upper = gelu_back(grad_hidden)[0]
    upper_low = grad_upper.astype(jnp.bfloat16)
    grad_normed_two = lax.dot_general(
        upper_low, weight_up, (((1,), (1,)), ((), ())), preferred_element_type=jnp.float32
    )
    grad_through, grad_second_gain, grad_second_shift = second_back(grad_normed_two)
    grad_residual = upstream.astype(jnp.float32) + grad_through
    branch_low = grad_residual.astype(jnp.bfloat16)
    context_grad = lax.dot_general(
        branch_low, weight_output, (((1,), (1,)), ((), ())), preferred_element_type=jnp.float32
    ).astype(jnp.bfloat16)
    grad_split = jnp.moveaxis(context_grad.reshape(local, ways, group_width), 1, 0)
    grad_split = lax.all_to_all(grad_split, "seq", split_axis=0, concat_axis=0, tiled=True)
    grad_split = grad_split.reshape(length, group_width)

    grad_down_weight = scatter_weight_grad(hidden, upstream, chips)
    grad_up_weight = scatter_weight_grad(normed_two, upper_low, chips)
    grad_output_weight = scatter_weight_grad(context, branch_low, chips)

    grad_qkv = attend_backward(slopes, qkv, grad_split, wide, log_totals)

    grad_normed = lax.dot_general(
        grad_qkv, weight_input, (((1,), (1,)), ((), ())), preferred_element_type=jnp.float32
    ).astype(jnp.bfloat16)
    grad_normed = lax.all_to_all(
        grad_normed.reshape(ways, local, model_width), "seq", split_axis=0, concat_axis=0, tiled=True
    )
    grad_normed = jnp.sum(grad_normed.astype(jnp.float32), axis=0)

    grad_columns = contract_tokens(normed, grad_qkv)
    grad_columns = jnp.moveaxis(
        grad_columns.reshape(ways, rings * CORES, owned_rows, 3 * group_width), 1, 0
    ).astype(jnp.bfloat16)
    grad_columns = lax.psum_scatter(
        grad_columns.reshape(-1, 3 * group_width), ("ring", "core"), scatter_dimension=0, tiled=True
    )
    grad_columns = lax.all_to_all(
        grad_columns.reshape(ways, owned_rows, 3 * group_width), "seq", split_axis=0, concat_axis=0, tiled=True
    )
    grad_input_weight = jnp.moveaxis(
        grad_columns.reshape(ways, owned_rows, 3, group_width), 0, 2
    ).reshape(owned_rows, 3 * model_width).astype(jnp.float32)

    bias_sums = jnp.sum(grad_qkv.astype(jnp.float32), axis=0)
    empty = jnp.zeros((2 * model_width,), jnp.float32)
    grad_input_bias = lax.dynamic_update_slice(empty, bias_sums[:group_width], (start,))
    grad_input_bias = lax.dynamic_update_slice(
        grad_input_bias, bias_sums[2 * group_width :], (model_width + start,)
    )

    _, first_back = jax.vjp(layer_norm, inputs, gain_first, shift_first)
    grad_entry, grad_first_gain, grad_first_shift = first_back(grad_normed)
    tokens_grad = grad_residual + grad_entry

    small = scatter_small(
        (
            grad_first_gain,
            grad_first_shift,
            grad_input_bias,
            jnp.sum(grad_residual, axis=0),
            grad_second_gain,
            grad_second_shift,
            jnp.sum(grad_upper, axis=0),
            jnp.sum(upstream.astype(jnp.float32), axis=0),
        ),
        chips * CORES,
    )
    return (
        layer_out.reshape(tokens_in.shape),
        tokens_grad.reshape(tokens_in.shape),
        small[0],
        small[1],
        grad_input_weight,
        small[2],
        grad_output_weight,
        small[3],
        small[4],
        small[5],
        grad_up_weight,
        small[6],
        grad_down_weight,
        small[7],
    )


def solution(mesh):
    ways, copies = mesh.shape["seq"], mesh.shape["dp"]
    split = Mesh(mesh.devices.reshape(ways, copies // CORES, CORES), WORLD)
    token = P(("ring", "core"), "seq", None)
    vector = P(WORLD)
    matrix = P(WORLD, None)
    weights = (vector, vector, matrix, vector, matrix, vector, vector, vector, matrix, vector, matrix, vector)
    return jax.shard_map(
        body,
        mesh=split,
        in_specs=(token, token) + weights,
        out_specs=(token, token) + weights,
        check_vma=False,
    )
```

time: 1370 us -> 796 us (0.58)
  matrix products: 417 us -> 97.4 us
  local copies, waits for them, and re-layouts: 159 us -> 65.7 us
  waiting for transfers between devices: 467 us -> 377 us
  other arithmetic: 127 us -> 56.6 us
  Pallas kernels: 0 us -> 64.6 us
  blocking collectives: 123 us -> 92 us
  starting transfers between devices: 34.2 us -> 18.3 us
  loops' own time: 14.3 us -> 0 us
    reduce_scatter x4, waiting for transfers between devices: 426 us -> 66.3 us  [the longest x3 66.3 us: scatter_weight_grad(): lax.psum_scatter(both, CHIPS, scatter_dimension=0, tiled=True)]
    dot_general x36 -> x11, matrix products: 384 us -> 62.5 us  [the longest x7 34.8 us: contract_tokens(): lax.dot_general(left, right, (((0,), (0,)), ((), ())), preferred_element_...]
    all_gather x4 -> x5, waiting for transfers between devices: 22 us -> 227 us  [the longest x3 150 us: gather_weight(): mine = lax.all_gather(shard, CHIPS, axis=0, tiled=False)]
    unnamed x10 -> x1, other arithmetic: 77.1 us -> 0.01 us
    pallas_call x0 -> x2, Pallas kernels: none -> 64.6 us  [the longest x1 43.4 us: attend_backward(): pl.pallas_call(backward_kernel, grid=(heads,), in_specs=[pl.BlockSpec(mem...]
    all_to_all x8 -> x4, waiting for transfers between devices: 16.7 us -> 73.9 us  [the longest x1 62.7 us: body(): lax.all_to_all(grad_normed.reshape(ways, local, model_width), 'seq', spli...]
    unnamed x151 -> x39, local copies, waits for them, and re-layouts: 72.5 us -> 22.8 us
    unnamed x2 -> x1, blocking collectives: 83.1 us -> 41.3 us
  transfers between devices with their start and end apart: 16 -> 19, of which waited for: 7 -> 8; matrix products, arithmetic and copies ran while one was open for 47% -> 20% of each run, Pallas kernels for 0% -> 8%
where the time goes in v1:
time: 796 us; the launch traced here: 786 us
  waiting for transfers between devices  377 us (47%)
  matrix products  97.4 us (12%)
  blocking collectives  92 us (12%)
  local copies, waits for them, and re-layouts  65.7 us (8%)
  Pallas kernels  64.6 us (8%)
  other arithmetic  56.6 us (7%)
  starting transfers between devices  18.3 us (2%)
  between operations  14.4 us (2%)
    all_gather x3, waiting for transfers between devices, gather_weight(): mine = lax.all_gather(shard, CHIPS, axis=0, tiled=False)  150 us
    reduce_scatter x3, waiting for transfers between devices, scatter_weight_grad(): lax.psum_scatter(both, CHIPS, scatter_dimension=0, tiled=True)  66.3 us
    all_to_all x1, waiting for transfers between devices, body(): lax.all_to_all(grad_normed.reshape(ways, local, model_width), 'seq', spli...  62.7 us
    all_gather x1, waiting for transfers between devices, body(): all_rows = lax.all_gather(rows_in, 'seq', axis=0, tiled=True)  52.6 us
    pallas_call x1, Pallas kernels, attend_backward(): pl.pallas_call(backward_kernel, grid=(heads,), in_specs=[pl.BlockSpec(mem...  43.4 us
    unnamed x1, blocking collectives  41.3 us
    all_gather x1, blocking collectives, gather_small(): lax.all_gather(packed.reshape(4, width // 4), WORLD, axis=0, tiled=False)  40.1 us
    dot_general x7, matrix products, contract_tokens(): lax.dot_general(left, right, (((0,), (0,)), ((), ())), preferred_element_...  34.8 us
  transfers between devices with their start and end apart: 19, of which 8 were waited for; matrix products, arithmetic and copies ran while one was open for 20% of the time, Pallas kernels for 8%

profile of v1, /device:TPU:0, one launch (start us, length us, event | category | flops | bytes accessed | tf_op | source)
XLA Modules:
  0.0 786.3 jit_solution(409893757073077408)
XLA Ops:
  8.0 1.1 reshape.242
  9.4 10.6 %all_to_all.25 = bf16[4,32,768]{2,1,0:T(8,128)(2,1)} all-to-all(bf16[4,32,768]{2,1,0:T(8,128)(2,1)S(1)} %reshape.243), channel_id=1, replica_groups=mesh['seq'=4,'ring'=4,'core'=2] {'seq'}, dimensions={0} | all-to-all | bytes 393216 | tf_op jit(solution)/shard_map/all_to_all | solution.py:304
  21.9 5.4 concatenate.9
  27.4 40.1 %all_gather.31 = bf16[32,4,128]{2,1,0:T(4,128)(2,1)S(1)} all-gather(bf16[1,4,128]{2,1,0:T(4,128)(2,1)S(1)} %bitcast.225), channel_id=1, replica_groups=mesh['seq'=4,'ring'=4,'core'=2] {'seq','ring','core'}, dimensions={0}, use_global_device_ids=true | all-gather | bytes 33792 | tf_op jit(solution)/shard_map/all_gather | solution.py:207
  69.5 25.0 %all-gather.13.cloned.1.call-done = bf16[32,32,768]{2,1,0:T(8,128)(2,1)} async-done(((bf16[4,32,768]{2,1,0:T(8,128)(2,1)}), bf16[32,32,768]{2,1,0:T(8,128)(2,1)}) %all-gather.13.cloned.1.call-update) | async-done | bytes 1572880 | tf_op jit(solution)/shard_map/all_gather | solution.py:305
  94.4 1.5 copy.64
  96.0 52.6 %all-gather.11.cloned.1.call-done = bf16[1,2048,1024]{2,1,0:T(8,128)(2,1)} async-done(((bf16[1,512,1024]{2,1,0:T(8,128)(2,1)}), bf16[1,2048,1024]{2,1,0:T(8,128)(2,1)}) %all-gather.11.cloned.1.call-update) | async-done | bytes 4194320 | tf_op jit(solution)/shard_map/all_gather | solution.py:300
  148.5 2.8 convert_reduce_fusion
  151.4 75.7 %all-gather.19.cloned.1.call-done = bf16[2048,1024]{1,0:T(8,128)(2,1)} async-done(((bf16[128,1024]{1,0:T(8,128)(2,1)}), bf16[2048,1024]{1,0:T(8,128)(2,1)}) %all-gather.19.cloned.1.call-update) | async-done | bytes 4194320 | tf_op jit(solution)/shard_map/all_gather | solution.py:234
  227.1 3.0 fusion.3
  230.1 74.1 %all-gather.17.cloned.1.call-done = bf16[512,4096]{1,0:T(8,128)(2,1)} async-done(((bf16[32,4096]{1,0:T(8,128)(2,1)}), bf16[512,4096]{1,0:T(8,128)(2,1)}) %all-gather.17.cloned.1.call-update) | async-done | bytes 4194320 | tf_op jit(solution)/shard_map/all_gather | solution.py:234
  304.2 8.0 %add_convert_fusion.2.q_ref.k_ref.v_ref = bf16[2048,768]{1,0:T(8,128)(2,1)} fusion(bf16[1024,768]{1,0:T(8,128)(2,1)S(1)} %bitcast.208, f32[768]{0:T(1024)S(1)} %pad_maximum_fusion.3, bf16[1,2048,1024]{2,1,0:T(8,128)(2,1)} %all-gather.11.cloned.1.call-done, f32[1024]{0:T(1024)S(1)} %add.168, f32[1024]{0:T(1024)S(1)} %mul.178, f32[2048]{0:T(1024)S(1)} %add_rsqrt_fusion, ...), kind=kOutput, calls=%fused_computation.30 | convolution fusion | flops 3236954112 | bytes 8940544 | tf_op jit(solution)/shard_map/dot_general | solution.py:321
  312.3 21.2 %attend_forward.1 = (bf16[2048,256]{1,0:T(8,128)(2,1)}, f32[256,2048]{1,0:T(8,128)}, f32[32,2048]{1,0:T(8,128)}) custom-call(f32[4]{0:T(128)} %multiply_exponential_fusion.slope_ref, bf16[2048,768]{1,0:T(8,128)(2,1)} %add_convert_fusion.2.q_ref.k_ref.v_ref, bf16[2048,768]{1,0:T(8,128)(2,1)} %add_convert_fusion.2.q_ref.k_ref.v_ref, ...), custom_call_target="tpu_custom_call" | custom-call | tf_op jit(solution)/shard_map/attend_forward/pallas_call | solution.py:80
  333.4 2.4 copy.65
  335.8 3.7 all-to-all-start.1
  339.8 1.5 select_bitcast_fusion.5
  341.3 1.5 pad_maximum_fusion.2
  342.8 11.2 %all-to-all-done.1 = bf16[4,512,256]{1,2,0:T(8,128)(2,1)S(1)} async-done(((bf16[4,512,256]{1,2,0:T(8,128)(2,1)}), bf16[4,512,256]{1,2,0:T(8,128)(2,1)S(1)}, u32[]{:S(2)}, u32[]{:S(2)}) %all-to-all-start.1) | async-done | bytes 1048608 | tf_op jit(solution)/shard_map/all_to_all | solution.py:327
  354.0 1.0 copy-done.4
  355.0 3.3 fusion.58
  358.7 1.4 add_convert_fusion.5
  360.0 2.3 copy.72
  362.3 3.0 constant_dynamic-slice_fusion.3
  365.5 5.1 select_bitcast_fusion.1
  370.6 7.5 pad_maximum_fusion.1
  378.1 5.7 select_bitcast_fusion.3
  383.9 7.5 pad_maximum_fusion
  391.4 12.7 %multiply_convert_fusion = (bf16[512,4096]{1,0:T(8,128)(2,1)}, f32[512,4096]{1,0:T(8,128)}) fusion(f32[4096]{0:T(1024)S(1)} %slice_bitcast_fusion, bf16[512,1024]{1,0:T(8,128)(2,1)S(1)} %copy-done.7, bf16[1024,4096]{1,0:T(8,128)(2,1)} %bitcast.189), kind=kOutput, calls=%fused_computation.28 | convolution fusion | flops 4315938816 | bytes 22036480 | tf_op jit(solution)/shard_map/dot_general | solution.py:337
  404.1 13.7 %fusion.59 = (f32[4096]{0:T(1024)S(1)}, bf16[512,4096]{1,0:T(8,128)(2,1)S(1)}) fusion(f32[512,4096]{1,0:T(8,128)} %get-tuple-element.65, f32[4096]{0:T(1024)S(1)} %slice_bitcast_fusion, bf16[4096,1024]{1,0:T(8,128)(2,1)} %bitcast.187, bf16[1,512,1024]{2,1,0:T(8,128)(2,1)S(1)} %copy-done.10), kind=kOutput, calls=%fused_computation.122 | convolution fusion | flops 4341100544 | bytes 22052864 | tf_op jit(solution)/shard_map/dot_general | solution.py:343
  417.8 5.0 multiply_reduce_fusion
  422.8 2.0 fusion.55
  424.8 7.7 reshape.272
  432.6 2.4 fusion.54
  435.0 1.7 convolution_convert_fusion.5
  436.7 1.3 convolution_convert_fusion.4
  438.0 1.0 copy.82
  439.1 4.4 all-to-all-start.2
  443.5 11.4 %constant_dynamic-slice_fusion.1 = (bf16[512,16,1,128]{3,2,1,0:T(2,128)(2,1)}, bf16[512,16,1,128]{3,2,1,0:T(2,128)(2,1)}) fusion(bf16[512,16,2,128]{3,2,1,0:T(2,128)(2,1)} %reshape.272, s32[]{:T(128)S(6)} %select_n.67, s32[]{:T(128)S(6)} %select_n.68), kind=kLoop, calls=%fused_computation.89 | loop fusion | bytes 8388616 | tf_op jit(solution)/shard_map/jit(dynamic_index_in_dim)/dynamic_slice | solution.py:244
  454.9 10.5 %copy.76 = bf16[512,16,1,128]{0,3,1,2:T(8,128)(2,1)} copy(bf16[512,16,1,128]{3,2,1,0:T(2,128)(2,1)} %get-tuple-element.38) | data formatting | bytes 4194304
  465.4 3.1 add_convert_fusion.3
  468.6 6.2 convolution_convert_fusion.1
  475.2 43.4 %attend_backward.1 = bf16[2048,768]{1,0:T(8,128)(2,1)} custom-call(f32[4]{0:T(128)} %multiply_exponential_fusion.slope_ref, bf16[2048,768]{1,0:T(8,128)(2,1)} %add_convert_fusion.2.q_ref.k_ref.v_ref, bf16[2048,768]{1,0:T(8,128)(2,1)} %add_convert_fusion.2.q_ref.k_ref.v_ref, bf16[2048,768]{1,0:T(8,128)(2,1)} %add_convert_fusion.2.q_ref.k_ref.v_ref, ...), custom_call_target="tpu_custom_call" | custom-call | tf_op jit(solution)/shard_map/attend_backward/pallas_call | solution.py:170
  518.6 7.2 convolution_convert_fusion.3
  525.8 1.3 copy.70
  527.2 10.5 %copy.75 = bf16[512,16,1,128]{0,3,1,2:T(8,128)(2,1)} copy(bf16[512,16,1,128]{3,2,1,0:T(2,128)(2,1)} %get-tuple-element.37) | data formatting | bytes 4194304
  537.7 7.5 add_convert_fusion
  545.7 4.9 convolution_convert_fusion
  550.6 7.1 collective-permute-done.4
  557.8 4.3 add_convert_fusion.1
  562.1 7.8 convolution_convert_fusion.2
  569.9 5.0 all-to-all-start.3
  575.5 10.9 %fusion.26 = bf16[1,512,1024]{2,1,0:T(8,128)(2,1)} fusion(f32[512,1024]{1,0:T(8,128)} %copy-done.1, bf16[512,4096]{1,0:T(8,128)(2,1)} %get-tuple-element.64, bf16[4096,1024]{1,0:T(8,128)(2,1)} %bitcast.188, f32[1024]{0:T(1024)S(1)} %add.190), kind=kOutput, calls=%fused_computation.65 | convolution fusion | flops 4296540160 | bytes 15732736 | tf_op jit(solution)/shard_map/dot_general | solution.py:341
  587.2 1.5 convert_element_type.136
  588.7 62.7 %all-to-all-done.3 = bf16[4,512,1024]{2,1,0:T(8,128)(2,1)} async-done(((bf16[4,512,1024]{2,1,0:T(8,128)(2,1)}), bf16[4,512,1024]{2,1,0:T(8,128)(2,1)}, u32[]{:S(2)}, u32[]{:S(2)}) %all-to-all-start.3) | async-done | bytes 4194336 | tf_op jit(solution)/shard_map/all_to_all | solution.py:370
  651.3 3.5 all-to-all-start.4
  654.9 4.1 convert_reduce_fusion.1
  659.0 0.7 fusion.22
  660.3 1.0 fusion.25
  661.6 41.3 %all-reduce = f32[32,384]{1,0:T(8,128)S(1)} all-reduce(f32[32,384]{1,0:T(8,128)S(1)} %concatenate.11), channel_id=7, replica_groups=mesh['seq'=4,'ring'=4,'core'=2] {'seq','ring','core'}, use_global_device_ids=true, to_apply=%region_19.20.clone | all-reduce | flops 12288 | bytes 98304
  703.5 3.6 add_bitcast_fusion
  708.8 0.9 reshape.276
  709.7 1.8 convert_element_type.144
  711.5 66.3 %reduce-scatter.9.cloned.1.call-done = bf16[32,4096]{1,0:T(8,128)(2,1)} async-done(((bf16[512,4096]{1,0:T(8,128)(2,1)}), bf16[32,4096]{1,0:T(8,128)(2,1)}) %reduce-scatter.9.cloned.1.call-update) | async-done | bytes 262160 | tf_op jit(solution)/shard_map/reduce_scatter | solution.py:256
  777.8 1.8 convert_element_type.140
  (117 shorter events, 11.6 us)
Async XLA Ops:
  7.2 61.9 %all-gather.15.cloned.1.call-start = ((), (), s32[]{:S(2)}) async-start(), calls=%async_computation.15 | async-start | bytes 1114112 | tf_op jit(solution)/shard_map/all_gather | solution.py:234
  7.9 86.5 %all-gather.13.cloned.1.call-start = ((), (), s32[]{:S(2)}) async-start(), calls=%async_computation.14 | async-start | bytes 1769472 | tf_op jit(solution)/shard_map/all_gather | solution.py:305
  20.0 128.5 %all-gather.11.cloned.1.call-start = ((), (), s32[]{:S(2)}) async-start(), calls=%async_computation.13 | async-start | bytes 5242880 | tf_op jit(solution)/shard_map/all_gather | solution.py:300
  20.7 206.3 %all-gather.19.cloned.1.call-start = ((), (), s32[]{:S(2)}) async-start(), calls=%async_computation.17 | async-start | bytes 4456448 | tf_op jit(solution)/shard_map/all_gather | solution.py:234
  21.3 282.9 %all-gather.17.cloned.1.call-start = ((), (), s32[]{:S(2)}) async-start(), calls=%async_computation.16 | async-start | bytes 4456448 | tf_op jit(solution)/shard_map/all_gather | solution.py:234
  69.1 270.7 %collective-permute-start = (bf16[16,32,1024]{2,1,0:T(8,128)(2,1)}, bf16[16,32,1024]{2,1,0:T(8,128)(2,1)}, u32[]{:S(2)}, u32[]{:S(2)}) collective-permute-start(bf16[16,32,1024]{2,1,0:T(8,128)(2,1)} %bitcast.212), channel_id=1, source_target_pairs={{0,1},{1,0},{2,3},{3,2},{4,5},{5,4},{6,7},{7,6},{8,9},{9,8},{10,11... | collective-permute-start | bytes 3145736 | tf_op jit(solution)/shard_map/ppermute | solution.py:230
  96.0 208.3 %copy-start.9 = (bf16[4,8,32,768]{3,2,1,0:T(8,128)(2,1)}, bf16[4,8,32,768]{3,2,1,0:T(8,128)(2,1)S(1)}, u32[]{:S(2)}) copy-start(bf16[4,8,32,768]{3,2,1,0:T(8,128)(2,1)S(1)} %copy.64) | copy-start | bytes 4718596
  227.1 138.3 %collective-permute-start.2 = (bf16[16,128,1024]{2,1,0:T(8,128)(2,1)}, bf16[16,128,1024]{2,1,0:T(8,128)(2,1)}, u32[]{:S(2)}, u32[]{:S(2)}) collective-permute-start(bf16[16,128,1024]{2,1,0:T(8,128)(2,1)} %bitcast.198), channel_id=1, source_target_pairs={{0,1},{1,0},{2,3},{3,2},{4,5},{5,4},{6,7},{7,6},{8,9},{9,8},{10,11... | collective-permute-start | bytes 12582920 | tf_op jit(solution)/shard_map/ppermute | solution.py:230
  304.2 73.9 %collective-permute-start.1 = (bf16[16,32,4096]{2,1,0:T(8,128)(2,1)}, bf16[16,32,4096]{2,1,0:T(8,128)(2,1)}, u32[]{:S(2)}, u32[]{:S(2)}) collective-permute-start(bf16[16,32,4096]{2,1,0:T(8,128)(2,1)} %bitcast.196), channel_id=1, source_target_pairs={{0,1},{1,0},{2,3},{3,2},{4,5},{5,4},{6,7},{7,6},{8,9},{9,8},{10,11... | collective-permute-start | bytes 12582920 | tf_op jit(solution)/shard_map/ppermute | solution.py:230
  333.4 6.4 copy-start.11
  335.8 18.2 %all-to-all-start.1 = ((bf16[4,512,256]{1,2,0:T(8,128)(2,1)}), bf16[4,512,256]{1,2,0:T(8,128)(2,1)S(1)}, u32[]{:S(2)}, u32[]{:S(2)}) async-start(bf16[4,512,256]{1,2,0:T(8,128)(2,1)} %copy.65), calls=%async_computation.1 | async-start | bytes 2097152 | tf_op jit(solution)/shard_map/all_to_all | solution.py:327
  339.8 15.2 %copy-start = (bf16[1,512,1024]{2,1,0:T(8,128)(2,1)S(1)}, bf16[1,512,1024]{2,1,0:T(8,128)(2,1)}, u32[]{:S(2)}) copy-start(bf16[1,512,1024]{2,1,0:T(8,128)(2,1)} %param.14) | copy-start | bytes 3145732
  354.0 1.0 copy-start.4
  358.3 64.5 %copy-start.1 = (f32[512,1024]{1,0:T(8,128)}, f32[512,1024]{1,0:T(8,128)S(1)}, u32[]{:S(2)}) copy-start(f32[512,1024]{1,0:T(8,128)S(1)} %get-tuple-element.63) | copy-start | bytes 6291460
  362.3 3.2 copy-start.6
  383.9 7.5 copy-start.7
  391.4 12.7 %copy-start.10 = (bf16[1,512,1024]{2,1,0:T(8,128)(2,1)S(1)}, bf16[1,512,1024]{2,1,0:T(8,128)(2,1)}, u32[]{:S(2)}) copy-start(bf16[1,512,1024]{2,1,0:T(8,128)(2,1)} %param.15) | copy-start | bytes 3145732
  391.4 26.4 %slice-start = ((s8[8388608]{0:T(1024)(128)(4,1)}), s8[4194304]{0:T(1024)(128)(4,1)S(1)}, s32[]{:S(2)}) async-start(s8[8388608]{0:T(1024)(128)(4,1)} %bitcast.190), calls=%async_computation.18 | async-start | bytes 8388608
  404.1 13.7 %slice-start.1 = ((s8[8388608]{0:T(1024)(128)(4,1)}), s8[4194304]{0:T(1024)(128)(4,1)S(1)}, s32[]{:S(2)}) async-start(s8[8388608]{0:T(1024)(128)(4,1)} %bitcast.190), calls=%async_computation.19 | async-start | bytes 8388608
  417.8 5.0 copy-start.14
  432.5 2.4 copy-start.8
  432.5 4.1 copy-start.5
  436.7 28.7 %collective-permute-start.3 = (bf16[512,1024]{1,0:T(8,128)(2,1)}, bf16[512,1024]{1,0:T(8,128)(2,1)}, u32[]{:S(2)}, u32[]{:S(2)}) collective-permute-start(bf16[512,1024]{1,0:T(8,128)(2,1)} %convolution_convert_fusion.5), channel_id=1, source_target_pairs={{0,1},{1,0},{2,3},{3,2},{4,5},{5,4},{6,7},{7,6},{8,9},{9,8},{10,11... | collective-permute-start | bytes 3145736 | tf_op jit(solution)/shard_map/ppermute | solution.py:230
  439.1 36.2 %all-to-all-start.2 = ((bf16[4,512,256]{2,1,0:T(8,128)(2,1)}), bf16[4,512,256]{2,1,0:T(8,128)(2,1)}, u32[]{:S(2)}, u32[]{:S(2)}) async-start(bf16[4,512,256]{2,1,0:T(8,128)(2,1)} %bitcast.202), calls=%async_computation.2 | async-start | bytes 2097152 | tf_op jit(solution)/shard_map/all_to_all | solution.py:358
  443.5 143.7 %reduce-scatter.7.cloned.1.call-start = ((), (), s32[]{:S(2)}) async-start(), calls=%async_computation.10 | async-start | bytes 1114112 | tf_op jit(solution)/shard_map/reduce_scatter | solution.py:256
  468.5 120.2 %reduce-scatter.5.cloned.1.call-start = ((), (), s32[]{:S(2)}) async-start(), calls=%async_computation.9 | async-start | bytes 1769472 | tf_op jit(solution)/shard_map/reduce_scatter | solution.py:379
  474.7 63.0 %collective-permute-start.5 = (bf16[2048,1024]{1,0:T(8,128)(2,1)}, bf16[2048,1024]{1,0:T(8,128)(2,1)}, u32[]{:S(2)}, u32[]{:S(2)}) collective-permute-start(bf16[2048,1024]{1,0:T(8,128)(2,1)} %convolution_convert_fusion.1), channel_id=1, source_target_pairs={{0,1},{1,0},{2,3},{3,2},{4,5},{5,4},{6,7},{7,6},{8,9},{9,8},{10,11... | collective-permute-start | bytes 12582920 | tf_op jit(solution)/shard_map/ppermute | solution.py:230
  527.1 182.6 %reduce-scatter.11.cloned.1.call-start = ((), (), s32[]{:S(2)}) async-start(), calls=%async_computation.12 | async-start | bytes 4456448 | tf_op jit(solution)/shard_map/reduce_scatter | solution.py:256
  545.2 232.6 %reduce-scatter.9.cloned.1.call-start = ((), (), s32[]{:S(2)}) async-start(), calls=%async_computation.11 | async-start | bytes 4456448 | tf_op jit(solution)/shard_map/reduce_scatter | solution.py:256
  545.6 12.1 %copy-start.12 = (bf16[512,16,1,32]{0,3,2,1:T(8,128)(2,1)S(1)}, bf16[512,16,1,32]{0,3,2,1:T(8,128)(2,1)}, u32[]{:S(2)}) copy-start(bf16[512,16,1,32]{0,3,2,1:T(8,128)(2,1)} %get-tuple-element.41) | copy-start | bytes 1572868
  545.7 12.1 %copy-start.15 = (bf16[512,4096]{1,0:T(8,128)(2,1)S(1)}, bf16[512,4096]{1,0:T(8,128)(2,1)}, u32[]{:S(2)}) copy-start(bf16[512,4096]{1,0:T(8,128)(2,1)} %copy-done.14) | copy-start | bytes 12582916
  550.5 7.2 collective-permute-start.4
  569.9 5.0 copy-start.13
  569.9 81.4 %all-to-all-start.3 = ((bf16[4,512,1024]{2,1,0:T(8,128)(2,1)}), bf16[4,512,1024]{2,1,0:T(8,128)(2,1)}, u32[]{:S(2)}, u32[]{:S(2)}) async-start(bf16[4,512,1024]{2,1,0:T(8,128)(2,1)} %bitcast.201), calls=%async_computation.3 | async-start | bytes 8388608 | tf_op jit(solution)/shard_map/all_to_all | solution.py:370
  575.5 10.9 %copy-start.3 = (bf16[2048,768]{1,0:T(8,128)(2,1)S(1)}, bf16[2048,768]{1,0:T(8,128)(2,1)}, u32[]{:S(2)}) copy-start(bf16[2048,768]{1,0:T(8,128)(2,1)} %attend_backward.1) | copy-start | bytes 9437188
  651.3 57.0 %all-to-all-start.4 = ((bf16[4,32,768]{2,1,0:T(8,128)(2,1)}), bf16[4,32,768]{2,1,0:T(8,128)(2,1)S(1)}, u32[]{:S(2)}, u32[]{:S(2)}) async-start(bf16[4,32,768]{2,1,0:T(8,128)(2,1)} %bitcast.222), calls=%async_computation.5 | async-start | bytes 393216 | tf_op jit(solution)/shard_map/all_to_all | solution.py:382
  659.0 1.3 copy-start.2
Sparse Core Ops, SparseCore 0:
  10.8 58.0 all-gather.14
  70.5 23.8 all-gather.12
  96.3 52.2 all-gather.10
  151.2 75.8 all-gather.18
  229.7 74.4 all-gather.16
  468.6 78.8 reduce-scatter.6
  549.9 31.5 reduce-scatter.4
  583.9 96.2 reduce-scatter.10
  682.6 95.1 reduce-scatter.8

commit v2 on v1

--- a/solution.py
+++ b/solution.py
@@ -32,7 +32,11 @@
     ids = lax.broadcasted_iota(jnp.int32, shape, axis)
     return (ids >= HEAD) == (half == 1)
 
-def forward_kernel(slope_ref, q_ref, k_ref, v_ref, ctx_ref, wide_ref, log_ref, q_turn, v_turn, scores):
+def estimate(micros):
+    return pl.CostEstimate(flops=int(micros * 1e8), bytes_accessed=0, transcendentals=0)
+
+def forward_kernel(slope_ref, q_ref, k_ref, v_ref, *refs):
+    ctx_ref, wide_ref, log_ref, q_turn, v_turn, scores = refs[-6:]
     head = pl.program_id(0)
     half = lax.rem(head, 2)
     length = q_ref.shape[0]
@@ -72,24 +76,23 @@
     def _():
         ctx_ref[...] = wide_ref[...].T.astype(jnp.bfloat16)
 
-def attend_forward(slopes, qkv):
-    length, triple = qkv.shape
-    heads = triple // (3 * HEAD)
-    pairs = heads // 2
-    spec = lambda part: pl.BlockSpec((length, 2 * HEAD), lambda h, part=part: (0, part * pairs + h // 2))
+def attend_forward(slopes, qkv, pair, deps=()):
+    length = qkv.shape[0]
+    spec = lambda part: pl.BlockSpec((length, 2 * HEAD), lambda h: (0, 3 * pair + part))
     return pl.pallas_call(
         forward_kernel,
-        grid=(heads,),
-        in_specs=[pl.BlockSpec(memory_space=pltpu.SMEM), spec(0), spec(1), spec(2)],
+        grid=(2,),
+        in_specs=[pl.BlockSpec(memory_space=pltpu.SMEM), spec(0), spec(1), spec(2)]
+        + [pl.BlockSpec(memory_space=pl.ANY)] * len(deps),
         out_specs=[
-            pl.BlockSpec((length, 2 * HEAD), lambda h: (0, h // 2)),
-            pl.BlockSpec((2 * HEAD, length), lambda h: (h // 2, 0)),
+            pl.BlockSpec((length, 2 * HEAD), lambda h: (0, 0)),
+            pl.BlockSpec((2 * HEAD, length), lambda h: (0, 0)),
             pl.BlockSpec((8, length), lambda h: (h, 0)),
         ],
         out_shape=[
-            jax.ShapeDtypeStruct((length, heads * HEAD), jnp.bfloat16),
-            jax.ShapeDtypeStruct((heads * HEAD, length), jnp.float32),
-            jax.ShapeDtypeStruct((heads * 8, length), jnp.float32),
+            jax.ShapeDtypeStruct((length, 2 * HEAD), jnp.bfloat16),
+            jax.ShapeDtypeStruct((2 * HEAD, length), jnp.float32),
+            jax.ShapeDtypeStruct((2 * 8, length), jnp.float32),
         ],
         scratch_shapes=[
             pltpu.VMEM((2 * HEAD, length), jnp.bfloat16),
@@ -97,16 +100,17 @@
             pltpu.VMEM((2, length // TILE, TILE, TILE), jnp.float32),
         ],
         compiler_params=pltpu.CompilerParams(vmem_limit_bytes=VMEM_BYTES),
+        cost_estimate=estimate(10.5),
         name="attend_forward",
-    )(slopes, qkv, qkv, qkv)
-
-def backward_kernel(slope_ref, q_ref, k_ref, v_ref, g_ref, wide_ref, log_ref, out_ref, q_turn, k_turn, g_turn, dq_turn, dk_sum, dv_sum):
+    )(slopes, qkv, qkv, qkv, *deps)
+
+def backward_kernel(slope_ref, q_ref, k_ref, v_ref, g_ref, wide_ref, log_ref, *refs):
+    out_ref, q_turn, k_turn, g_turn, dq_turn, dk_sum, dv_sum = refs[-7:]
     head = pl.program_id(0)
     half = lax.rem(head, 2)
     length = q_ref.shape[0]
     tiles = length // TILE
-    heads = out_ref.shape[1] // (3 * HEAD)
-    wide = heads * HEAD
+    wide = 2 * HEAD
 
     @pl.when(half == 0)
     def _():
@@ -153,31 +157,27 @@
 
         @pl.when(half == 1)
         def _():
-            lane = pl.multiple_of((head // 2) * 2 * HEAD, 2 * HEAD)
-            out_ref[span, pl.ds(wide + lane, 2 * HEAD)] = ((dk_sum[span, :] + dk) * HEAD ** -0.5).astype(jnp.bfloat16)
-            out_ref[span, pl.ds(2 * wide + lane, 2 * HEAD)] = (dv_sum[span, :] + dv).astype(jnp.bfloat16)
+            out_ref[span, wide : 2 * wide] = ((dk_sum[span, :] + dk) * HEAD ** -0.5).astype(jnp.bfloat16)
+            out_ref[span, 2 * wide :] = (dv_sum[span, :] + dv).astype(jnp.bfloat16)
 
     @pl.when(half == 1)
     def _():
-        lane = pl.multiple_of((head // 2) * 2 * HEAD, 2 * HEAD)
-        out_ref[:, pl.ds(lane, 2 * HEAD)] = (dq_turn[...] * HEAD ** -0.5).T.astype(jnp.bfloat16)
-
-def attend_backward(slopes, qkv, grad, wide, log):
-    length, triple = qkv.shape
-    heads = triple // (3 * HEAD)
-    pairs = heads // 2
-    spec = lambda part: pl.BlockSpec((length, 2 * HEAD), lambda h, part=part: (0, part * pairs + h // 2))
+        out_ref[:, :wide] = (dq_turn[...] * HEAD ** -0.5).T.astype(jnp.bfloat16)
+
+def attend_backward(slopes, qkv, grad, wide, log, pair, deps=()):
+    length = qkv.shape[0]
+    spec = lambda part: pl.BlockSpec((length, 2 * HEAD), lambda h: (0, 3 * pair + part))
     return pl.pallas_call(
         backward_kernel,
-        grid=(heads,),
+        grid=(2,),
         in_specs=[
             pl.BlockSpec(memory_space=pltpu.SMEM), spec(0), spec(1), spec(2),
-            pl.BlockSpec((length, 2 * HEAD), lambda h: (0, h // 2)),
-            pl.BlockSpec((2 * HEAD, length), lambda h: (h // 2, 0)),
+            pl.BlockSpec((length, 2 * HEAD), lambda h: (0, pair)),
+            pl.BlockSpec((2 * HEAD, length), lambda h: (0, 0)),
             pl.BlockSpec((8, length), lambda h: (h, 0)),
-        ],
-        out_specs=pl.BlockSpec((length, triple), lambda h: (0, 0)),
-        out_shape=jax.ShapeDtypeStruct((length, triple), jnp.bfloat16),
+        ] + [pl.BlockSpec(memory_space=pl.ANY)] * len(deps),
+        out_specs=pl.BlockSpec((length, 6 * HEAD), lambda h: (0, 0)),
+        out_shape=jax.ShapeDtypeStruct((length, 6 * HEAD), jnp.bfloat16),
         scratch_shapes=[
             pltpu.VMEM((2 * HEAD, length), jnp.bfloat16),
             pltpu.VMEM((2 * HEAD, length), jnp.bfloat16),
@@ -187,8 +187,546 @@
             pltpu.VMEM((length, 2 * HEAD), jnp.float32),
         ],
         compiler_params=pltpu.CompilerParams(vmem_limit_bytes=VMEM_BYTES),
+        cost_estimate=estimate(22),
         name="attend_backward",
-    )(slopes, qkv, qkv, qkv, grad, wide, log)
+    )(slopes, qkv, qkv, qkv, grad, wide, log, *deps)
+
+GELU_RATE = math.sqrt(2.0 / math.pi)
+GELU_CUBE = 0.044715
+CONTRACT_LAST = (((1,), (1,)), ((), ()))
+
+
+def feed_forward_kernel(groups, table_ref, x_ref, g_ref, bias_ref, *refs):
+    outs, scratch = refs[-11:-4], refs[-4:]
+    chips = table_ref.shape[0] // 2
+    down_refs, up_refs = refs[: 2 * groups], refs[2 * groups : -11]
+    up_groups = len(up_refs) // 2
+    layer_ref, back_ref, down_keep, down_send, up_keep, up_send, bias_out = outs
+    x_turn, up_tile, down_tile, grad_tile = scratch
+    step = pl.program_id(0)
+    core = table_ref[2 * chips]
+    size = chips // groups
+    owned = up_refs[0].shape[1]
+    span = down_refs[0].shape[1]
+
+    @pl.when(step == 0)
+    def _():
+        x_turn[...] = x_ref[...].T
+        layer_ref[...] = jnp.zeros_like(layer_ref)
+        back_ref[...] = jnp.zeros_like(back_ref)
+
+    def up_rows(place, who):
+        start = table_ref[chips + place] * (CORES * owned) + who * owned
+        return pl.ds(pl.multiple_of(start, owned), owned)
+
+    for place in range(chips):
+        group, at = divmod(place, chips // up_groups)
+        up_tile[up_rows(place, core), :] = up_refs[group][at]
+        up_tile[up_rows(place, 1 - core), :] = up_refs[up_groups + group][at]
+
+    def down_rows(who):
+        return pl.ds(pl.multiple_of(who * span, span), span)
+
+    for group in range(groups):
+
+        @pl.when(step // size == group)
+        def _():
+            down_tile[down_rows(core), :] = down_refs[group][0]
+            down_tile[down_rows(1 - core), :] = down_refs[groups + group][0]
+
+    upper = _dot(x_ref[...], up_tile[...]) + bias_ref[...]
+    square = upper * upper
+    turned = jnp.tanh(GELU_RATE * (upper + GELU_CUBE * upper * square))
+    lift = 0.5 * (1.0 + turned)
+    slope = lift + 0.5 * upper * (1.0 - turned * turned) * (GELU_RATE * (1.0 + 3.0 * GELU_CUBE * square))
+    hidden = (upper * lift).astype(jnp.bfloat16)
+    grad_upper = lax.dot_general(
+        g_ref[...], down_tile[...], CONTRACT_LAST, preferred_element_type=jnp.float32
+    ) * slope
+    bias_out[...] = jnp.sum(grad_upper, axis=0, keepdims=True)
+    upper_low = grad_upper.astype(jnp.bfloat16)
+    layer_ref[...] += _dot(hidden, down_tile[...])
+    back_ref[...] += lax.dot_general(
+        upper_low, up_tile[...], CONTRACT_LAST, preferred_element_type=jnp.float32
+    )
+    grad_tile[...] = _dot(hidden.T, g_ref[...]).astype(jnp.bfloat16)
+    down_keep[0] = grad_tile[down_rows(core), :]
+    down_send[0] = grad_tile[down_rows(1 - core), :]
+    up_tile[...] = _dot(x_turn[...], upper_low).astype(jnp.bfloat16)
+    for place in range(chips):
+        up_keep[place] = up_tile[up_rows(place, core), :]
+        up_send[place] = up_tile[up_rows(place, 1 - core), :]
+
+
+def group_place(group, size):
+    return lambda s, *t: (jnp.clip(s - group * size, 0, size - 1), 0, 0)
+
+
+def feed_forward(table, x, g, bias, down, up):
+    tokens, width = x.shape
+    groups = len(down) // 2
+    size = down[0].shape[0]
+    owned, inner = up[0].shape[1:]
+    chips = groups * size
+    span = inner // (chips * CORES)
+    tile = CORES * span
+    whole = lambda s, t: (0, 0)
+    column = lambda s, t: (0, t[s])
+    columns = lambda s, t: (0, 0, t[s])
+    down_spec = lambda place: pl.BlockSpec((1, span, width), place)
+    up_spec = pl.BlockSpec((up[0].shape[0], owned, tile), columns)
+    shape = jax.ShapeDtypeStruct
+    return pl.pallas_call(
+        functools.partial(feed_forward_kernel, groups),
+        grid_spec=pltpu.PrefetchScalarGridSpec(
+            num_scalar_prefetch=1,
+            grid=(chips,),
+            in_specs=[
+                pl.BlockSpec((tokens, width), whole),
+                pl.BlockSpec((tokens, width), whole),
+                pl.BlockSpec((1, tile), column),
+            ]
+            + [down_spec(group_place(group, size)) for group in range(groups)] * 2
+            + [up_spec] * len(up),
+            out_specs=[
+                pl.BlockSpec((tokens, width), whole),
+                pl.BlockSpec((tokens, width), whole),
+                down_spec(lambda s, t: (s, 0, 0)),
+                down_spec(lambda s, t: (s, 0, 0)),
+                pl.BlockSpec((chips, owned, tile), columns),
+                pl.BlockSpec((chips, owned, tile), columns),
+                pl.BlockSpec((1, tile), column),
+            ],
+            scratch_shapes=[
+                pltpu.VMEM((width, tokens), jnp.bfloat16),
+                pltpu.VMEM((width, tile), jnp.bfloat16),
+                pltpu.VMEM((tile, width), jnp.bfloat16),
+                pltpu.VMEM((tile, width), jnp.bfloat16),
+            ],
+        ),
+        out_shape=[
+            shape((tokens, width), jnp.float32),
+            shape((tokens, width), jnp.float32),
+            shape((chips, span, width), jnp.bfloat16),
+            shape((chips, span, width), jnp.bfloat16),
+            shape((chips, owned, inner), jnp.bfloat16),
+            shape((chips, owned, inner), jnp.bfloat16),
+            shape((1, inner), jnp.float32),
+        ],
+        compiler_params=pltpu.CompilerParams(vmem_limit_bytes=VMEM_BYTES),
+        cost_estimate=estimate(45),
+        name="feed_forward",
+    )(table, x, g, bias, *down, *up)
+
+
+def bits_of(size):
+    return [1 << b for b in range(size.bit_length() - 1)]
+
+
+def swap(value, step):
+    axis, bit = step
+    return lax.ppermute(value, axis, [(i, i ^ bit) for i in range(lax.axis_size(axis))])
+
+
+def other_core(value):
+    return swap(value, ("core", 1))
+
+
+def offsets_of(steps, rings):
+    found = [0]
+    for axis, bit in steps:
+        found = found + [o ^ (bit * rings if axis == "seq" else bit) for o in found]
+    return found
+
+
+def grow(value, steps):
+    for step in steps:
+        value = jnp.concatenate((value, swap(value, step)), axis=0)
+    return value
+
+
+def after(values, *others):
+    values = tuple(values)
+    return pl.pallas_call(
+        lambda *refs: None,
+        in_specs=[pl.BlockSpec(memory_space=pl.ANY)] * (len(values) + len(others)),
+        out_specs=[pl.BlockSpec(memory_space=pl.ANY)] * len(values),
+        out_shape=[jax.ShapeDtypeStruct(value.shape, value.dtype) for value in values],
+        input_output_aliases={i: i for i in range(len(values))},
+        name="after",
+    )(*values, *others)
+
+
+def direct(value, axis):
+    return [value] + [swap(value, (axis, m)) for m in range(1, lax.axis_size(axis))]
+
+
+def add_low(left, right):
+    return (left.astype(jnp.float32) + right.astype(jnp.float32)).astype(jnp.bfloat16)
+
+
+def collect(groups, axis):
+    total = groups[0].astype(jnp.float32)
+    for m in range(1, len(groups)):
+        total = total + swap(groups[m], (axis, m)).astype(jnp.float32)
+    return total
+
+
+def collect_next(total, axis):
+    low = total.astype(jnp.bfloat16)
+    own = total[0]
+    for m in range(1, total.shape[0]):
+        own = own + swap(low[m], (axis, m)).astype(jnp.float32)
+    return own
+
+
+def spread(blocks, axis):
+    me = lax.axis_index(axis)
+    out = jnp.zeros_like(blocks)
+    for m in range(lax.axis_size(axis)):
+        block = lax.dynamic_slice_in_dim(blocks, me ^ m, 1, 0)
+        came = block if m == 0 else swap(block, (axis, m))
+        out = lax.dynamic_update_slice_in_dim(out, came, me ^ m, 0)
+    return out
+
+
+def group_columns(weight, ways):
+    rows = weight.shape[0]
+    parts = weight.reshape(rows, 3, ways, -1, 2 * HEAD)
+    return jnp.transpose(parts, (2, 0, 3, 1, 4)).reshape(ways, rows, -1)
+
+
+def ungroup_columns(grouped):
+    ways, rows, _ = grouped.shape
+    parts = grouped.reshape(ways, rows, -1, 3, 2 * HEAD)
+    return jnp.transpose(parts, (1, 3, 0, 2, 4)).reshape(rows, -1)
+
+
+def pair_columns(bias, seq_index, ways):
+    parts = bias.reshape(2, ways, -1, 2 * HEAD)
+    mine = lax.dynamic_index_in_dim(parts, seq_index, 1, keepdims=False)
+    return jnp.stack((mine[0], jnp.zeros_like(mine[0]), mine[1]), axis=1).reshape(-1)
+
+
+def unpair_columns(sums, seq_index, ways):
+    parts = sums.reshape(-1, 3, 2 * HEAD)
+    mine = jnp.stack((parts[:, 0], parts[:, 2]))
+    out = jnp.zeros((2, ways) + mine.shape[1:], jnp.float32)
+    return lax.dynamic_update_slice_in_dim(out, mine[:, None], seq_index, 1).reshape(-1)
+
+
+def norm_parts(values):
+    centre = values - jnp.mean(values, axis=-1, keepdims=True)
+    factor = lax.rsqrt(jnp.mean(centre * centre, axis=-1, keepdims=True) + EPSILON)
+    return centre * factor, factor
+
+
+def norm_back(grad, gain, unit, factor):
+    turned = grad * gain
+    inner = jnp.mean(turned * unit, axis=-1, keepdims=True)
+    return factor * (turned - jnp.mean(turned, axis=-1, keepdims=True) - unit * inner)
+
+
+def project_kernel(ways, table_ref, *refs):
+    rows, w_ref, gain_ref, shift_ref, bias_ref = refs[:5]
+    qkv_ref, normed_ref, unit_ref, weight_ref = refs[-4:]
+    step = pl.program_id(0)
+    copies = w_ref.shape[0]
+    owned = weight_ref.shape[0] // (ways * copies)
+
+    @pl.when(step == 0)
+    def _():
+        for place in range(copies):
+            for sender in range(ways):
+                start = (sender * copies + (table_ref[1] ^ place)) * owned
+                weight_ref[pl.ds(pl.multiple_of(start, owned), owned), :] = w_ref[place, sender, :owned, :]
+
+    unit, _ = norm_parts(rows[...].astype(jnp.float32))
+    normed = (unit * gain_ref[...] + shift_ref[...]).astype(jnp.bfloat16)
+    unit_ref[...] = unit.astype(jnp.bfloat16)
+    normed_ref[...] = normed
+    qkv_ref[...] = (_dot(normed, weight_ref[...]) + bias_ref[...]).astype(jnp.bfloat16)
+
+
+def project(table, tokens, packed, gain, shift, bias, ways, owned, deps=()):
+    width = tokens.shape[1]
+    local = tokens.shape[0] // ways
+    copies, _, _, triple = packed.shape
+    whole = lambda s, t: (0, 0)
+    place = lambda s, t: (s, 0)
+    full = lambda array: pl.BlockSpec(array.shape, lambda s, t: (0,) * array.ndim)
+    operands = (packed, gain, shift, bias)
+    shape = jax.ShapeDtypeStruct
+    length = ways * local
+    return pl.pallas_call(
+        functools.partial(project_kernel, ways),
+        grid_spec=pltpu.PrefetchScalarGridSpec(
+            num_scalar_prefetch=1,
+            grid=(ways,),
+            in_specs=[pl.BlockSpec((local, width), place)]
+            + [full(array) for array in operands]
+            + [pl.BlockSpec(memory_space=pl.ANY)] * len(deps),
+            out_specs=[
+                pl.BlockSpec((local, triple), place),
+                pl.BlockSpec((local, width), place),
+                pl.BlockSpec((local, width), place),
+                pl.BlockSpec((width, triple), whole),
+            ],
+        ),
+        out_shape=[
+            shape((length, triple), jnp.bfloat16),
+            shape((length, width), jnp.bfloat16),
+            shape((length, width), jnp.bfloat16),
+            shape((width, triple), jnp.bfloat16),
+        ],
+        compiler_params=pltpu.CompilerParams(vmem_limit_bytes=VMEM_BYTES),
+        cost_estimate=estimate(9),
+        name="project",
+    )(table, tokens, *operands, *deps)
+
+
+def input_grad_kernel(low_ref, high_ref, w_ref, normed_ref, unit_ref, *refs):
+    part_ref, weight_ref, sum_ref, bias_ref, total = refs[-5:]
+    step = pl.program_id(0)
+
+    @pl.when(step == 0)
+    def _():
+        total[...] = jnp.zeros_like(total)
+        sum_ref[...] = jnp.zeros_like(sum_ref)
+        bias_ref[...] = jnp.zeros_like(bias_ref)
+
+    grad = jnp.concatenate((low_ref[...], high_ref[...]), axis=1)
+    part = lax.dot_general(grad, w_ref[...], CONTRACT_LAST, preferred_element_type=jnp.float32)
+    part_ref[...] = part.astype(jnp.bfloat16)
+    total[...] += _dot(normed_ref[...].T, grad)
+    sum_ref[0:1] += jnp.sum(part * unit_ref[...].astype(jnp.float32), axis=0, keepdims=True)
+    sum_ref[1:2] += jnp.sum(part, axis=0, keepdims=True)
+    bias_ref[0:1] += jnp.sum(grad.astype(jnp.float32), axis=0, keepdims=True)
+
+    @pl.when(step == pl.num_programs(0) - 1)
+    def _():
+        weight_ref[...] = total[...].astype(jnp.bfloat16)
+
+
+def input_grad(low, high, weight, normed, unit, deps=()):
+    length, width = normed.shape
+    triple = weight.shape[1]
+    rows = 512
+    block = lambda columns: pl.BlockSpec((rows, columns), lambda s: (s, 0))
+    whole = lambda *size: pl.BlockSpec(size, lambda s: (0, 0))
+    shape = jax.ShapeDtypeStruct
+    return pl.pallas_call(
+        input_grad_kernel,
+        grid=(length // rows,),
+        in_specs=[block(triple // 2), block(triple // 2), whole(width, triple), block(width), block(width)]
+        + [pl.BlockSpec(memory_space=pl.ANY)] * len(deps),
+        out_specs=[block(width), whole(width, triple), whole(8, width), whole(8, triple)],
+        out_shape=[
+            shape((length, width), jnp.bfloat16),
+            shape((width, triple), jnp.bfloat16),
+            shape((8, width), jnp.float32),
+            shape((8, triple), jnp.float32),
+        ],
+        scratch_shapes=[pltpu.VMEM((width, triple), jnp.float32)],
+        compiler_params=pltpu.CompilerParams(vmem_limit_bytes=VMEM_BYTES),
+        cost_estimate=estimate(10),
+        name="input_grad",
+    )(low, high, weight, normed, unit, *deps)
+
+
+def output_rows(table_ref, place, who, owned):
+    start = table_ref[place] * (CORES * owned) + who * owned
+    return pl.ds(pl.multiple_of(start, owned), owned)
+
+
+def join_groups(ref):
+    return jnp.concatenate([ref[s] for s in range(ref.shape[0])], axis=1)
+
+
+def output_kernel(table_ref, context_ref, x_ref, bias_ref, gain_ref, shift_ref, *refs):
+    residual_ref, normed_ref, weight_ref = refs[-3:]
+    parts = refs[:-3]
+    groups = len(parts) // 2
+    size, owned, _ = parts[0].shape
+    core = table_ref[2 * groups * size]
+
+    @pl.when(pl.program_id(0) == 0)
+    def _():
+        for place in range(groups * size):
+            group, at = divmod(place, size)
+            weight_ref[output_rows(table_ref, place, core, owned), :] = parts[group][at]
+            weight_ref[output_rows(table_ref, place, 1 - core, owned), :] = parts[groups + group][at]
+
+    branch = _dot(join_groups(context_ref), weight_ref[...]) + bias_ref[...]
+    residual = x_ref[...].astype(jnp.float32) + branch
+    residual_ref[...] = residual
+    unit, _ = norm_parts(residual)
+    normed_ref[...] = (unit * gain_ref[...] + shift_ref[...]).astype(jnp.bfloat16)
+
+
+def project_output(table, context, parts, first, x, bias, gain, shift):
+    local, width = x.shape
+    ways = context.shape[0]
+    rows = 256
+    vector = pl.BlockSpec((1, width), lambda s, t: (0, 0))
+    block = pl.BlockSpec((rows, width), lambda s, t: (s, 0))
+    heads = pl.BlockSpec((ways, rows, width // ways), lambda s, t: (0, s, 0))
+    size, total, _ = parts[0].shape
+    owned = total - first
+    weight = pl.BlockSpec((size, owned, width), lambda s, t: (0, first // owned, 0))
+    shape = jax.ShapeDtypeStruct
+    return pl.pallas_call(
+        output_kernel,
+        grid_spec=pltpu.PrefetchScalarGridSpec(
+            num_scalar_prefetch=1,
+            grid=(local // rows,),
+            in_specs=[heads, block, vector, vector, vector] + [weight] * len(parts),
+            out_specs=[block, block, pl.BlockSpec((width, width), lambda s, t: (0, 0))],
+        ),
+        out_shape=[
+            shape((local, width), jnp.float32),
+            shape((local, width), jnp.bfloat16),
+            shape((width, width), jnp.bfloat16),
+        ],
+        compiler_params=pltpu.CompilerParams(vmem_limit_bytes=VMEM_BYTES),
+        cost_estimate=estimate(5),
+        name="project_output",
+    )(table, context, x, bias, gain, shift, *parts)
+
+
+def residual_kernel(table_ref, grad_ref, residual_ref, up_ref, context_ref, w_ref, gain_ref, *refs):
+    out_ref, context_grad_ref, keep_ref, send_ref, sum_ref, total, held = refs[-7:]
+    step = pl.program_id(0)
+    chips, owned, _ = keep_ref.shape
+    ways = context_ref.shape[0]
+    core = table_ref[2 * chips]
+
+    @pl.when(step == 0)
+    def _():
+        total[...] = jnp.zeros_like(total)
+        sum_ref[...] = jnp.zeros_like(sum_ref)
+
+    unit, factor = norm_parts(residual_ref[...])
+    grad = grad_ref[...]
+    upstream = up_ref[...].astype(jnp.float32)
+    through = upstream + norm_back(grad, gain_ref[...], unit, factor)
+    out_ref[...] = through
+    branch = through.astype(jnp.bfloat16)
+    context_grad = lax.dot_general(
+        branch, w_ref[...], CONTRACT_LAST, preferred_element_type=jnp.float32
+    ).astype(jnp.bfloat16)
+    wide = context_grad.shape[1] // ways
+    for s in range(ways):
+        context_grad_ref[s] = context_grad[:, s * wide : (s + 1) * wide]
+    total[...] += _dot(join_groups(context_ref).T, branch)
+    for row, term in enumerate((grad * unit, grad, through, upstream)):
+        sum_ref[row : row + 1] += jnp.sum(term, axis=0, keepdims=True)
+
+    @pl.when(step == pl.num_programs(0) - 1)
+    def _():
+        held[...] = total[...].astype(jnp.bfloat16)
+        for place in range(chips):
+            keep_ref[place] = held[output_rows(table_ref, place, core, owned), :]
+            send_ref[place] = held[output_rows(table_ref, place, 1 - core, owned), :]
+
+
+def residual_grad(table, grad, residual, upstream, context, weight, gain, chips):
+    local, width = residual.shape
+    ways = context.shape[0]
+    rows = 256
+    owned = width // (chips * CORES)
+    whole = lambda *size: pl.BlockSpec(size, lambda s, t: (0,) * len(size))
+    block = pl.BlockSpec((rows, width), lambda s, t: (s, 0))
+    heads = pl.BlockSpec((ways, rows, width // ways), lambda s, t: (0, s, 0))
+    shape = jax.ShapeDtypeStruct
+    return pl.pallas_call(
+        residual_kernel,
+        grid_spec=pltpu.PrefetchScalarGridSpec(
+            num_scalar_prefetch=1,
+            grid=(local // rows,),
+            in_specs=[block, block, block, heads, whole(width, width), whole(1, width)],
+            out_specs=[block, heads, whole(chips, owned, width), whole(chips, owned, width), whole(8, width)],
+            scratch_shapes=[pltpu.VMEM((width, width), jnp.float32), pltpu.VMEM((width, width), jnp.bfloat16)],
+        ),
+        out_shape=[
+            shape((local, width), jnp.float32),
+            shape((ways, local, width // ways), jnp.bfloat16),
+            shape((chips, owned, width), jnp.bfloat16),
+            shape((chips, owned, width), jnp.bfloat16),
+            shape((8, width), jnp.float32),
+        ],
+        compiler_params=pltpu.CompilerParams(vmem_limit_bytes=VMEM_BYTES),
+        cost_estimate=estimate(7),
+        name="residual_grad",
+    )(table, grad, residual, upstream, context, weight, gain)
+
+
+def meet_kernel(groups, up_groups, down_keep, down_came, output_keep, output_came, up_keep, up_came, *refs):
+    step = pl.program_id(0)
+    size = pl.num_programs(0) // groups
+    span = down_keep.shape[1]
+
+    def both(left, right):
+        return (left[0].astype(jnp.float32) + right[0].astype(jnp.float32)).astype(jnp.bfloat16)
+
+    for group in range(groups):
+
+        @pl.when(step // size == group)
+        def _():
+            refs[group][0, :span] = both(down_keep, down_came)
+            refs[group][0, span:] = both(output_keep, output_came)
+
+    for group in range(up_groups):
+
+        @pl.when(step // (pl.num_programs(0) // up_groups) == group)
+        def _():
+            refs[groups + group][0] = both(up_keep, up_came)
+
+
+def meet(down_keep, down_came, output_keep, output_came, up_keep, up_came, groups, up_groups):
+    chips, span, width = down_keep.shape
+    owned, inner = up_keep.shape[1:]
+    block = lambda rows, columns: pl.BlockSpec((1, rows, columns), lambda s: (s, 0, 0))
+    parts = [(span + owned, width, chips // groups, group) for group in range(groups)]
+    parts += [(owned, inner, chips // up_groups, group) for group in range(up_groups)]
+    outs = [pl.BlockSpec((1, rows, columns), group_place(group, size)) for rows, columns, size, group in parts]
+    shapes = [jax.ShapeDtypeStruct((size, rows, columns), jnp.bfloat16) for rows, columns, size, _ in parts]
+    return pl.pallas_call(
+        functools.partial(meet_kernel, groups, up_groups),
+        grid=(chips,),
+        in_specs=[block(span, width)] * 2 + [block(owned, width)] * 2 + [block(owned, inner)] * 2,
+        out_specs=outs,
+        out_shape=shapes,
+        compiler_params=pltpu.CompilerParams(vmem_limit_bytes=VMEM_BYTES),
+        cost_estimate=estimate(9),
+        name="meet",
+    )(down_keep, down_came, output_keep, output_came, up_keep, up_came)
+
+
+def halve(value, step, kind):
+    axis, bit = step
+    mine = (lax.axis_index(axis) // bit) % 2
+    sent = lax.dynamic_index_in_dim(value, 1 - mine, 0, keepdims=False).astype(kind)
+    kept = lax.dynamic_index_in_dim(value, mine, 0, keepdims=False)
+    return kept.astype(jnp.float32) + swap(sent, step).astype(jnp.float32)
+
+
+def scatter_copies(value, kind):
+    rings = lax.axis_size("ring")
+    value = jnp.moveaxis(value.reshape((rings, CORES) + value.shape[1:]), 1, 0)
+    value = halve(value, ("core", 1), kind)
+    for bit in bits_of(rings):
+        shape = value.shape
+        value = jnp.moveaxis(value.reshape((shape[0] // 2, 2) + shape[1:]), 1, 0)
+        value = halve(value, ("ring", bit), kind)
+    return value[0]
+
+
+def scatter_seq(value, kind):
+    for bit in reversed(bits_of(lax.axis_size("seq"))):
+        value = halve(value.reshape((2, value.shape[0] // 2) + value.shape[1:]), ("seq", bit), kind)
+    return value[0]
+
 
 def layer_norm(values, norm_gain, norm_shift):
     centre = values - jnp.mean(values, axis=-1, keepdims=True)
@@ -226,10 +764,6 @@
     return out
 
 
-def other_core(value):
-    return lax.ppermute(value, "core", [(0, 1), (1, 0)])
-
-
 def gather_weight(shard):
     mine = lax.all_gather(shard, CHIPS, axis=0, tiled=False)
     theirs = other_core(mine)
@@ -256,7 +790,7 @@
     return lax.psum_scatter(both, CHIPS, scatter_dimension=0, tiled=True).astype(jnp.float32)
 
 
-def body(
+def plain_body(
     tokens_in,
     out_grad,
     first_gain,
@@ -299,8 +833,7 @@
 
     all_rows = lax.all_gather(rows_in, "seq", axis=0, tiled=True)
     owned_rows = input_weight.shape[0]
-    by_group = input_weight.reshape(owned_rows, 3, ways, group_width)
-    by_group = jnp.moveaxis(by_group, 2, 0).reshape(ways, owned_rows, 3 * group_width)
+    by_group = group_columns(input_weight, ways)
     columns = lax.all_to_all(by_group, "seq", split_axis=0, concat_axis=0, tiled=True)
     columns = lax.all_gather(columns, ("ring", "core"), axis=0, tiled=False)
     weight_input = jnp.moveaxis(columns, 0, 1).reshape(model_width, 3 * group_width)
@@ -310,20 +843,15 @@
     weight_down = gather_weight(down_weight)
 
     normed = layer_norm(all_rows.astype(jnp.float32), gain_first, shift_first).astype(jnp.bfloat16)
-    start = seq_index * group_width
-    bias_group = jnp.concatenate(
-        (
-            lax.dynamic_slice_in_dim(bias_input, start, group_width),
-            jnp.zeros((group_width,), jnp.float32),
-            lax.dynamic_slice_in_dim(bias_input, model_width + start, group_width),
-        )
-    )
+    bias_group = pair_columns(bias_input, seq_index, ways)
     qkv = (jnp.dot(normed, weight_input, preferred_element_type=jnp.float32) + bias_group).astype(
         jnp.bfloat16
     )
     head_ids = (seq_index * head_group + jnp.arange(head_group, dtype=jnp.int32)).astype(jnp.float32)
     slopes = jnp.exp2(-8.0 * (head_ids + 1.0) / HEADS)
-    context_split, wide, log_totals = attend_forward(slopes, qkv)
+    pairs = range(head_group // 2)
+    kept = [attend_forward(slopes[2 * p : 2 * p + 2], qkv, p) for p in pairs]
+    context_split = jnp.concatenate([k[0] for k in kept], axis=1)
     context = lax.all_to_all(
         context_split.reshape(ways, local, group_width), "seq", split_axis=0, concat_axis=0, tiled=True
     )
@@ -362,7 +890,15 @@
     grad_up_weight = scatter_weight_grad(normed_two, upper_low, chips)
     grad_output_weight = scatter_weight_grad(context, branch_low, chips)
 
-    grad_qkv = attend_backward(slopes, qkv, grad_split, wide, log_totals)
+    grad_qkv = jnp.concatenate(
+        [
+            attend_backward(
+                slopes[2 * p : 2 * p + 2], qkv, grad_split, kept[p][1], kept[p][2], p
+            )
+            for p in pairs
+        ],
+        axis=1,
+    )
 
     grad_normed = lax.dot_general(
         grad_qkv, weight_input, (((1,), (1,)), ((), ())), preferred_element_type=jnp.float32
@@ -382,17 +918,8 @@
     grad_columns = lax.all_to_all(
         grad_columns.reshape(ways, owned_rows, 3 * group_width), "seq", split_axis=0, concat_axis=0, tiled=True
     )
-    grad_input_weight = jnp.moveaxis(
-        grad_columns.reshape(ways, owned_rows, 3, group_width), 0, 2
-    ).reshape(owned_rows, 3 * model_width).astype(jnp.float32)
-
-    bias_sums = jnp.sum(grad_qkv.astype(jnp.float32), axis=0)
-    empty = jnp.zeros((2 * model_width,), jnp.float32)
-    grad_input_bias = lax.dynamic_update_slice(empty, bias_sums[:group_width], (start,))
-    grad_input_bias = lax.dynamic_update_slice(
-        grad_input_bias, bias_sums[2 * group_width :], (model_width + start,)
-    )
-
+    grad_input_weight = ungroup_columns(grad_columns).astype(jnp.float32)
+    grad_input_bias = unpair_columns(jnp.sum(grad_qkv.astype(jnp.float32), axis=0), seq_index, ways)
     _, first_back = jax.vjp(layer_norm, inputs, gain_first, shift_first)
     grad_entry, grad_first_gain, grad_first_shift = first_back(grad_normed)
     tokens_grad = grad_residual + grad_entry
@@ -428,6 +955,185 @@
     )
 
 
+def blocked_body(
+    tokens_in,
+    out_grad,
+    first_gain,
+    first_shift,
+    input_weight,
+    input_bias,
+    output_weight,
+    output_bias,
+    second_gain,
+    second_shift,
+    up_weight,
+    up_bias,
+    down_weight,
+    down_bias,
+):
+    ways = lax.axis_size("seq")
+    rings = lax.axis_size("ring")
+    chips = ways * rings
+    copies = rings * CORES
+    world = chips * CORES
+    model_width = tokens_in.shape[-1]
+    head_group = model_width // ways // HEAD
+    rows_in = tokens_in.reshape(-1, model_width)
+    local = rows_in.shape[0]
+    length = local * ways
+    upstream = out_grad.reshape(local, model_width)
+    seq_index = lax.axis_index("seq")
+    core = lax.axis_index("core")
+    chip_index = seq_index * rings + lax.axis_index("ring")
+    copy_index = lax.axis_index("ring") * CORES + core
+
+    ring = lax.axis_index("ring")
+    far_bit, near_bit = rings // 2, 1
+    down_away = [s * rings + r for s in range(ways) for r in range(rings)]
+    up_away = [s * rings + near + far for near in (0, near_bit) for s in range(ways) for far in (0, far_bit)]
+    down_table, up_table = (jnp.array(away, jnp.int32) ^ chip_index for away in (down_away, up_away))
+    table = jnp.concatenate((down_table, up_table, core[None]))
+
+    vectors = (first_gain, first_shift, input_bias, output_bias, second_gain, second_shift, up_bias, down_bias)
+    sizes = [vector.shape[0] for vector in vectors]
+    owned = input_weight.shape[0]
+    by_group = group_columns(input_weight, ways)
+    triple = by_group.shape[-1]
+    packed = jnp.concatenate([jnp.pad(vector, (0, 128 - vector.shape[0]))[None] for vector in vectors])
+    packed = jnp.pad(packed, ((0, 8 - len(sizes)), (0, triple - 128)))
+    by_group = jnp.concatenate((by_group, jnp.broadcast_to(packed[None], (ways, 8, triple))), axis=1)
+    owned_down = down_weight.shape[0]
+    down_shard = jnp.concatenate((down_weight, output_weight))
+    grouped = spread(by_group, "seq")
+    columns = grouped[None]
+    for bit in (far_bit, near_bit):
+        columns = jnp.stack((columns, swap(columns, ("ring", bit))), axis=1).reshape((-1,) + by_group.shape)
+    up_one = jnp.stack((up_weight, swap(up_weight, ("ring", far_bit))))
+    down_one = jnp.stack(direct(down_shard, "ring"))
+    columns = jnp.stack((columns, other_core(columns)), axis=1).reshape((copies,) + by_group.shape)
+    found = columns[:, :, owned : owned + len(sizes), :128].reshape(world, -1)
+    here = jnp.arange(world, dtype=jnp.int32)
+    wanted = ((here % copies) ^ copy_index) * ways + here // copies
+    pick = (wanted[:, None] == here[None, :]).astype(jnp.bfloat16)
+    found = jnp.dot(pick, found, preferred_element_type=jnp.float32)
+    vectors = [found[:, 128 * i : 128 * i + size].reshape(1, -1) for i, size in enumerate(sizes)]
+    gain_first, shift_first, bias_input, bias_output, gain_second, shift_second, bias_up, bias_down = vectors
+    bias_group = pair_columns(bias_input[0], seq_index, ways)[None]
+
+    all_rows = lax.all_gather(rows_in, "seq", tiled=True)
+
+    up_near = jnp.concatenate(direct(up_one, "seq"))
+    (down_one,) = after((down_one,), all_rows)
+    (up_near,) = after((up_near,), columns)
+    down_mine = direct(down_one, "seq")
+    up_far = swap(up_near, ("ring", near_bit))
+
+    places = jnp.stack((seq_index, copy_index)).astype(jnp.int32)
+    qkv, normed, unit, weight_input = project(
+        places, all_rows, columns, gain_first, shift_first, bias_group, ways, owned, (down_one, up_near)
+    )
+    head_ids = (seq_index * head_group + jnp.arange(head_group, dtype=jnp.int32)).astype(jnp.float32)
+    slopes = jnp.exp2(-8.0 * (head_ids + 1.0) / HEADS)
+
+    def exchange(value):
+        return lax.all_to_all(
+            value.reshape(ways, local, -1), "seq", split_axis=0, concat_axis=0, tiled=True
+        )
+
+    kept, contexts, done = [], [], ()
+    for pair in range(2):
+        context, wide, log_totals = attend_forward(slopes[2 * pair : 2 * pair + 2], qkv, pair, done)
+        kept.append((wide, log_totals))
+        contexts.append(context)
+        done = (log_totals,)
+    context = exchange(jnp.concatenate(contexts, axis=1))
+
+    mine = list(after(down_mine + [up_near, up_far], context))
+    theirs = [other_core(group) for group in mine]
+    down = mine[:ways] + theirs[:ways]
+    up = mine[ways:] + theirs[ways:]
+    residual, normed_two, weight_output = project_output(
+        table, context, down, owned_down, rows_in, bias_output, gain_second, shift_second
+    )
+    layer, grad_normed_two, down_keep, down_send, up_keep, up_send, grad_up_bias = feed_forward(
+        table, normed_two, upstream, bias_up, down, up
+    )
+    grad_residual, context_grad, output_keep, output_send, middle_sums = residual_grad(
+        table, grad_normed_two, residual, upstream, context, weight_output, gain_second, chips
+    )
+    layer_out = (residual + layer + bias_down).astype(jnp.bfloat16)
+
+    context_grad = exchange(context_grad).reshape(length, -1)
+    met = list(
+        meet(down_keep, other_core(down_send), output_keep, other_core(output_send), up_keep, other_core(up_send), ways, 2)
+    )
+    met = list(after(met, context_grad))
+    came = [swap(met[m], ("seq", m)) for m in range(1, ways)] + [swap(met[ways + 1], ("ring", near_bit))]
+
+    grads = []
+    for pair in range(2):
+        ready = grads + [met[0]]
+        grads.append(attend_backward(slopes[2 * pair : 2 * pair + 2], qkv, context_grad, *kept[pair], pair, ready))
+    came = after(came, grads[1])
+    down_sum = met[0].astype(jnp.float32)
+    for part in came[: ways - 1]:
+        down_sum = down_sum + part.astype(jnp.float32)
+    down_sum = down_sum.astype(jnp.bfloat16)
+    up_sum = (met[ways].astype(jnp.float32) + came[ways - 1].astype(jnp.float32)).astype(jnp.bfloat16)
+    up_sum = up_sum.reshape((ways, 2) + up_sum.shape[1:])
+
+    part, grad_columns, first_sums, bias_sums = input_grad(
+        grads[0], grads[1], weight_input, normed, unit, (down_sum, up_sum)
+    )
+    down_sum = collect_next(down_sum, "ring")
+    up_sum = collect_next(up_sum, "seq")
+    grad_up_weight = up_sum[0] + swap(up_sum[1].astype(jnp.bfloat16), ("ring", far_bit)).astype(jnp.float32)
+    grad_down_weight, grad_output_weight = down_sum[:owned_down], down_sum[owned_down:]
+    grad_normed = jnp.sum(exchange(part).astype(jnp.float32), axis=0)
+    inputs = rows_in.astype(jnp.float32)
+    tokens_grad = grad_residual + norm_back(grad_normed, gain_first, *norm_parts(inputs))
+
+    sums = (
+        first_sums[0],
+        first_sums[1],
+        unpair_columns(bias_sums[0], seq_index, ways),
+        middle_sums[2],
+        middle_sums[0],
+        middle_sums[1],
+        grad_up_bias[0],
+        middle_sums[3],
+    )
+    rows = [jnp.pad(term.reshape(world, -1), ((0, 0), (0, 128 - size))) for term, size in zip(sums, sizes)]
+    rows = jnp.stack(rows, axis=1).astype(jnp.bfloat16)
+    rows = jnp.pad(rows, ((0, 0), (0, 8 - len(sizes)), (0, triple - 128)))
+    both = jnp.concatenate((grad_columns.reshape(world, owned, triple), rows), axis=1)
+    both = both.reshape(ways, rings, CORES, owned + 8, triple)
+    came = other_core(lax.dynamic_index_in_dim(both, 1 - core, 2, keepdims=False))
+    both = add_low(lax.dynamic_index_in_dim(both, core, 2, keepdims=False), came)
+    ring = lax.axis_index("ring")
+    both = collect([lax.dynamic_index_in_dim(both, ring ^ m, 1, keepdims=False) for m in range(rings)], "ring")
+    both = spread(both.astype(jnp.bfloat16), "seq")
+    grad_input_weight = ungroup_columns(both[:, :owned]).astype(jnp.float32)
+    rows = jnp.sum(both[:, owned:, :128].astype(jnp.float32), axis=0)
+    small = [rows[i, :size] for i, size in enumerate(sizes)]
+    return (
+        layer_out.reshape(tokens_in.shape),
+        tokens_grad.reshape(tokens_in.shape),
+        small[0],
+        small[1],
+        grad_input_weight,
+        small[2],
+        grad_output_weight,
+        small[3],
+        small[4],
+        small[5],
+        grad_up_weight,
+        small[6],
+        grad_down_weight,
+        small[7],
+    )
+
+
 def solution(mesh):
     ways, copies = mesh.shape["seq"], mesh.shape["dp"]
     split = Mesh(mesh.devices.reshape(ways, copies // CORES, CORES), WORLD)
@@ -435,8 +1141,9 @@
     vector = P(WORLD)
     matrix = P(WORLD, None)
     weights = (vector, vector, matrix, vector, matrix, vector, vector, vector, matrix, vector, matrix, vector)
+    step = blocked_body if ways == 4 else plain_body
     return jax.shard_map(
-        body,
+        step,
         mesh=split,
         in_specs=(token, token) + weights,
         out_specs=(token, token) + weights,

time: 796 us -> 443 us (0.56)
  waiting for transfers between devices: 377 us -> 137 us
  Pallas kernels: 64.6 us -> 170 us
  matrix products: 97.4 us -> 0.2 us
  blocking collectives: 92 us -> 0 us
  starting transfers between devices: 18.3 us -> 59.1 us
  local copies, waits for them, and re-layouts: 65.7 us -> 28.8 us
  other arithmetic: 56.6 us -> 28.1 us
    all_gather x5 -> x1, waiting for transfers between devices: 227 us -> 0.01 us  [blocked_body(): all_rows = lax.all_gather(rows_in, 'seq', tiled=True)]
    ppermute x6 -> x44, waiting for transfers between devices: 7.16 us -> 112 us  [swap(): lax.ppermute(value, axis, [(i, i ^ bit) for i in range(lax.axis_size(axis...]
    pallas_call x2 -> x15, Pallas kernels: 64.6 us -> 170 us  [the longest x2 46.1 us: attend_backward(): pl.pallas_call(backward_kernel, grid=(2,), in_specs=[pl.BlockSpec(memory_...]
    dot_general x15 -> x1, matrix products: 97.4 us -> 0.2 us  [blocked_body(): found = jnp.dot(pick, found, preferred_element_type=jnp.float32)]
    reduce_scatter x4 -> x0, waiting for transfers between devices: 66.3 us -> none  [the longest x3 66.3 us: scatter_weight_grad(): lax.psum_scatter(both, CHIPS, scatter_dimension=0, tiled=True)]
    all_to_all x4 -> x3, waiting for transfers between devices: 73.9 us -> 25.2 us  [exchange(): lax.all_to_all(value.reshape(ways, local, -1), 'seq', split_axis=0, conca...]
    ppermute x6 -> x44, starting transfers between devices: 0.97 us -> 46.5 us  [swap(): lax.ppermute(value, axis, [(i, i ^ bit) for i in range(lax.axis_size(axis...]
    unnamed x1 -> x0, blocking collectives: 41.3 us -> none
  transfers between devices with their start and end apart: 19 -> 48, of which waited for: 8 -> 21; matrix products, arithmetic and copies ran while one was open for 20% -> 9% of each run, Pallas kernels for 8% -> 28%
where the time goes in v2:
time: 443 us; the launch traced here: 438 us
  Pallas kernels  170 us (38%)
  waiting for transfers between devices  137 us (31%)
  starting transfers between devices  59.1 us (13%)
  local copies, waits for them, and re-layouts  28.8 us (7%)
  other arithmetic  28.1 us (6%)
  between operations  15.1 us (3%)
    ppermute x44, waiting for transfers between devices, swap(): lax.ppermute(value, axis, [(i, i ^ bit) for i in range(lax.axis_size(axis...  112 us
    ppermute x44, starting transfers between devices, swap(): lax.ppermute(value, axis, [(i, i ^ bit) for i in range(lax.axis_size(axis...  46.5 us
    pallas_call x2, Pallas kernels, attend_backward(): pl.pallas_call(backward_kernel, grid=(2,), in_specs=[pl.BlockSpec(memory_...  46.1 us
    pallas_call x1, Pallas kernels, feed_forward(): pl.pallas_call(functools.partial(feed_forward_kernel, groups), grid_spec=...  45.7 us
    all_to_all x3, waiting for transfers between devices, exchange(): lax.all_to_all(value.reshape(ways, local, -1), 'seq', split_axis=0, conca...  25.2 us
    pallas_call x2, Pallas kernels, attend_forward(): pl.pallas_call(forward_kernel, grid=(2,), in_specs=[pl.BlockSpec(memory_s...  23.6 us
    pallas_call x1, Pallas kernels, meet(): pl.pallas_call(functools.partial(meet_kernel, groups, up_groups), grid=(c...  15.4 us
    pallas_call x1, Pallas kernels, input_grad(): pl.pallas_call(input_grad_kernel, grid=(length // rows,), in_specs=[block...  12.7 us
  transfers between devices with their start and end apart: 48, of which 21 were waited for; matrix products, arithmetic and copies ran while one was open for 9% of the time, Pallas kernels for 28%

profile of v2, /device:TPU:0, one launch (start us, length us, event | category | flops | bytes accessed | tf_op | source)
XLA Modules:
  0.0 438.4 jit_solution(8365359789629546954)
XLA Ops:
  9.2 3.0 collective-permute-start.6
  12.2 2.6 collective-permute-start.7
  17.7 1.8 collective-permute-start
  19.5 1.7 collective-permute-start.9
  22.4 1.5 collective-permute-start.1
  24.0 2.7 collective-permute-done.1
  26.7 2.2 collective-permute-start.2
  28.9 4.2 collective-permute-done.2
  33.1 1.5 collective-permute-start.3
  34.6 26.7 %collective-permute-done.9 = bf16[32,4096]{1,0:T(8,128)(2,1)S(1)} collective-permute-done((bf16[32,4096]{1,0:T(8,128)(2,1)S(1)}, bf16[32,4096]{1,0:T(8,128)(2,1)S(1)}, u32[]{:S(2)}, u32[]{:S(2)}) %collective-permute-start.9) | collective-permute-done | bytes 262176 | tf_op jit(solution)/shard_map/ppermute | solution.py:328
  61.3 1.6 collective-permute-start.10
  62.9 2.2 collective-permute-done.3
  65.3 1.6 collective-permute-start.11
  66.9 1.4 collective-permute-start.12
  68.3 1.2 pad_maximum_fusion.1.refs_0_
  69.6 7.5 %collective-permute-done.4 = bf16[2,4,40,768]{3,2,1,0:T(8,128)(2,1)S(1)} collective-permute-done((bf16[2,4,40,768]{3,2,1,0:T(8,128)(2,1)S(1)}, bf16[2,4,40,768]{3,2,1,0:T(8,128)(2,1)S(1)}, u32[]{:S(2)}, u32[]{:S(2)}) %collective-permute-start.4) | collective-permute-done | bytes 491552 | tf_op jit(solution)/shard_map/ppermute | solution.py:328
  77.3 5.5 %collective-permute-done.10 = bf16[2,32,4096]{2,1,0:T(8,128)(2,1)S(1)} collective-permute-done((bf16[2,32,4096]{2,1,0:T(8,128)(2,1)S(1)}, bf16[2,32,4096]{2,1,0:T(8,128)(2,1)S(1)}, u32[]{:S(2)}, u32[]{:S(2)}) %collective-permute-start.10) | collective-permute-done | bytes 524320 | tf_op jit(solution)/shard_map/ppermute | solution.py:328
  82.9 10.8 %collective-permute-done.12 = bf16[2,32,4096]{2,1,0:T(8,128)(2,1)S(1)} collective-permute-done((bf16[2,32,4096]{2,1,0:T(8,128)(2,1)S(1)}, bf16[2,32,4096]{2,1,0:T(8,128)(2,1)S(1)}, u32[]{:S(2)}, u32[]{:S(2)}) %collective-permute-start.12) | collective-permute-done | bytes 524320 | tf_op jit(solution)/shard_map/ppermute | solution.py:328
  95.1 1.3 copy-done.4
  96.4 1.6 collective-permute-start.16
  101.4 2.4 collective-permute-start.15
  103.8 10.6 %project.1 = (bf16[2048,768]{1,0:T(8,128)(2,1)}, bf16[2048,1024]{1,0:T(8,128)(2,1)}, bf16[2048,1024]{1,0:T(8,128)(2,1)}, bf16[1024,768]{1,0:T(8,128)(2,1)}) custom-call(s32[2]{0:T(128)} %pad_add_fusion.1.table_ref, bf16[2048,1024]{1,0:T(8,128)(2,1)} %bitcast.157, bf16[8,4,40,768]{3,2,1,0:T(8,128)(2,1)} %bitcast.152, f32[1,1024]{1,0:T(1,128)} %reshape.173.refs_2_, ...), custom_call_target="tpu_custom_call" | custom-call | flops 900000000 | tf_op jit(solution)/shard_map/project/pallas_call | solution.py:461
  114.4 11.8 %attend_forward.2 = (bf16[2048,128]{1,0:T(8,128)(2,1)}, f32[128,2048]{1,0:T(8,128)}, f32[16,2048]{1,0:T(8,128)}) custom-call(f32[2]{0:T(128)} %get-tuple-element.161.slope_ref, bf16[2048,768]{1,0:T(8,128)(2,1)} %get-tuple-element.65.q_ref.k_ref.v_ref, bf16[2048,768]{1,0:T(8,128)(2,1)} %get-tuple-element.65.q_ref.k_ref.v_ref, ...), custom_call_target="tpu_custom_call" | custom-call | flops 1050000000 | tf_op jit(solution)/shard_map/attend_forward/pallas_call | solution.py:82
  126.2 11.8 %attend_forward.3 = (bf16[2048,128]{1,0:T(8,128)(2,1)}, f32[128,2048]{1,0:T(8,128)}, f32[16,2048]{1,0:T(8,128)}) custom-call(f32[2]{0:T(128)} %get-tuple-element.162.slope_ref, bf16[2048,768]{1,0:T(8,128)(2,1)} %get-tuple-element.65.q_ref.k_ref.v_ref, bf16[2048,768]{1,0:T(8,128)(2,1)} %get-tuple-element.65.q_ref.k_ref.v_ref, ...), custom_call_target="tpu_custom_call" | custom-call | flops 1050000000 | tf_op jit(solution)/shard_map/attend_forward/pallas_call | solution.py:82
  138.0 2.1 pad_maximum_fusion.2
  140.1 4.0 all-to-all-start
  144.2 25.2 %all-to-all-done.refs_6_.context_ref = bf16[4,512,256]{2,1,0:T(8,128)(2,1)S(1)} async-done(((bf16[4,512,256]{2,1,0:T(8,128)(2,1)}), bf16[4,512,256]{2,1,0:T(8,128)(2,1)S(1)}, u32[]{:S(2)}, u32[]{:S(2)}) %all-to-all-start) | async-done | bytes 1048608 | tf_op jit(solution)/shard_map/all_to_all | solution.py:1039
  171.8 4.1 collective-permute-done.17.refs_4_
  179.6 4.3 collective-permute-done.19.refs_6_
  183.9 1.9 collective-permute-done.20.refs_7_
  185.8 5.8 %project_output.1 = (f32[512,1024]{1,0:T(8,128)}, bf16[512,1024]{1,0:T(8,128)(2,1)}, bf16[1024,1024]{1,0:T(8,128)(2,1)}) custom-call(s32[33]{0:T(128)} %pad_add_fusion.table_ref, bf16[4,512,256]{2,1,0:T(8,128)(2,1)} %copy-done.6, bf16[512,1024]{1,0:T(8,128)(2,1)} %bitcast.148, f32[1,1024]{1,0:T(1,128)} %reshape.176.bias_ref, f32[1,1024]{1,0:T(1,128)} %reshape.177.gain_ref, ...), custom_call_target="tpu_custom_call" | custom-call | flops 500000000 | tf_op jit(solution)/shard_map/project_output/pallas_call | solution.py:578
  191.6 45.7 %feed_forward.1 = (f32[512,1024]{1,0:T(8,128)}, f32[512,1024]{1,0:T(8,128)}, bf16[16,128,1024]{2,1,0:T(8,128)(2,1)}, bf16[16,128,1024]{2,1,0:T(8,128)(2,1)}, bf1...) custom-call(s32[33]{0:T(128)} %pad_add_fusion.table_ref, ...), custom_call_target="tpu_custom_call" | custom-call | flops 4499999744 | tf_op jit(solution)/shard_map/feed_forward/pallas_call | solution.py:279
  237.9 9.7 %residual_grad.1 = (f32[512,1024]{1,0:T(8,128)}, bf16[4,512,256]{2,1,0:T(8,128)(2,1)}, bf16[16,32,1024]{2,1,0:T(8,128)(2,1)}, bf16[16,32,1024]{2,1,0:T(8,128)(2,1)}, f32[8,1024]{1,0:T(8,128)}) custom-call(s32[33]{0:T(128)} %pad_add_fusion.table_ref, f32[512,1024]{1,0:T(8,128)} %get-tuple-element.78.grad_ref, f32[512,1024]{1,0:T(8,128)} %get-tuple-element.73.residual_ref, ...), custom_call_target="tpu_custom_call" | custom-call | flops 700000000 | tf_op jit(solution)/shard_map/residual_grad/pallas_call | solution.py:642
  247.8 3.7 all-to-all-start.1
  253.2 15.4 %meet.1 = (bf16[4,160,1024]{2,1,0:T(8,128)(2,1)}, bf16[4,160,1024]{2,1,0:T(8,128)(2,1)}, bf16[4,160,1024]{2,1,0:T(8,128)(2,1)}, bf16[4,160,1024]{2,1,0:T(8,128)(...) custom-call(bf16[16,128,1024]{2,1,0:T(8,128)(2,1)} %get-tuple-element.83.down_keep, ...), custom_call_target="tpu_custom_call" | custom-call | flops 900000000 | tf_op jit(solution)/shard_map/meet/pallas_call | solution.py:694
  271.1 1.5 collective-permute-start.26
  272.6 1.3 collective-permute-start.27
  278.6 3.1 fusion.11
  281.7 22.9 %attend_backward.2.refs_0_.low_ref = bf16[2048,384]{1,0:T(8,128)(2,1)} custom-call(f32[2]{0:T(128)} %get-tuple-element.161.slope_ref, bf16[2048,768]{1,0:T(8,128)(2,1)} %get-tuple-element.65.q_ref.k_ref.v_ref, bf16[2048,768]{1,0:T(8,128)(2,1)} %get-tuple-element.65.q_ref.k_ref.v_ref, bf16[2048,768]{1,0:T(8,128)(2,1)} %get-tuple-element.65.q_ref.k_ref.v_ref, ...), custom_call_target="tpu_custom_call" | custom-call | flops 2200000000 | tf_op jit(solution)/shard_map/attend_backward/pallas_call | solution.py:170
  304.7 23.2 %attend_backward.3.refs_4_.high_ref = bf16[2048,384]{1,0:T(8,128)(2,1)} custom-call(f32[2]{0:T(128)} %get-tuple-element.162.slope_ref, bf16[2048,768]{1,0:T(8,128)(2,1)} %get-tuple-element.65.q_ref.k_ref.v_ref, bf16[2048,768]{1,0:T(8,128)(2,1)} %get-tuple-element.65.q_ref.k_ref.v_ref, bf16[2048,768]{1,0:T(8,128)(2,1)} %get-tuple-element.65.q_ref.k_ref.v_ref, ...), custom_call_target="tpu_custom_call" | custom-call | flops 2200000000 | tf_op jit(solution)/shard_map/attend_backward/pallas_call | solution.py:170
  327.8 3.7 collective-permute-done.27.refs_1_
  331.5 2.4 add_convert_fusion
  333.9 1.2 fusion.35
  336.9 3.3 add_convert_fusion.1.refs_0_
  342.1 2.4 collective-permute-start.38
  344.5 1.4 collective-permute-start.39
  345.9 12.7 %input_grad.1 = (bf16[2048,1024]{1,0:T(8,128)(2,1)}, bf16[1024,768]{1,0:T(8,128)(2,1)}, f32[8,1024]{1,0:T(8,128)}, f32[8,768]{1,0:T(8,128)}) custom-call(bf16[2048,384]{1,0:T(8,128)(2,1)} %attend_backward.2.refs_0_.low_ref, bf16[2048,384]{1,0:T(8,128)(2,1)} %attend_backward.3.refs_4_.high_ref, bf16[1024,768]{1,0:T(8,128)(2,1)} %get-tuple-element.98.w_ref, ...), custom_call_target="tpu_custom_call" | custom-call | flops 1000000000 | tf_op jit(solution)/shard_map/input_grad/pallas_call | solution.py:518
  360.6 1.7 collective-permute-start.42
  362.4 1.5 fusion.13
  364.0 4.9 %all-to-all-start.2 = ((bf16[4,512,1024]{2,1,0:T(8,128)(2,1)}), bf16[4,512,1024]{2,1,0:T(8,128)(2,1)}, u32[]{:S(2)}, u32[]{:S(2)}) async-start(bf16[4,512,1024]{2,1,0:T(8,128)(2,1)} %bitcast.158), calls=%async_computation.2 | async-start | bytes 8388608 | tf_op jit(solution)/shard_map/all_to_all | solution.py:1039
  369.0 1.5 fusion.15
  372.0 4.8 %collective-permute-done.42 = bf16[2,32,4096]{2,1,0:T(8,128)(2,1)} collective-permute-done((bf16[2,32,4096]{2,1,0:T(8,128)(2,1)}, bf16[2,32,4096]{2,1,0:T(8,128)(2,1)}, u32[]{:S(2)}, u32[]{:S(2)}) %collective-permute-start.42) | collective-permute-done | bytes 524320 | tf_op jit(solution)/shard_map/ppermute | solution.py:328
  376.8 1.6 convert_add_fusion.1
  378.9 3.0 collective-permute-start.32
  381.8 1.4 collective-permute-start.33
  383.9 1.6 collective-permute-done.31
  385.5 18.5 %collective-permute-done.32 = bf16[4,40,768]{2,1,0:T(8,128)(2,1)S(1)} collective-permute-done((bf16[4,40,768]{2,1,0:T(8,128)(2,1)S(1)}, bf16[4,40,768]{2,1,0:T(8,128)(2,1)S(1)}, u32[]{:S(2)}, u32[]{:S(2)}) %collective-permute-start.32) | collective-permute-done | bytes 245792 | tf_op jit(solution)/shard_map/ppermute | solution.py:328
  405.2 6.3 %collective-permute-done.43 = bf16[32,4096]{1,0:T(8,128)(2,1)S(1)} collective-permute-done((bf16[32,4096]{1,0:T(8,128)(2,1)S(1)}, bf16[32,4096]{1,0:T(8,128)(2,1)S(1)}, u32[]{:S(2)}, u32[]{:S(2)}) %collective-permute-start.43) | collective-permute-done | bytes 262176 | tf_op jit(solution)/shard_map/ppermute | solution.py:328
  412.3 1.2 collective-permute-start.35
  413.5 1.2 collective-permute-start.36
  414.7 5.5 %collective-permute-done.34 = bf16[1,40,768]{2,1,0:T(8,128)(2,1)S(1)} collective-permute-done((bf16[1,40,768]{2,1,0:T(8,128)(2,1)S(1)}, bf16[1,40,768]{2,1,0:T(8,128)(2,1)S(1)}, u32[]{:S(2)}, u32[]{:S(2)}) %collective-permute-start.34) | collective-permute-done | bytes 61472 | tf_op jit(solution)/shard_map/ppermute | solution.py:328
  421.6 1.1 reshape.188
  424.2 3.4 convert_reduce_fusion
  429.2 2.0 fusion.8
  (227 shorter events, 42.1 us)
Async XLA Ops:
  7.2 10.3 %copy-start.27 = (bf16[32]{0:T(256)(128)(2,1)S(1)}, bf16[32]{0:T(256)(128)(2,1)}, u32[]{:S(2)}) copy-start(bf16[32]{0:T(256)(128)(2,1)} %param.23) | copy-start | bytes 196
  7.2 10.3 %copy-start.26 = (bf16[32]{0:T(256)(128)(2,1)S(1)}, bf16[32]{0:T(256)(128)(2,1)}, u32[]{:S(2)}) copy-start(bf16[32]{0:T(256)(128)(2,1)} %param.24) | copy-start | bytes 196
  7.2 10.3 %copy-start.29 = (bf16[32]{0:T(256)(128)(2,1)S(1)}, bf16[32]{0:T(256)(128)(2,1)}, u32[]{:S(2)}) copy-start(bf16[32]{0:T(256)(128)(2,1)} %param.19) | copy-start | bytes 196
  7.2 10.3 %copy-start.28 = (bf16[64]{0:T(256)(128)(2,1)S(1)}, bf16[64]{0:T(256)(128)(2,1)}, u32[]{:S(2)}) copy-start(bf16[64]{0:T(256)(128)(2,1)} %param.21) | copy-start | bytes 388
  7.2 10.3 %copy-start.25 = (bf16[128]{0:T(256)(128)(2,1)S(1)}, bf16[128]{0:T(256)(128)(2,1)}, u32[]{:S(2)}) copy-start(bf16[128]{0:T(256)(128)(2,1)} %param.27) | copy-start | bytes 772
  7.2 12.2 %copy-start.15 = (bf16[32,4096]{1,0:T(8,128)(2,1)S(1)}, bf16[32,4096]{1,0:T(8,128)(2,1)}, u32[]{:S(2)}) copy-start(bf16[32,4096]{1,0:T(8,128)(2,1)} %param.26) | copy-start | bytes 786436
  7.2 93.0 %all-gather.3.cloned.1.call-start = ((), (), s32[]{:S(2)}) async-start(), calls=%async_computation.3 | async-start | bytes 5242880 | tf_op jit(solution)/shard_map/all_gather | solution.py:1023
  9.2 56.2 %collective-permute-start.6 = (bf16[160,1024]{1,0:T(8,128)(2,1)S(1)}, bf16[160,1024]{1,0:T(8,128)(2,1)S(1)}, u32[]{:S(2)}, u32[]{:S(2)}) collective-permute-start(bf16[160,1024]{1,0:T(8,128)(2,1)S(1)} %constant_dynamic-update-slice_fusion), channel_id=1, source_target_pairs={{0,2},{2,0},{4,6},{6,4},{1,3},{3,1},{5,7},{7,5},{8,10},{10,8},{12,... | collective-permute-start | bytes 983048 | tf_op jit(solution)/shard_map/ppermute | solution.py:328
  12.2 54.7 %collective-permute-start.7 = (bf16[160,1024]{1,0:T(8,128)(2,1)S(1)}, bf16[160,1024]{1,0:T(8,128)(2,1)S(1)}, u32[]{:S(2)}, u32[]{:S(2)}) collective-permute-start(bf16[160,1024]{1,0:T(8,128)(2,1)S(1)} %constant_dynamic-update-slice_fusion), channel_id=1, source_target_pairs={{0,4},{2,6},{4,0},{6,2},{1,5},{3,7},{5,1},{7,3},{8,12},{10,14},{12... | collective-permute-start | bytes 983048 | tf_op jit(solution)/shard_map/ppermute | solution.py:328
  14.8 53.6 %collective-permute-start.8 = (bf16[160,1024]{1,0:T(8,128)(2,1)S(1)}, bf16[160,1024]{1,0:T(8,128)(2,1)S(1)}, u32[]{:S(2)}, u32[]{:S(2)}) collective-permute-start(bf16[160,1024]{1,0:T(8,128)(2,1)S(1)} %constant_dynamic-update-slice_fusion), channel_id=1, source_target_pairs={{0,6},{2,4},{4,2},{6,0},{1,7},{3,5},{5,3},{7,1},{8,14},{10,12},{12... | collective-permute-start | bytes 983048 | tf_op jit(solution)/shard_map/ppermute | solution.py:328
  17.7 4.8 %collective-permute-start = (bf16[1,40,768]{2,1,0:T(8,128)(2,1)S(1)}, bf16[1,40,768]{2,1,0:T(8,128)(2,1)S(1)}, u32[]{:S(2)}, u32[]{:S(2)}) collective-permute-start(bf16[1,40,768]{2,1,0:T(8,128)(2,1)S(1)} %get-tuple-element.143), channel_id=1, source_target_pairs={{0,8},{8,0},{16,24},{24,16},{1,9},{9,1},{17,25},{25,17},{2,10},{10... | collective-permute-start | bytes 184328 | tf_op jit(solution)/shard_map/ppermute | solution.py:328
  19.5 41.8 %collective-permute-start.9 = (bf16[32,4096]{1,0:T(8,128)(2,1)S(1)}, bf16[32,4096]{1,0:T(8,128)(2,1)S(1)}, u32[]{:S(2)}, u32[]{:S(2)}) collective-permute-start(bf16[32,4096]{1,0:T(8,128)(2,1)S(1)} %copy-done.15), channel_id=1, source_target_pairs={{0,4},{2,6},{4,0},{6,2},{1,5},{3,7},{5,1},{7,3},{8,12},{10,14},{12... | collective-permute-start | bytes 786440 | tf_op jit(solution)/shard_map/ppermute | solution.py:328
  22.4 4.2 collective-permute-start.1
  26.7 6.4 %collective-permute-start.2 = (bf16[1,40,768]{2,1,0:T(8,128)(2,1)S(1)}, bf16[1,40,768]{2,1,0:T(8,128)(2,1)S(1)}, u32[]{:S(2)}, u32[]{:S(2)}) collective-permute-start(bf16[1,40,768]{2,1,0:T(8,128)(2,1)S(1)} %get-tuple-element.141), channel_id=1, source_target_pairs={{0,24},{8,16},{16,8},{24,0},{1,25},{9,17},{17,9},{25,1},{2,26},{10... | collective-permute-start | bytes 184328 | tf_op jit(solution)/shard_map/ppermute | solution.py:328
  33.1 32.0 %collective-permute-start.3 = (bf16[1,4,40,768]{3,2,1,0:T(8,128)(2,1)S(1)}, bf16[1,4,40,768]{3,2,1,0:T(8,128)(2,1)S(1)}, u32[]{:S(2)}, u32[]{:S(2)}) collective-permute-start(bf16[1,4,40,768]{3,2,1,0:T(8,128)(2,1)S(1)} %bitcast.171), channel_id=1, source_target_pairs={{0,4},{2,6},{4,0},{6,2},{1,5},{3,7},{5,1},{7,3},{8,12},{10,14},{12... | collective-permute-start | bytes 737288 | tf_op jit(solution)/shard_map/ppermute | solution.py:328
  61.3 21.5 %collective-permute-start.10 = (bf16[2,32,4096]{2,1,0:T(8,128)(2,1)S(1)}, bf16[2,32,4096]{2,1,0:T(8,128)(2,1)S(1)}, u32[]{:S(2)}, u32[]{:S(2)}) collective-permute-start(bf16[2,32,4096]{2,1,0:T(8,128)(2,1)S(1)} %pad_maximum_fusion.4), channel_id=1, source_target_pairs={{0,8},{8,0},{16,24},{24,16},{1,9},{9,1},{17,25},{25,17},{2,10},{10... | collective-permute-start | bytes 1572872 | tf_op jit(solution)/shard_map/ppermute | solution.py:328
  65.2 11.9 %collective-permute-start.4 = (bf16[2,4,40,768]{3,2,1,0:T(8,128)(2,1)S(1)}, bf16[2,4,40,768]{3,2,1,0:T(8,128)(2,1)S(1)}, u32[]{:S(2)}, u32[]{:S(2)}) collective-permute-start(bf16[2,4,40,768]{3,2,1,0:T(8,128)(2,1)S(1)} %get-tuple-element.136), channel_id=1, source_target_pairs={{0,2},{2,0},{4,6},{6,4},{1,3},{3,1},{5,7},{7,5},{8,10},{10,8},{12,... | collective-permute-start | bytes 1474568 | tf_op jit(solution)/shard_map/ppermute | solution.py:328
  65.3 17.5 %collective-permute-start.11 = (bf16[2,32,4096]{2,1,0:T(8,128)(2,1)S(1)}, bf16[2,32,4096]{2,1,0:T(8,128)(2,1)S(1)}, u32[]{:S(2)}, u32[]{:S(2)}) collective-permute-start(bf16[2,32,4096]{2,1,0:T(8,128)(2,1)S(1)} %pad_maximum_fusion.4), channel_id=1, source_target_pairs={{0,16},{8,24},{16,0},{24,8},{1,17},{9,25},{17,1},{25,9},{2,18},{10... | collective-permute-start | bytes 1572872 | tf_op jit(solution)/shard_map/ppermute | solution.py:328
  66.9 26.8 %collective-permute-start.12 = (bf16[2,32,4096]{2,1,0:T(8,128)(2,1)S(1)}, bf16[2,32,4096]{2,1,0:T(8,128)(2,1)S(1)}, u32[]{:S(2)}, u32[]{:S(2)}) collective-permute-start(bf16[2,32,4096]{2,1,0:T(8,128)(2,1)S(1)} %pad_maximum_fusion.4), channel_id=1, source_target_pairs={{0,24},{8,16},{16,8},{24,0},{1,25},{9,17},{17,9},{25,1},{2,26},{10... | collective-permute-start | bytes 1572872 | tf_op jit(solution)/shard_map/ppermute | solution.py:328
  77.2 16.6 %collective-permute-start.5 = (bf16[4,4,40,768]{3,2,1,0:T(8,128)(2,1)S(1)}, bf16[4,4,40,768]{3,2,1,0:T(8,128)(2,1)S(1)}, u32[]{:S(2)}, u32[]{:S(2)}) collective-permute-start(bf16[4,4,40,768]{3,2,1,0:T(8,128)(2,1)S(1)} %bitcast.161), channel_id=1, source_target_pairs={{0,1},{1,0},{2,3},{3,2},{4,5},{5,4},{6,7},{7,6},{8,9},{9,8},{10,11... | collective-permute-start | bytes 2949128 | tf_op jit(solution)/shard_map/ppermute | solution.py:328
  96.4 47.8 %collective-permute-start.16 = (bf16[8,32,4096]{2,1,0:T(8,128)(2,1)}, bf16[8,32,4096]{2,1,0:T(8,128)(2,1)}, u32[]{:S(2)}, u32[]{:S(2)}) collective-permute-start(bf16[8,32,4096]{2,1,0:T(8,128)(2,1)} %after.6.refs_6_.refs_4_), channel_id=1, source_target_pairs={{0,2},{2,0},{4,6},{6,4},{1,3},{3,1},{5,7},{7,5},{8,10},{10,8},{12,... | collective-permute-start | bytes 6291464 | tf_op jit(solution)/shard_map/ppermute | solution.py:328
  100.3 69.1 %collective-permute-start.13 = (bf16[4,160,1024]{2,1,0:T(8,128)(2,1)}, bf16[4,160,1024]{2,1,0:T(8,128)(2,1)S(1)}, u32[]{:S(2)}, u32[]{:S(2)}) collective-permute-start(bf16[4,160,1024]{2,1,0:T(8,128)(2,1)} %after.5.refs_5_.refs_0_), channel_id=1, source_target_pairs={{0,8},{8,0},{16,24},{24,16},{1,9},{9,1},{17,25},{25,17},{2,10},{10... | collective-permute-start | bytes 3932168 | tf_op jit(solution)/shard_map/ppermute | solution.py:328
  100.8 68.5 %collective-permute-start.14 = (bf16[4,160,1024]{2,1,0:T(8,128)(2,1)}, bf16[4,160,1024]{2,1,0:T(8,128)(2,1)}, u32[]{:S(2)}, u32[]{:S(2)}) collective-permute-start(bf16[4,160,1024]{2,1,0:T(8,128)(2,1)} %after.5.refs_5_.refs_0_), channel_id=1, source_target_pairs={{0,16},{8,24},{16,0},{24,8},{1,17},{9,25},{17,1},{25,9},{2,18},{10... | collective-permute-start | bytes 3932168 | tf_op jit(solution)/shard_map/ppermute | solution.py:328
  101.4 68.0 %collective-permute-start.15 = (bf16[4,160,1024]{2,1,0:T(8,128)(2,1)}, bf16[4,160,1024]{2,1,0:T(8,128)(2,1)}, u32[]{:S(2)}, u32[]{:S(2)}) collective-permute-start(bf16[4,160,1024]{2,1,0:T(8,128)(2,1)} %after.5.refs_5_.refs_0_), channel_id=1, source_target_pairs={{0,24},{8,16},{16,8},{24,0},{1,25},{9,17},{17,9},{25,1},{2,26},{10... | collective-permute-start | bytes 3932168 | tf_op jit(solution)/shard_map/ppermute | solution.py:328
  126.1 11.8 %copy-start.16 = (bf16[2048,128]{1,0:T(8,128)(2,1)S(1)}, bf16[2048,128]{1,0:T(8,128)(2,1)}, u32[]{:S(2)}) copy-start(bf16[2048,128]{1,0:T(8,128)(2,1)} %get-tuple-element.66) | copy-start | bytes 1572868
  140.1 29.3 %all-to-all-start = ((bf16[4,512,256]{2,1,0:T(8,128)(2,1)}), bf16[4,512,256]{2,1,0:T(8,128)(2,1)S(1)}, u32[]{:S(2)}, u32[]{:S(2)}) async-start(bf16[4,512,256]{2,1,0:T(8,128)(2,1)} %bitcast.33), calls=%async_computation | async-start | bytes 2097152 | tf_op jit(solution)/shard_map/all_to_all | solution.py:1039
  144.2 31.9 %copy-start.30 = (s32[16]{0:T(128)S(1)}, s32[16]{0:T(128)}, u32[]{:S(2)}) copy-start(s32[16]{0:T(128)} %constant.101.clone) | copy-start | bytes 196
  170.8 5.1 %collective-permute-start.17 = (bf16[4,160,1024]{2,1,0:T(8,128)(2,1)}, bf16[4,160,1024]{2,1,0:T(8,128)(2,1)S(1)}, u32[]{:S(2)}, u32[]{:S(2)}) collective-permute-start(bf16[4,160,1024]{2,1,0:T(8,128)(2,1)} %get-tuple-element.69.refs_0_), channel_id=1, source_target_pairs={{0,1},{1,0},{2,3},{3,2},{4,5},{5,4},{6,7},{7,6},{8,9},{9,8},{10,11... | collective-permute-start | bytes 3932168 | tf_op jit(solution)/shard_map/ppermute | solution.py:328
  170.8 20.8 %collective-permute-start.21 = (bf16[8,32,4096]{2,1,0:T(8,128)(2,1)}, bf16[8,32,4096]{2,1,0:T(8,128)(2,1)}, u32[]{:S(2)}, u32[]{:S(2)}) collective-permute-start(bf16[8,32,4096]{2,1,0:T(8,128)(2,1)} %get-tuple-element.75.refs_8_), channel_id=1, source_target_pairs={{0,1},{1,0},{2,3},{3,2},{4,5},{5,4},{6,7},{7,6},{8,9},{9,8},{10,11... | collective-permute-start | bytes 6291464 | tf_op jit(solution)/shard_map/ppermute | solution.py:328
  171.3 20.3 %collective-permute-start.22 = (bf16[8,32,4096]{2,1,0:T(8,128)(2,1)}, bf16[8,32,4096]{2,1,0:T(8,128)(2,1)}, u32[]{:S(2)}, u32[]{:S(2)}) collective-permute-start(bf16[8,32,4096]{2,1,0:T(8,128)(2,1)} %get-tuple-element.76.refs_9_), channel_id=1, source_target_pairs={{0,1},{1,0},{2,3},{3,2},{4,5},{5,4},{6,7},{7,6},{8,9},{9,8},{10,11... | collective-permute-start | bytes 6291464 | tf_op jit(solution)/shard_map/ppermute | solution.py:328
  171.3 8.3 %collective-permute-start.18 = (bf16[4,160,1024]{2,1,0:T(8,128)(2,1)}, bf16[4,160,1024]{2,1,0:T(8,128)(2,1)S(1)}, u32[]{:S(2)}, u32[]{:S(2)}) collective-permute-start(bf16[4,160,1024]{2,1,0:T(8,128)(2,1)} %get-tuple-element.70.refs_1_), channel_id=1, source_target_pairs={{0,1},{1,0},{2,3},{3,2},{4,5},{5,4},{6,7},{7,6},{8,9},{9,8},{10,11... | collective-permute-start | bytes 3932168 | tf_op jit(solution)/shard_map/ppermute | solution.py:328
  171.8 12.1 %collective-permute-start.19 = (bf16[4,160,1024]{2,1,0:T(8,128)(2,1)}, bf16[4,160,1024]{2,1,0:T(8,128)(2,1)}, u32[]{:S(2)}, u32[]{:S(2)}) collective-permute-start(bf16[4,160,1024]{2,1,0:T(8,128)(2,1)} %get-tuple-element.71.refs_2_), channel_id=1, source_target_pairs={{0,1},{1,0},{2,3},{3,2},{4,5},{5,4},{6,7},{7,6},{8,9},{9,8},{10,11... | collective-permute-start | bytes 3932168 | tf_op jit(solution)/shard_map/ppermute | solution.py:328
  175.9 9.9 %copy-start.11 = (bf16[4,160,1024]{2,1,0:T(8,128)(2,1)}, bf16[4,160,1024]{2,1,0:T(8,128)(2,1)S(1)}, u32[]{:S(2)}) copy-start(bf16[4,160,1024]{2,1,0:T(8,128)(2,1)S(1)} %collective-permute-done.17.refs_4_) | copy-start | bytes 3932164
  175.9 9.9 %collective-permute-start.20 = (bf16[4,160,1024]{2,1,0:T(8,128)(2,1)}, bf16[4,160,1024]{2,1,0:T(8,128)(2,1)}, u32[]{:S(2)}, u32[]{:S(2)}) collective-permute-start(bf16[4,160,1024]{2,1,0:T(8,128)(2,1)} %get-tuple-element.72.refs_3_), channel_id=1, source_target_pairs={{0,1},{1,0},{2,3},{3,2},{4,5},{5,4},{6,7},{7,6},{8,9},{9,8},{10,11... | collective-permute-start | bytes 3932168 | tf_op jit(solution)/shard_map/ppermute | solution.py:328
  237.3 14.9 %collective-permute-start.23 = (bf16[16,128,1024]{2,1,0:T(8,128)(2,1)}, bf16[16,128,1024]{2,1,0:T(8,128)(2,1)}, u32[]{:S(2)}, u32[]{:S(2)}) collective-permute-start(bf16[16,128,1024]{2,1,0:T(8,128)(2,1)} %get-tuple-element.84), channel_id=1, source_target_pairs={{0,1},{1,0},{2,3},{3,2},{4,5},{5,4},{6,7},{7,6},{8,9},{9,8},{10,11... | collective-permute-start | bytes 12582920 | tf_op jit(solution)/shard_map/ppermute | solution.py:328
  237.5 14.8 %collective-permute-start.25 = (bf16[16,32,4096]{2,1,0:T(8,128)(2,1)}, bf16[16,32,4096]{2,1,0:T(8,128)(2,1)}, u32[]{:S(2)}, u32[]{:S(2)}) collective-permute-start(bf16[16,32,4096]{2,1,0:T(8,128)(2,1)} %get-tuple-element.88), channel_id=1, source_target_pairs={{0,1},{1,0},{2,3},{3,2},{4,5},{5,4},{6,7},{7,6},{8,9},{9,8},{10,11... | collective-permute-start | bytes 12582920 | tf_op jit(solution)/shard_map/ppermute | solution.py:328
  247.6 4.7 %collective-permute-start.24 = (bf16[16,32,1024]{2,1,0:T(8,128)(2,1)}, bf16[16,32,1024]{2,1,0:T(8,128)(2,1)S(1)}, u32[]{:S(2)}, u32[]{:S(2)}) collective-permute-start(bf16[16,32,1024]{2,1,0:T(8,128)(2,1)} %get-tuple-element.86), channel_id=1, source_target_pairs={{0,1},{1,0},{2,3},{3,2},{4,5},{5,4},{6,7},{7,6},{8,9},{9,8},{10,11... | collective-permute-start | bytes 3145736 | tf_op jit(solution)/shard_map/ppermute | solution.py:328
  247.8 20.9 %all-to-all-start.1 = ((bf16[4,512,256]{2,1,0:T(8,128)(2,1)}), bf16[4,512,256]{2,1,0:T(8,128)(2,1)S(1)}, u32[]{:S(2)}, u32[]{:S(2)}) async-start(bf16[4,512,256]{2,1,0:T(8,128)(2,1)} %get-tuple-element.81), calls=%async_computation.1 | async-start | bytes 2097152 | tf_op jit(solution)/shard_map/all_to_all | solution.py:1039
  269.7 8.9 %copy-start.24 = (f32[1,4096]{1,0:T(1,128)S(1)}, f32[1,4096]{1,0:T(1,128)}, u32[]{:S(2)}) copy-start(f32[1,4096]{1,0:T(1,128)} %get-tuple-element.115) | copy-start | bytes 49156
  269.7 9.0 %copy-start.10 = (f32[512,1024]{1,0:T(8,128)S(1)}, f32[512,1024]{1,0:T(8,128)}, u32[]{:S(2)}) copy-start(f32[512,1024]{1,0:T(8,128)} %get-tuple-element.73.residual_ref) | copy-start | bytes 6291460
  269.7 61.8 %collective-permute-start.29 = (bf16[8,32,4096]{2,1,0:T(8,128)(2,1)}, bf16[8,32,4096]{2,1,0:T(8,128)(2,1)}, u32[]{:S(2)}, u32[]{:S(2)}) collective-permute-start(bf16[8,32,4096]{2,1,0:T(8,128)(2,1)} %get-tuple-element.104), channel_id=1, source_target_pairs={{0,2},{2,0},{4,6},{6,4},{1,3},{3,1},{5,7},{7,5},{8,10},{10,8},{12,... | collective-permute-start | bytes 6291464 | tf_op jit(solution)/shard_map/ppermute | solution.py:328
  271.1 56.7 %collective-permute-start.26 = (bf16[4,160,1024]{2,1,0:T(8,128)(2,1)}, bf16[4,160,1024]{2,1,0:T(8,128)(2,1)}, u32[]{:S(2)}, u32[]{:S(2)}) collective-permute-start(bf16[4,160,1024]{2,1,0:T(8,128)(2,1)} %get-tuple-element.101), channel_id=1, source_target_pairs={{0,8},{8,0},{16,24},{24,16},{1,9},{9,1},{17,25},{25,17},{2,10},{10... | collective-permute-start | bytes 3932168 | tf_op jit(solution)/shard_map/ppermute | solution.py:328
  272.6 58.9 %collective-permute-start.27 = (bf16[4,160,1024]{2,1,0:T(8,128)(2,1)}, bf16[4,160,1024]{2,1,0:T(8,128)(2,1)}, u32[]{:S(2)}, u32[]{:S(2)}) collective-permute-start(bf16[4,160,1024]{2,1,0:T(8,128)(2,1)} %get-tuple-element.102), channel_id=1, source_target_pairs={{0,16},{8,24},{16,0},{24,8},{1,17},{9,25},{17,1},{25,9},{2,18},{10... | collective-permute-start | bytes 3932168 | tf_op jit(solution)/shard_map/ppermute | solution.py:328
  273.8 57.7 %collective-permute-start.28 = (bf16[4,160,1024]{2,1,0:T(8,128)(2,1)}, bf16[4,160,1024]{2,1,0:T(8,128)(2,1)}, u32[]{:S(2)}, u32[]{:S(2)}) collective-permute-start(bf16[4,160,1024]{2,1,0:T(8,128)(2,1)} %get-tuple-element.103), channel_id=1, source_target_pairs={{0,24},{8,16},{16,8},{24,0},{1,25},{9,17},{17,9},{25,1},{2,26},{10... | collective-permute-start | bytes 3932168 | tf_op jit(solution)/shard_map/ppermute | solution.py:328
  333.9 6.3 %copy-start.3 = (bf16[8,32,4096]{2,1,0:T(8,128)(2,1)}, bf16[8,32,4096]{2,1,0:T(8,128)(2,1)S(1)}, u32[]{:S(2)}) copy-start(bf16[8,32,4096]{2,1,0:T(8,128)(2,1)S(1)} %add_convert_fusion) | copy-start | bytes 6291460
  335.1 36.9 %collective-permute-start.40 = (bf16[2,32,4096]{2,1,0:T(8,128)(2,1)}, bf16[2,32,4096]{2,1,0:T(8,128)(2,1)S(1)}, u32[]{:S(2)}, u32[]{:S(2)}) collective-permute-start(bf16[2,32,4096]{2,1,0:T(8,128)(2,1)} %get-tuple-element.124), channel_id=1, source_target_pairs={{0,8},{8,0},{16,24},{24,16},{1,9},{9,1},{17,25},{25,17},{2,10},{10... | collective-permute-start | bytes 1572872 | tf_op jit(solution)/shard_map/ppermute | solution.py:328
  336.1 36.0 %collective-permute-start.41 = (bf16[2,32,4096]{2,1,0:T(8,128)(2,1)}, bf16[2,32,4096]{2,1,0:T(8,128)(2,1)}, u32[]{:S(2)}, u32[]{:S(2)}) collective-permute-start(bf16[2,32,4096]{2,1,0:T(8,128)(2,1)} %get-tuple-element.126), channel_id=1, source_target_pairs={{0,16},{8,24},{16,0},{24,8},{1,17},{9,25},{17,1},{25,9},{2,18},{10... | collective-permute-start | bytes 1572872 | tf_op jit(solution)/shard_map/ppermute | solution.py:328
  341.5 19.0 %collective-permute-start.37 = (bf16[160,1024]{1,0:T(8,128)(2,1)S(1)}, bf16[160,1024]{1,0:T(8,128)(2,1)S(1)}, u32[]{:S(2)}, u32[]{:S(2)}) collective-permute-start(bf16[160,1024]{1,0:T(8,128)(2,1)S(1)} %get-tuple-element.129), channel_id=1, source_target_pairs={{0,2},{2,0},{4,6},{6,4},{1,3},{3,1},{5,7},{7,5},{8,10},{10,8},{12,... | collective-permute-start | bytes 983048 | tf_op jit(solution)/shard_map/ppermute | solution.py:328
  342.1 26.8 %collective-permute-start.38 = (bf16[160,1024]{1,0:T(8,128)(2,1)}, bf16[160,1024]{1,0:T(8,128)(2,1)}, u32[]{:S(2)}, u32[]{:S(2)}) collective-permute-start(bf16[160,1024]{1,0:T(8,128)(2,1)} %get-tuple-element.131), channel_id=1, source_target_pairs={{0,4},{2,6},{4,0},{6,2},{1,5},{3,7},{5,1},{7,3},{8,12},{10,14},{12... | collective-permute-start | bytes 983048 | tf_op jit(solution)/shard_map/ppermute | solution.py:328
  344.5 24.5 %collective-permute-start.39 = (bf16[160,1024]{1,0:T(8,128)(2,1)}, bf16[160,1024]{1,0:T(8,128)(2,1)}, u32[]{:S(2)}, u32[]{:S(2)}) collective-permute-start(bf16[160,1024]{1,0:T(8,128)(2,1)} %get-tuple-element.130), channel_id=1, source_target_pairs={{0,6},{2,4},{4,2},{6,0},{1,7},{3,5},{5,3},{7,1},{8,14},{10,12},{12... | collective-permute-start | bytes 983048 | tf_op jit(solution)/shard_map/ppermute | solution.py:328
  345.9 14.6 %copy-start.22 = (bf16[32,32]{1,0:T(8,128)(2,1)S(1)}, bf16[32,32]{1,0:T(8,128)(2,1)}, u32[]{:S(2)}) copy-start(bf16[32,32]{1,0:T(8,128)(2,1)} %reshape_squeeze.31) | copy-start | bytes 6148
  345.9 14.6 %copy-start.21 = (bf16[32,32]{1,0:T(8,128)(2,1)S(1)}, bf16[32,32]{1,0:T(8,128)(2,1)}, u32[]{:S(2)}) copy-start(bf16[32,32]{1,0:T(8,128)(2,1)} %reshape_squeeze.32) | copy-start | bytes 6148
  345.9 14.6 %copy-start.20 = (bf16[32,32]{1,0:T(8,128)(2,1)S(1)}, bf16[32,32]{1,0:T(8,128)(2,1)}, u32[]{:S(2)}) copy-start(bf16[32,32]{1,0:T(8,128)(2,1)} %reshape_squeeze.33) | copy-start | bytes 6148
  345.9 16.4 %copy-start.19 = (bf16[32,32]{1,0:T(8,128)(2,1)S(1)}, bf16[32,32]{1,0:T(8,128)(2,1)}, u32[]{:S(2)}) copy-start(bf16[32,32]{1,0:T(8,128)(2,1)} %reshape_squeeze.34) | copy-start | bytes 6148
  360.6 16.2 %collective-permute-start.42 = (bf16[2,32,4096]{2,1,0:T(8,128)(2,1)}, bf16[2,32,4096]{2,1,0:T(8,128)(2,1)}, u32[]{:S(2)}, u32[]{:S(2)}) collective-permute-start(bf16[2,32,4096]{2,1,0:T(8,128)(2,1)} %get-tuple-element.125), channel_id=1, source_target_pairs={{0,24},{8,16},{16,8},{24,0},{1,25},{9,17},{17,9},{25,1},{2,26},{10... | collective-permute-start | bytes 1572872 | tf_op jit(solution)/shard_map/ppermute | solution.py:328
  364.0 60.2 %all-to-all-start.2 = ((bf16[4,512,1024]{2,1,0:T(8,128)(2,1)}), bf16[4,512,1024]{2,1,0:T(8,128)(2,1)}, u32[]{:S(2)}, u32[]{:S(2)}) async-start(bf16[4,512,1024]{2,1,0:T(8,128)(2,1)} %bitcast.158), calls=%async_computation.2 | async-start | bytes 8388608 | tf_op jit(solution)/shard_map/all_to_all | solution.py:1039
  368.9 9.5 %collective-permute-start.30 = (bf16[4,4,40,768]{3,2,0,1:T(8,128)(2,1)S(1)}, bf16[4,4,40,768]{3,2,0,1:T(8,128)(2,1)S(1)}, u32[]{:S(2)}, u32[]{:S(2)}) collective-permute-start(bf16[4,4,40,768]{3,2,0,1:T(8,128)(2,1)S(1)} %bitcast.170), channel_id=1, source_target_pairs={{0,1},{1,0},{2,3},{3,2},{4,5},{5,4},{6,7},{7,6},{8,9},{9,8},{10,11... | collective-permute-start | bytes 2949128 | tf_op jit(solution)/shard_map/ppermute | solution.py:328
  378.8 6.7 %collective-permute-start.31 = (bf16[4,40,768]{2,1,0:T(8,128)(2,1)S(1)}, bf16[4,40,768]{2,1,0:T(8,128)(2,1)S(1)}, u32[]{:S(2)}, u32[]{:S(2)}) collective-permute-start(bf16[4,40,768]{2,1,0:T(8,128)(2,1)S(1)} %get-tuple-element.132), channel_id=1, source_target_pairs={{0,2},{2,0},{4,6},{6,4},{1,3},{3,1},{5,7},{7,5},{8,10},{10,8},{12,... | collective-permute-start | bytes 737288 | tf_op jit(solution)/shard_map/ppermute | solution.py:328
  378.9 25.1 %collective-permute-start.32 = (bf16[4,40,768]{2,1,0:T(8,128)(2,1)S(1)}, bf16[4,40,768]{2,1,0:T(8,128)(2,1)S(1)}, u32[]{:S(2)}, u32[]{:S(2)}) collective-permute-start(bf16[4,40,768]{2,1,0:T(8,128)(2,1)S(1)} %get-tuple-element.134), channel_id=1, source_target_pairs={{0,4},{2,6},{4,0},{6,2},{1,5},{3,7},{5,1},{7,3},{8,12},{10,14},{12... | collective-permute-start | bytes 737288 | tf_op jit(solution)/shard_map/ppermute | solution.py:328
  381.8 22.2 %collective-permute-start.33 = (bf16[4,40,768]{2,1,0:T(8,128)(2,1)S(1)}, bf16[4,40,768]{2,1,0:T(8,128)(2,1)S(1)}, u32[]{:S(2)}, u32[]{:S(2)}) collective-permute-start(bf16[4,40,768]{2,1,0:T(8,128)(2,1)S(1)} %get-tuple-element.133), channel_id=1, source_target_pairs={{0,6},{2,4},{4,2},{6,0},{1,7},{3,5},{5,3},{7,1},{8,14},{10,12},{12... | collective-permute-start | bytes 737288 | tf_op jit(solution)/shard_map/ppermute | solution.py:328
  383.3 28.1 %collective-permute-start.43 = (bf16[32,4096]{1,0:T(8,128)(2,1)S(1)}, bf16[32,4096]{1,0:T(8,128)(2,1)S(1)}, u32[]{:S(2)}, u32[]{:S(2)}) collective-permute-start(bf16[32,4096]{1,0:T(8,128)(2,1)S(1)} %fusion.22), channel_id=1, source_target_pairs={{0,4},{2,6},{4,0},{6,2},{1,5},{3,7},{5,1},{7,3},{8,12},{10,14},{12... | collective-permute-start | bytes 786440 | tf_op jit(solution)/shard_map/ppermute | solution.py:328
  404.2 16.0 %collective-permute-start.34 = (bf16[1,40,768]{2,1,0:T(8,128)(2,1)S(1)}, bf16[1,40,768]{2,1,0:T(8,128)(2,1)S(1)}, u32[]{:S(2)}, u32[]{:S(2)}) collective-permute-start(bf16[1,40,768]{2,1,0:T(8,128)(2,1)S(1)} %get-tuple-element.139), channel_id=1, source_target_pairs={{0,8},{8,0},{16,24},{24,16},{1,9},{9,1},{17,25},{25,17},{2,10},{10... | collective-permute-start | bytes 184328 | tf_op jit(solution)/shard_map/ppermute | solution.py:328
  412.3 8.1 %collective-permute-start.35 = (bf16[1,40,768]{2,1,0:T(8,128)(2,1)S(1)}, bf16[1,40,768]{2,1,0:T(8,128)(2,1)S(1)}, u32[]{:S(2)}, u32[]{:S(2)}) collective-permute-start(bf16[1,40,768]{2,1,0:T(8,128)(2,1)S(1)} %get-tuple-element.138), channel_id=1, source_target_pairs={{0,16},{8,24},{16,0},{24,8},{1,17},{9,25},{17,1},{25,9},{2,18},{10... | collective-permute-start | bytes 184328 | tf_op jit(solution)/shard_map/ppermute | solution.py:328
  413.5 7.6 %collective-permute-start.36 = (bf16[1,40,768]{2,1,0:T(8,128)(2,1)S(1)}, bf16[1,40,768]{2,1,0:T(8,128)(2,1)S(1)}, u32[]{:S(2)}, u32[]{:S(2)}) collective-permute-start(bf16[1,40,768]{2,1,0:T(8,128)(2,1)S(1)} %get-tuple-element.137), channel_id=1, source_target_pairs={{0,24},{8,16},{16,8},{24,0},{1,25},{9,17},{17,9},{25,1},{2,26},{10... | collective-permute-start | bytes 184328 | tf_op jit(solution)/shard_map/ppermute | solution.py:328
  (15 other events, 35.4 us)
Sparse Core Ops, SparseCore 0:
  14.9 63.7 all-gather.2

commit v3 on v2

--- a/solution.py
+++ b/solution.py
@@ -196,7 +196,7 @@
 CONTRACT_LAST = (((1,), (1,)), ((), ()))
 
 
-def feed_forward_kernel(groups, table_ref, x_ref, g_ref, bias_ref, *refs):
+def feed_forward_kernel(groups, per, table_ref, x_ref, g_ref, bias_ref, *refs):
     outs, scratch = refs[-11:-4], refs[-4:]
     chips = table_ref.shape[0] // 2
     down_refs, up_refs = refs[: 2 * groups], refs[2 * groups : -11]
@@ -205,7 +205,7 @@
     x_turn, up_tile, down_tile, grad_tile = scratch
     step = pl.program_id(0)
     core = table_ref[2 * chips]
-    size = chips // groups
+    steps = chips // (groups * per)
     owned = up_refs[0].shape[1]
     span = down_refs[0].shape[1]
 
@@ -224,15 +224,17 @@
         up_tile[up_rows(place, core), :] = up_refs[group][at]
         up_tile[up_rows(place, 1 - core), :] = up_refs[up_groups + group][at]
 
-    def down_rows(who):
-        return pl.ds(pl.multiple_of(who * span, span), span)
+    def down_rows(at, who):
+        chip = lax.rem(table_ref[step * per + at], per)
+        return pl.ds(pl.multiple_of((chip * CORES + who) * span, span), span)
 
     for group in range(groups):
 
-        @pl.when(step // size == group)
+        @pl.when(step // steps == group)
         def _():
-            down_tile[down_rows(core), :] = down_refs[group][0]
-            down_tile[down_rows(1 - core), :] = down_refs[groups + group][0]
+            for at in range(per):
+                down_tile[down_rows(at, core), :] = down_refs[group][at]
+                down_tile[down_rows(at, 1 - core), :] = down_refs[groups + group][at]
 
     upper = _dot(x_ref[...], up_tile[...]) + bias_ref[...]
     square = upper * upper
@@ -250,8 +252,9 @@
         upper_low, up_tile[...], CONTRACT_LAST, preferred_element_type=jnp.float32
     )
     grad_tile[...] = _dot(hidden.T, g_ref[...]).astype(jnp.bfloat16)
-    down_keep[0] = grad_tile[down_rows(core), :]
-    down_send[0] = grad_tile[down_rows(1 - core), :]
+    for at in range(per):
+        down_keep[at] = grad_tile[down_rows(at, core), :]
+        down_send[at] = grad_tile[down_rows(at, 1 - core), :]
     up_tile[...] = _dot(x_turn[...], upper_low).astype(jnp.bfloat16)
     for place in range(chips):
         up_keep[place] = up_tile[up_rows(place, core), :]
@@ -262,39 +265,39 @@
     return lambda s, *t: (jnp.clip(s - group * size, 0, size - 1), 0, 0)
 
 
-def feed_forward(table, x, g, bias, down, up):
+def feed_forward(table, x, g, bias, down, up, per=2):
     tokens, width = x.shape
     groups = len(down) // 2
-    size = down[0].shape[0]
-    owned, inner = up[0].shape[1:]
+    size, span, _ = down[0].shape
+    owned = up[0].shape[1]
+    inner = bias.shape[1]
     chips = groups * size
-    span = inner // (chips * CORES)
-    tile = CORES * span
+    tile = per * CORES * span
     whole = lambda s, t: (0, 0)
-    column = lambda s, t: (0, t[s])
-    columns = lambda s, t: (0, 0, t[s])
-    down_spec = lambda place: pl.BlockSpec((1, span, width), place)
-    up_spec = pl.BlockSpec((up[0].shape[0], owned, tile), columns)
+    column = lambda s, t: (0, t[s * per] // per)
+    columns = lambda s, t: (0, 0, t[s * per] // per)
+    down_spec = lambda place: pl.BlockSpec((per, span, width), place)
+    up_spec = lambda count: pl.BlockSpec((count, owned, tile), columns)
     shape = jax.ShapeDtypeStruct
     return pl.pallas_call(
-        functools.partial(feed_forward_kernel, groups),
+        functools.partial(feed_forward_kernel, groups, per),
         grid_spec=pltpu.PrefetchScalarGridSpec(
             num_scalar_prefetch=1,
-            grid=(chips,),
+            grid=(chips // per,),
             in_specs=[
                 pl.BlockSpec((tokens, width), whole),
                 pl.BlockSpec((tokens, width), whole),
                 pl.BlockSpec((1, tile), column),
             ]
-            + [down_spec(group_place(group, size)) for group in range(groups)] * 2
-            + [up_spec] * len(up),
+            + [down_spec(group_place(group, size // per)) for group in range(groups)] * 2
+            + [up_spec(array.shape[0]) for array in up],
             out_specs=[
                 pl.BlockSpec((tokens, width), whole),
                 pl.BlockSpec((tokens, width), whole),
                 down_spec(lambda s, t: (s, 0, 0)),
                 down_spec(lambda s, t: (s, 0, 0)),
-                pl.BlockSpec((chips, owned, tile), columns),
-                pl.BlockSpec((chips, owned, tile), columns),
+                up_spec(chips),
+                up_spec(chips),
                 pl.BlockSpec((1, tile), column),
             ],
             scratch_shapes=[
@@ -357,6 +360,10 @@
     )(*values, *others)
 
 
+def widen(value, step):
+    return jnp.stack((value, swap(value, step)), axis=1).reshape((-1,) + value.shape[1:])
+
+
 def direct(value, axis):
     return [value] + [swap(value, (axis, m)) for m in range(1, lax.axis_size(axis))]
 
@@ -372,12 +379,11 @@
     return total
 
 
-def collect_next(total, axis):
-    low = total.astype(jnp.bfloat16)
-    own = total[0]
-    for m in range(1, total.shape[0]):
-        own = own + swap(low[m], (axis, m)).astype(jnp.float32)
-    return own
+def fold(total, axis):
+    for bit in bits_of(total.shape[0]):
+        pairs = total.reshape((total.shape[0] // 2, 2) + total.shape[1:])
+        total = pairs[:, 0] + swap(pairs[:, 1].astype(jnp.bfloat16), (axis, bit)).astype(jnp.float32)
+    return total[0]
 
 
 def spread(blocks, axis):
@@ -428,8 +434,9 @@
 
 
 def project_kernel(ways, table_ref, *refs):
-    rows, w_ref, gain_ref, shift_ref, bias_ref = refs[:5]
-    qkv_ref, normed_ref, unit_ref, weight_ref = refs[-4:]
+    own_ref, one_ref, two_ref, low_ref, high_ref, w_ref, gain_ref, shift_ref, bias_ref = refs[:9]
+    qkv_ref, normed_ref, unit_ref, weight_ref, rows = refs[-5:]
+    cut = low_ref.shape[0]
     step = pl.program_id(0)
     copies = w_ref.shape[0]
     owned = weight_ref.shape[0] // (ways * copies)
@@ -441,6 +448,17 @@
                 start = (sender * copies + (table_ref[1] ^ place)) * owned
                 weight_ref[pl.ds(pl.multiple_of(start, owned), owned), :] = w_ref[place, sender, :owned, :]
 
+    for block, ref in enumerate((own_ref, one_ref, two_ref)):
+
+        @pl.when(step == block)
+        def _():
+            rows[...] = ref[...]
+
+    @pl.when(step == 3)
+    def _():
+        rows[:cut] = low_ref[...]
+        rows[cut:] = high_ref[...]
+
     unit, _ = norm_parts(rows[...].astype(jnp.float32))
     normed = (unit * gain_ref[...] + shift_ref[...]).astype(jnp.bfloat16)
     unit_ref[...] = unit.astype(jnp.bfloat16)
@@ -448,14 +466,13 @@
     qkv_ref[...] = (_dot(normed, weight_ref[...]) + bias_ref[...]).astype(jnp.bfloat16)
 
 
-def project(table, tokens, packed, gain, shift, bias, ways, owned, deps=()):
-    width = tokens.shape[1]
-    local = tokens.shape[0] // ways
+def project(table, blocks, packed, gain, shift, bias, ways, owned, deps=()):
+    local, width = blocks[0].shape
     copies, _, _, triple = packed.shape
     whole = lambda s, t: (0, 0)
-    place = lambda s, t: (s, 0)
+    place = lambda s, t: (t[0] ^ s, 0)
     full = lambda array: pl.BlockSpec(array.shape, lambda s, t: (0,) * array.ndim)
-    operands = (packed, gain, shift, bias)
+    operands = tuple(blocks) + (packed, gain, shift, bias)
     shape = jax.ShapeDtypeStruct
     length = ways * local
     return pl.pallas_call(
@@ -463,8 +480,7 @@
         grid_spec=pltpu.PrefetchScalarGridSpec(
             num_scalar_prefetch=1,
             grid=(ways,),
-            in_specs=[pl.BlockSpec((local, width), place)]
-            + [full(array) for array in operands]
+            in_specs=[full(array) for array in operands]
             + [pl.BlockSpec(memory_space=pl.ANY)] * len(deps),
             out_specs=[
                 pl.BlockSpec((local, triple), place),
@@ -472,6 +488,7 @@
                 pl.BlockSpec((local, width), place),
                 pl.BlockSpec((width, triple), whole),
             ],
+            scratch_shapes=[pltpu.VMEM((local, width), jnp.bfloat16)],
         ),
         out_shape=[
             shape((length, triple), jnp.bfloat16),
@@ -482,7 +499,7 @@
         compiler_params=pltpu.CompilerParams(vmem_limit_bytes=VMEM_BYTES),
         cost_estimate=estimate(9),
         name="project",
-    )(table, tokens, *operands, *deps)
+    )(table, *operands, *deps)
 
 
 def input_grad_kernel(low_ref, high_ref, w_ref, normed_ref, unit_ref, *refs):
@@ -554,8 +571,8 @@
     def _():
         for place in range(groups * size):
             group, at = divmod(place, size)
-            weight_ref[output_rows(table_ref, place, core, owned), :] = parts[group][at]
-            weight_ref[output_rows(table_ref, place, 1 - core, owned), :] = parts[groups + group][at]
+            weight_ref[output_rows(table_ref, groups * size + place, core, owned), :] = parts[group][at]
+            weight_ref[output_rows(table_ref, groups * size + place, 1 - core, owned), :] = parts[groups + group][at]
 
     branch = _dot(join_groups(context_ref), weight_ref[...]) + bias_ref[...]
     residual = x_ref[...].astype(jnp.float32) + branch
@@ -564,16 +581,15 @@
     normed_ref[...] = (unit * gain_ref[...] + shift_ref[...]).astype(jnp.bfloat16)
 
 
-def project_output(table, context, parts, first, x, bias, gain, shift):
+def project_output(table, context, parts, x, bias, gain, shift):
     local, width = x.shape
     ways = context.shape[0]
     rows = 256
     vector = pl.BlockSpec((1, width), lambda s, t: (0, 0))
     block = pl.BlockSpec((rows, width), lambda s, t: (s, 0))
     heads = pl.BlockSpec((ways, rows, width // ways), lambda s, t: (0, s, 0))
-    size, total, _ = parts[0].shape
-    owned = total - first
-    weight = pl.BlockSpec((size, owned, width), lambda s, t: (0, first // owned, 0))
+    size, owned, total = parts[0].shape
+    weight = pl.BlockSpec((size, owned, width), lambda s, t: (0, 0, total // width - 1))
     shape = jax.ShapeDtypeStruct
     return pl.pallas_call(
         output_kernel,
@@ -663,37 +679,37 @@
 
 def meet_kernel(groups, up_groups, down_keep, down_came, output_keep, output_came, up_keep, up_came, *refs):
     step = pl.program_id(0)
-    size = pl.num_programs(0) // groups
+    steps = pl.num_programs(0)
     span = down_keep.shape[1]
 
     def both(left, right):
-        return (left[0].astype(jnp.float32) + right[0].astype(jnp.float32)).astype(jnp.bfloat16)
+        return (left[...].astype(jnp.float32) + right[...].astype(jnp.float32)).astype(jnp.bfloat16)
 
     for group in range(groups):
 
-        @pl.when(step // size == group)
+        @pl.when(step // (steps // groups) == group)
         def _():
-            refs[group][0, :span] = both(down_keep, down_came)
-            refs[group][0, span:] = both(output_keep, output_came)
+            refs[group][:, :span] = both(down_keep, down_came)
+            refs[group][:, span:] = both(output_keep, output_came)
 
     for group in range(up_groups):
 
-        @pl.when(step // (pl.num_programs(0) // up_groups) == group)
+        @pl.when(step // (steps // up_groups) == group)
         def _():
-            refs[groups + group][0] = both(up_keep, up_came)
-
-
-def meet(down_keep, down_came, output_keep, output_came, up_keep, up_came, groups, up_groups):
+            refs[groups + group][...] = both(up_keep, up_came)
+
+
+def meet(down_keep, down_came, output_keep, output_came, up_keep, up_came, groups, up_groups, per=2):
     chips, span, width = down_keep.shape
     owned, inner = up_keep.shape[1:]
-    block = lambda rows, columns: pl.BlockSpec((1, rows, columns), lambda s: (s, 0, 0))
+    block = lambda rows, columns: pl.BlockSpec((per, rows, columns), lambda s: (s, 0, 0))
     parts = [(span + owned, width, chips // groups, group) for group in range(groups)]
     parts += [(owned, inner, chips // up_groups, group) for group in range(up_groups)]
-    outs = [pl.BlockSpec((1, rows, columns), group_place(group, size)) for rows, columns, size, group in parts]
+    outs = [pl.BlockSpec((per, rows, columns), group_place(group, size // per)) for rows, columns, size, group in parts]
     shapes = [jax.ShapeDtypeStruct((size, rows, columns), jnp.bfloat16) for rows, columns, size, _ in parts]
     return pl.pallas_call(
         functools.partial(meet_kernel, groups, up_groups),
-        grid=(chips,),
+        grid=(chips // per,),
         in_specs=[block(span, width)] * 2 + [block(owned, width)] * 2 + [block(owned, inner)] * 2,
         out_specs=outs,
         out_shape=shapes,
@@ -1002,14 +1018,23 @@
     packed = jnp.concatenate([jnp.pad(vector, (0, 128 - vector.shape[0]))[None] for vector in vectors])
     packed = jnp.pad(packed, ((0, 8 - len(sizes)), (0, triple - 128)))
     by_group = jnp.concatenate((by_group, jnp.broadcast_to(packed[None], (ways, 8, triple))), axis=1)
-    owned_down = down_weight.shape[0]
-    down_shard = jnp.concatenate((down_weight, output_weight))
-    grouped = spread(by_group, "seq")
+    up_shard = jnp.concatenate((up_weight, output_weight), axis=1)
+    seq_steps = [("seq", bit) for bit in bits_of(ways)]
+    one, two = (swap(rows_in, step) for step in seq_steps)
+    up_one = widen(up_shard[None], ("ring", far_bit))
+    (by_group,) = after((by_group,), up_one)
+    (grouped,) = after((spread(by_group, "seq"),), one, two)
+    cut = local // 2
+    low, high = swap(two[:cut], seq_steps[0]), swap(one[cut:], seq_steps[1])
+    blocks = (rows_in, one, two, low, high)
     columns = grouped[None]
     for bit in (far_bit, near_bit):
-        columns = jnp.stack((columns, swap(columns, ("ring", bit))), axis=1).reshape((-1,) + by_group.shape)
-    up_one = jnp.stack((up_weight, swap(up_weight, ("ring", far_bit))))
-    down_one = jnp.stack(direct(down_shard, "ring"))
+        columns = widen(columns, ("ring", bit))
+        if bit == far_bit:
+            (columns,) = after((columns,), low, high)
+            (down_one,) = after((down_weight[None],), columns)
+    for bit in (far_bit, near_bit):
+        down_one = widen(down_one, ("ring", bit))
     columns = jnp.stack((columns, other_core(columns)), axis=1).reshape((copies,) + by_group.shape)
     found = columns[:, :, owned : owned + len(sizes), :128].reshape(world, -1)
     here = jnp.arange(world, dtype=jnp.int32)
@@ -1020,17 +1045,17 @@
     gain_first, shift_first, bias_input, bias_output, gain_second, shift_second, bias_up, bias_down = vectors
     bias_group = pair_columns(bias_input[0], seq_index, ways)[None]
 
-    all_rows = lax.all_gather(rows_in, "seq", tiled=True)
-
+
+    (up_one,) = after((up_one,), low, high)
     up_near = jnp.concatenate(direct(up_one, "seq"))
-    (down_one,) = after((down_one,), all_rows)
-    (up_near,) = after((up_near,), columns)
+    (down_one,) = after((down_one,), up_near)
+    (up_near,) = after((up_near,), columns, down_one)
     down_mine = direct(down_one, "seq")
     up_far = swap(up_near, ("ring", near_bit))
 
     places = jnp.stack((seq_index, copy_index)).astype(jnp.int32)
     qkv, normed, unit, weight_input = project(
-        places, all_rows, columns, gain_first, shift_first, bias_group, ways, owned, (down_one, up_near)
+        places, blocks, columns, gain_first, shift_first, bias_group, ways, owned
     )
     head_ids = (seq_index * head_group + jnp.arange(head_group, dtype=jnp.int32)).astype(jnp.float32)
     slopes = jnp.exp2(-8.0 * (head_ids + 1.0) / HEADS)
@@ -1040,20 +1065,21 @@
             value.reshape(ways, local, -1), "seq", split_axis=0, concat_axis=0, tiled=True
         )
 
-    kept, contexts, done = [], [], ()
+    swapped = other_core(up_near)
+    kept, contexts, done = [], [], (down_one, up_near)
     for pair in range(2):
         context, wide, log_totals = attend_forward(slopes[2 * pair : 2 * pair + 2], qkv, pair, done)
         kept.append((wide, log_totals))
         contexts.append(context)
-        done = (log_totals,)
+        done = (log_totals, swapped)
     context = exchange(jnp.concatenate(contexts, axis=1))
 
-    mine = list(after(down_mine + [up_near, up_far], context))
-    theirs = [other_core(group) for group in mine]
-    down = mine[:ways] + theirs[:ways]
-    up = mine[ways:] + theirs[ways:]
+    late = list(after([up_far] + down_mine, context))
+    theirs = [other_core(group) for group in late]
+    down = late[1:] + theirs[1:]
+    up = [up_near, late[0], swapped, theirs[0]]
     residual, normed_two, weight_output = project_output(
-        table, context, down, owned_down, rows_in, bias_output, gain_second, shift_second
+        table, context, up, rows_in, bias_output, gain_second, shift_second
     )
     layer, grad_normed_two, down_keep, down_send, up_keep, up_send, grad_up_bias = feed_forward(
         table, normed_two, upstream, bias_up, down, up
@@ -1061,7 +1087,6 @@
     grad_residual, context_grad, output_keep, output_send, middle_sums = residual_grad(
         table, grad_normed_two, residual, upstream, context, weight_output, gain_second, chips
     )
-    layer_out = (residual + layer + bias_down).astype(jnp.bfloat16)
 
     context_grad = exchange(context_grad).reshape(length, -1)
     met = list(
@@ -1070,29 +1095,24 @@
     met = list(after(met, context_grad))
     came = [swap(met[m], ("seq", m)) for m in range(1, ways)] + [swap(met[ways + 1], ("ring", near_bit))]
 
-    grads = []
+    grads, ready = [], [met[0], met[ways]]
     for pair in range(2):
-        ready = grads + [met[0]]
         grads.append(attend_backward(slopes[2 * pair : 2 * pair + 2], qkv, context_grad, *kept[pair], pair, ready))
-    came = after(came, grads[1])
+        ready = [grads[0]]
+    (up_came,) = after(came[ways - 1 :], grads[1])
+    up_sum = (met[ways].astype(jnp.float32) + up_came.astype(jnp.float32)).astype(jnp.bfloat16)
+    up_sum = up_sum.reshape((ways, 2) + up_sum.shape[1:])
     down_sum = met[0].astype(jnp.float32)
-    for part in came[: ways - 1]:
-        down_sum = down_sum + part.astype(jnp.float32)
-    down_sum = down_sum.astype(jnp.bfloat16)
-    up_sum = (met[ways].astype(jnp.float32) + came[ways - 1].astype(jnp.float32)).astype(jnp.bfloat16)
-    up_sum = up_sum.reshape((ways, 2) + up_sum.shape[1:])
+    for group in after(came[: ways - 1], up_sum):
+        down_sum = down_sum + group.astype(jnp.float32)
 
     part, grad_columns, first_sums, bias_sums = input_grad(
         grads[0], grads[1], weight_input, normed, unit, (down_sum, up_sum)
     )
-    down_sum = collect_next(down_sum, "ring")
-    up_sum = collect_next(up_sum, "seq")
-    grad_up_weight = up_sum[0] + swap(up_sum[1].astype(jnp.bfloat16), ("ring", far_bit)).astype(jnp.float32)
-    grad_down_weight, grad_output_weight = down_sum[:owned_down], down_sum[owned_down:]
-    grad_normed = jnp.sum(exchange(part).astype(jnp.float32), axis=0)
-    inputs = rows_in.astype(jnp.float32)
-    tokens_grad = grad_residual + norm_back(grad_normed, gain_first, *norm_parts(inputs))
-
+    up_came = [swap(up_sum[m], ("seq", m)) for m in range(1, ways)]
+    down_sum = down_sum.reshape((2, 2) + down_sum.shape[1:])
+    down_came = swap(down_sum[:, 1].astype(jnp.bfloat16), ("ring", near_bit))
+    down_sum = down_sum[:, 0] + down_came.astype(jnp.float32)
     sums = (
         first_sums[0],
         first_sums[1],
@@ -1109,11 +1129,37 @@
     both = jnp.concatenate((grad_columns.reshape(world, owned, triple), rows), axis=1)
     both = both.reshape(ways, rings, CORES, owned + 8, triple)
     came = other_core(lax.dynamic_index_in_dim(both, 1 - core, 2, keepdims=False))
-    both = add_low(lax.dynamic_index_in_dim(both, core, 2, keepdims=False), came)
+    (came,) = after((came,), *up_came, down_came)
+    both = lax.dynamic_index_in_dim(both, core, 2, keepdims=False).astype(jnp.float32) + came.astype(jnp.float32)
     ring = lax.axis_index("ring")
-    both = collect([lax.dynamic_index_in_dim(both, ring ^ m, 1, keepdims=False) for m in range(rings)], "ring")
-    both = spread(both.astype(jnp.bfloat16), "seq")
-    grad_input_weight = ungroup_columns(both[:, :owned]).astype(jnp.float32)
+    both = jnp.stack([lax.dynamic_index_in_dim(both, ring ^ m, 1, keepdims=False) for m in range(rings)])
+    up_sum = up_sum[0].astype(jnp.float32)
+    for group in up_came:
+        up_sum = up_sum + group.astype(jnp.float32)
+    grad_normed = jnp.sum(exchange(part).astype(jnp.float32), axis=0)
+    inputs = rows_in.astype(jnp.float32)
+    tokens_grad = grad_residual + norm_back(grad_normed, gain_first, *norm_parts(inputs))
+
+    (layer,) = after((layer,), both)
+    layer_out = (residual + layer + bias_down).astype(jnp.bfloat16)
+    both = fold(both, "ring").astype(jnp.bfloat16)
+    down_low, up_low = after([value[1].astype(jnp.bfloat16) for value in (down_sum, up_sum)], both)
+    down_came, up_came = swap(down_low, ("ring", far_bit)), swap(up_low, ("ring", far_bit))
+    both = spread(both, "seq")
+    down_came, up_came = after((down_came, up_came), tokens_grad)
+    down_sum = down_sum[0] + down_came.astype(jnp.float32)
+    grad_up_weight = up_sum[0] + up_came.astype(jnp.float32)
+    grad_down_weight, grad_output_weight = down_sum[: down_weight.shape[0]], down_sum[down_weight.shape[0] :]
+    wide = 2 * HEAD
+    grad_input_weight = jnp.concatenate(
+        [
+            both[sender, :owned, (3 * pair + part) * wide : (3 * pair + part + 1) * wide]
+            for part in range(3)
+            for sender in range(ways)
+            for pair in range(head_group // 2)
+        ],
+        axis=1,
+    ).astype(jnp.float32)
     rows = jnp.sum(both[:, owned:, :128].astype(jnp.float32), axis=0)
     small = [rows[i, :size] for i, size in enumerate(sizes)]
     return (

time: 443 us -> 407 us (0.919)
  waiting for transfers between devices: 137 us -> 93.9 us
  local copies, waits for them, and re-layouts: 28.8 us -> 42.7 us
  between operations: 15.1 us -> 1.85 us
  other arithmetic: 28.1 us -> 37.5 us
  Pallas kernels: 170 us -> 162 us
  starting transfers between devices: 59.1 us -> 64.8 us
    ppermute x44 -> x45, waiting for transfers between devices: 112 us -> 90.1 us  [swap(): lax.ppermute(value, axis, [(i, i ^ bit) for i in range(lax.axis_size(axis...]
    all_to_all x3, waiting for transfers between devices: 25.2 us -> 3.8 us  [exchange(): lax.all_to_all(value.reshape(ways, local, -1), 'seq', split_axis=0, conca...]
    unnamed x76 -> x123, local copies, waits for them, and re-layouts: 8.82 us -> 18.5 us
    add x3 -> x7, other arithmetic: 3.93 us -> 12.1 us  [the longest x1 3.62 us: blocked_body(): down_sum = down_sum + group.astype(jnp.float32)]
    ppermute x44 -> x45, starting transfers between devices: 46.5 us -> 52.2 us  [swap(): lax.ppermute(value, axis, [(i, i ^ bit) for i in range(lax.axis_size(axis...]
    pallas_call x1, Pallas kernels: 45.7 us -> 41 us  [feed_forward(): pl.pallas_call(functools.partial(feed_forward_kernel, groups, per), grid_...]
  transfers between devices with their start and end apart: 48 -> 48, of which waited for: 21 -> 17; matrix products, arithmetic and copies ran while one was open for 9% -> 14% of each run, Pallas kernels for 28% -> 30%
where the time goes in v3:
time: 407 us; the launch traced here: 403 us
  Pallas kernels  162 us (40%)
  waiting for transfers between devices  93.9 us (23%)
  starting transfers between devices  64.8 us (16%)
  local copies, waits for them, and re-layouts  42.7 us (10%)
  other arithmetic  37.5 us (9%)
    ppermute x45, waiting for transfers between devices, swap(): lax.ppermute(value, axis, [(i, i ^ bit) for i in range(lax.axis_size(axis...  90.1 us
    ppermute x45, starting transfers between devices, swap(): lax.ppermute(value, axis, [(i, i ^ bit) for i in range(lax.axis_size(axis...  52.2 us
    pallas_call x2, Pallas kernels, attend_backward(): pl.pallas_call(backward_kernel, grid=(2,), in_specs=[pl.BlockSpec(memory_...  46.2 us
    pallas_call x1, Pallas kernels, feed_forward(): pl.pallas_call(functools.partial(feed_forward_kernel, groups, per), grid_...  41 us
    pallas_call x2, Pallas kernels, attend_forward(): pl.pallas_call(forward_kernel, grid=(2,), in_specs=[pl.BlockSpec(memory_s...  23.6 us
    unnamed x123, local copies, waits for them, and re-layouts  18.5 us
    all_to_all x3, starting transfers between devices, exchange(): lax.all_to_all(value.reshape(ways, local, -1), 'seq', split_axis=0, conca...  12.6 us
    pallas_call x1, Pallas kernels, input_grad(): pl.pallas_call(input_grad_kernel, grid=(length // rows,), in_specs=[block...  12.6 us
  transfers between devices with their start and end apart: 48, of which 17 were waited for; matrix products, arithmetic and copies ran while one was open for 14% of the time, Pallas kernels for 30%

profile of v3, /device:TPU:0, one launch (start us, length us, event | category | flops | bytes accessed | tf_op | source)
XLA Modules:
  0.0 403.2 jit_solution(1160314266923907193)
XLA Ops:
  0.7 1.7 copy.194
  2.4 2.9 collective-permute-start
  5.4 1.5 collective-permute-start.1
  8.7 2.6 collective-permute-start.4
  13.5 12.0 %collective-permute-done.4 = bf16[1,32,5120]{2,1,0:T(8,128)(2,1)S(1)} collective-permute-done((bf16[1,32,5120]{2,1,0:T(8,128)(2,1)S(1)}, bf16[1,32,5120]{2,1,0:T(8,128)(2,1)S(1)}, u32[]{:S(2)}, u32[]{:S(2)}) %collective-permute-start.4) | collective-permute-done | bytes 327712 | tf_op jit(solution)/shard_map/ppermute | solution.py:331
  28.4 2.5 collective-permute-start.7
  34.5 1.4 collective-permute-start.3
  36.6 2.6 collective-permute-start.8
  39.2 9.4 %collective-permute-done.8 = bf16[1,4,40,768]{3,2,1,0:T(8,128)(2,1)S(1)} collective-permute-done((bf16[1,4,40,768]{3,2,1,0:T(8,128)(2,1)}, bf16[1,4,40,768]{3,2,1,0:T(8,128)(2,1)S(1)}, u32[]{:S(2)}, u32[]{:S(2)}) %collective-permute-start.8) | collective-permute-done | bytes 245792 | tf_op jit(solution)/shard_map/ppermute | solution.py:331
  48.6 1.8 maximum_bitcast_fusion.1.refs_0_
  53.0 2.4 collective-permute-start.15
  55.5 3.3 collective-permute-start.11
  58.7 10.5 %collective-permute-done.9 = bf16[2,4,40,768]{3,2,1,0:T(8,128)(2,1)S(1)} collective-permute-done((bf16[2,4,40,768]{3,2,1,0:T(8,128)(2,1)}, bf16[2,4,40,768]{3,2,1,0:T(8,128)(2,1)S(1)}, u32[]{:S(2)}, u32[]{:S(2)}) %collective-permute-start.9) | collective-permute-done | bytes 491552 | tf_op jit(solution)/shard_map/ppermute | solution.py:331
  69.6 3.1 collective-permute-start.12
  72.7 10.0 %collective-permute-done.14 = bf16[2,32,5120]{2,1,0:T(8,128)(2,1)} collective-permute-done((bf16[2,32,5120]{2,1,0:T(8,128)(2,1)}, bf16[2,32,5120]{2,1,0:T(8,128)(2,1)}, u32[]{:S(2)}, u32[]{:S(2)}) %collective-permute-start.14) | collective-permute-done | bytes 655392 | tf_op jit(solution)/shard_map/ppermute | solution.py:331
  82.7 3.2 pad_maximum_fusion.refs_1_.refs_0_
  87.2 1.4 copy.81
  90.3 1.6 collective-permute-start.18
  92.4 1.4 collective-permute-start.20
  96.9 11.4 %project.1 = (bf16[2048,768]{1,0:T(8,128)(2,1)}, bf16[2048,1024]{1,0:T(8,128)(2,1)}, bf16[2048,1024]{1,0:T(8,128)(2,1)}, bf16[1024,768]{1,0:T(8,128)(2,1)}) custom-call(s32[2]{0:T(128)} %pad_add_fusion.1.table_ref, bf16[512,1024]{1,0:T(8,128)(2,1)} %bitcast.278, bf16[512,1024]{1,0:T(8,128)(2,1)} %copy-done.13, bf16[512,1024]{1,0:T(8,128)(2,1)} %copy-done.14, ...), custom_call_target="tpu_custom_call" | custom-call | flops 900000000 | tf_op jit(solution)/shard_map/project/pallas_call | solution.py:478
  108.3 11.7 %attend_forward.2 = (bf16[2048,128]{1,0:T(8,128)(2,1)}, f32[128,2048]{1,0:T(8,128)}, f32[16,2048]{1,0:T(8,128)}) custom-call(f32[2]{0:T(128)} %get-tuple-element.160.slope_ref, bf16[2048,768]{1,0:T(8,128)(2,1)} %get-tuple-element.67.q_ref.k_ref.v_ref, bf16[2048,768]{1,0:T(8,128)(2,1)} %get-tuple-element.67.q_ref.k_ref.v_ref, ...), custom_call_target="tpu_custom_call" | custom-call | flops 1050000000 | tf_op jit(solution)/shard_map/attend_forward/pallas_call | solution.py:82
  120.1 11.8 %attend_forward.3 = (bf16[2048,128]{1,0:T(8,128)(2,1)}, f32[128,2048]{1,0:T(8,128)}, f32[16,2048]{1,0:T(8,128)}) custom-call(f32[2]{0:T(128)} %get-tuple-element.161.slope_ref, bf16[2048,768]{1,0:T(8,128)(2,1)} %get-tuple-element.67.q_ref.k_ref.v_ref, bf16[2048,768]{1,0:T(8,128)(2,1)} %get-tuple-element.67.q_ref.k_ref.v_ref, ...), custom_call_target="tpu_custom_call" | custom-call | flops 1050000000 | tf_op jit(solution)/shard_map/attend_forward/pallas_call | solution.py:82
  131.9 2.1 pad_maximum_fusion.4
  134.0 4.0 %all-to-all-start = ((bf16[4,512,256]{2,1,0:T(8,128)(2,1)}), bf16[4,512,256]{2,1,0:T(8,128)(2,1)S(1)}, u32[]{:S(2)}, u32[]{:S(2)}) async-start(bf16[4,512,256]{2,1,0:T(8,128)(2,1)} %bitcast.37), calls=%async_computation | async-start | bytes 2097152 | tf_op jit(solution)/shard_map/all_to_all | solution.py:1064
  138.1 1.4 collective-permute-done.19.refs_3_
  139.5 8.8 %collective-permute-done.17.refs_0_ = bf16[8,32,5120]{2,1,0:T(8,128)(2,1)} collective-permute-done((bf16[8,32,5120]{2,1,0:T(8,128)(2,1)}, bf16[8,32,5120]{2,1,0:T(8,128)(2,1)}, u32[]{:S(2)}, u32[]{:S(2)}) %collective-permute-start.17) | collective-permute-done | bytes 2621472 | tf_op jit(solution)/shard_map/ppermute | solution.py:331
  148.3 3.2 all-to-all-done.refs_5_.context_ref
  156.8 4.7 %collective-permute-done.21.refs_3_.refs_11_ = bf16[8,32,5120]{2,1,0:T(8,128)(2,1)} collective-permute-done((bf16[8,32,5120]{2,1,0:T(8,128)(2,1)}, bf16[8,32,5120]{2,1,0:T(8,128)(2,1)}, u32[]{:S(2)}, u32[]{:S(2)}) %collective-permute-start.21) | collective-permute-done | bytes 2621472 | tf_op jit(solution)/shard_map/ppermute | solution.py:331
  161.5 5.8 %project_output.1 = (f32[512,1024]{1,0:T(8,128)}, bf16[512,1024]{1,0:T(8,128)(2,1)}, bf16[1024,1024]{1,0:T(8,128)(2,1)}) custom-call(s32[33]{0:T(128)} %pad_add_fusion.table_ref, bf16[4,512,256]{2,1,0:T(8,128)(2,1)} %copy-done.6, bf16[512,1024]{1,0:T(8,128)(2,1)} %bitcast.279, f32[1,1024]{1,0:T(1,128)} %reshape.212.bias_ref, f32[1,1024]{1,0:T(1,128)} %reshape.213.gain_ref, ...), custom_call_target="tpu_custom_call" | custom-call | flops 500000000 | tf_op jit(solution)/shard_map/project_output/pallas_call | solution.py:594
  168.9 41.0 %feed_forward.1 = (f32[512,1024]{1,0:T(8,128)}, f32[512,1024]{1,0:T(8,128)}, bf16[16,128,1024]{2,1,0:T(8,128)(2,1)}, bf16[16,128,1024]{2,1,0:T(8,128)(2,1)}, bf1...) custom-call(s32[33]{0:T(128)} %pad_add_fusion.table_ref, ...), custom_call_target="tpu_custom_call" | custom-call | flops 4499999744 | tf_op jit(solution)/shard_map/feed_forward/pallas_call | solution.py:282
  210.5 9.7 %residual_grad.1 = (f32[512,1024]{1,0:T(8,128)}, bf16[4,512,256]{2,1,0:T(8,128)(2,1)}, bf16[16,32,1024]{2,1,0:T(8,128)(2,1)}, bf16[16,32,1024]{2,1,0:T(8,128)(2,1)}, f32[8,1024]{1,0:T(8,128)}) custom-call(s32[33]{0:T(128)} %pad_add_fusion.table_ref, f32[512,1024]{1,0:T(8,128)} %get-tuple-element.79.grad_ref, f32[512,1024]{1,0:T(8,128)} %get-tuple-element.72.residual_ref, ...), custom_call_target="tpu_custom_call" | custom-call | flops 700000000 | tf_op jit(solution)/shard_map/residual_grad/pallas_call | solution.py:658
  220.4 3.7 all-to-all-start.1
  225.9 12.1 %meet.1 = (bf16[4,160,1024]{2,1,0:T(8,128)(2,1)}, bf16[4,160,1024]{2,1,0:T(8,128)(2,1)}, bf16[4,160,1024]{2,1,0:T(8,128)(2,1)}, bf16[4,160,1024]{2,1,0:T(8,128)(...) custom-call(bf16[16,128,1024]{2,1,0:T(8,128)(2,1)} %get-tuple-element.83.down_keep, ...), custom_call_target="tpu_custom_call" | custom-call | flops 900000000 | tf_op jit(solution)/shard_map/meet/pallas_call | solution.py:710
  239.5 1.7 collective-permute-start.32
  242.4 1.5 collective-permute-start.29
  244.6 1.3 collective-permute-start.31
  246.0 23.1 %attend_backward.2.refs_0_.low_ref = bf16[2048,384]{1,0:T(8,128)(2,1)} custom-call(f32[2]{0:T(128)} %get-tuple-element.160.slope_ref, bf16[2048,768]{1,0:T(8,128)(2,1)} %get-tuple-element.67.q_ref.k_ref.v_ref, bf16[2048,768]{1,0:T(8,128)(2,1)} %get-tuple-element.67.q_ref.k_ref.v_ref, bf16[2048,768]{1,0:T(8,128)(2,1)} %get-tuple-element.67.q_ref.k_ref.v_ref, ...), custom_call_target="tpu_custom_call" | custom-call | flops 2200000000 | tf_op jit(solution)/shard_map/attend_backward/pallas_call | solution.py:170
  269.0 23.1 %attend_backward.3.refs_1_.high_ref = bf16[2048,384]{1,0:T(8,128)(2,1)} custom-call(f32[2]{0:T(128)} %get-tuple-element.161.slope_ref, bf16[2048,768]{1,0:T(8,128)(2,1)} %get-tuple-element.67.q_ref.k_ref.v_ref, bf16[2048,768]{1,0:T(8,128)(2,1)} %get-tuple-element.67.q_ref.k_ref.v_ref, bf16[2048,768]{1,0:T(8,128)(2,1)} %get-tuple-element.67.q_ref.k_ref.v_ref, ...), custom_call_target="tpu_custom_call" | custom-call | flops 2200000000 | tf_op jit(solution)/shard_map/attend_backward/pallas_call | solution.py:170
  292.2 1.3 copy-done.11
  293.5 3.0 add_convert_fusion
  297.8 1.4 collective-permute-start.34
  299.9 1.3 collective-permute-start.36
  301.3 2.3 collective-permute-done.31.refs_2_
  303.6 3.6 convert_add_fusion.refs_0_
  307.2 1.6 copy-done.3
  310.9 12.6 %input_grad.1 = (bf16[2048,1024]{1,0:T(8,128)(2,1)}, bf16[1024,768]{1,0:T(8,128)(2,1)}, f32[8,1024]{1,0:T(8,128)}, f32[8,768]{1,0:T(8,128)}) custom-call(bf16[2048,384]{1,0:T(8,128)(2,1)} %attend_backward.2.refs_0_.low_ref, bf16[2048,384]{1,0:T(8,128)(2,1)} %attend_backward.3.refs_1_.high_ref, bf16[1024,768]{1,0:T(8,128)(2,1)} %get-tuple-element.99.w_ref, ...), custom_call_target="tpu_custom_call" | custom-call | flops 1000000000 | tf_op jit(solution)/shard_map/input_grad/pallas_call | solution.py:535
  325.5 2.2 fusion.12
  327.7 4.8 %all-to-all-start.2 = ((bf16[4,512,1024]{2,1,0:T(8,128)(2,1)}), bf16[4,512,1024]{2,1,0:T(8,128)(2,1)}, u32[]{:S(2)}, u32[]{:S(2)}) async-start(bf16[4,512,1024]{2,1,0:T(8,128)(2,1)} %bitcast.297), calls=%async_computation.2 | async-start | bytes 8388608 | tf_op jit(solution)/shard_map/all_to_all | solution.py:1064
  332.6 1.8 convert_add_fusion.2
  336.1 1.4 copy-done.15
  337.5 1.4 convert_add_fusion.1
  341.8 1.3 fusion.9
  344.3 9.7 %collective-permute-done.38 = bf16[2,4,40,768]{3,2,1,0:T(8,128)(2,1)S(1)} collective-permute-done((bf16[2,4,40,768]{3,2,1,0:T(8,128)(2,1)}, bf16[2,4,40,768]{3,2,1,0:T(8,128)(2,1)S(1)}, u32[]{:S(2)}, u32[]{:S(2)}) %collective-permute-start.38) | collective-permute-done | bytes 491552 | tf_op jit(solution)/shard_map/ppermute | solution.py:331
  354.1 3.3 collective-permute-start.39
  357.5 3.1 fusion.10
  360.5 8.2 %collective-permute-done.39 = bf16[1,4,40,768]{3,2,1,0:T(8,128)(2,1)S(1)} collective-permute-done((bf16[1,4,40,768]{3,2,1,0:T(8,128)(2,1)S(1)}, bf16[1,4,40,768]{3,2,1,0:T(8,128)(2,1)S(1)}, u32[]{:S(2)}, u32[]{:S(2)}) %collective-permute-start.39) | collective-permute-done | bytes 245792 | tf_op jit(solution)/shard_map/ppermute | solution.py:331
  369.4 2.9 collective-permute-start.44
  372.4 1.4 collective-permute-start.40
  373.7 1.5 collective-permute-start.41
  376.7 5.8 %collective-permute-done.40 = bf16[1,40,768]{2,1,0:T(8,128)(2,1)S(1)} collective-permute-done((bf16[1,40,768]{2,1,0:T(8,128)(2,1)S(1)}, bf16[1,40,768]{2,1,0:T(8,128)(2,1)S(1)}, u32[]{:S(2)}, u32[]{:S(2)}) %collective-permute-start.40) | collective-permute-done | bytes 61472 | tf_op jit(solution)/shard_map/ppermute | solution.py:331
  382.6 1.8 collective-permute-done.42
  387.0 3.4 convert_reduce_fusion
  392.0 2.0 fusion.7.refs_2_
  394.1 4.0 collective-permute-done.44.refs_1_
  (294 shorter events, 56.9 us)
Async XLA Ops:
  0.6 12.1 %copy-start.44 = (bf16[32]{0:T(256)(128)(2,1)S(1)}, bf16[32]{0:T(256)(128)(2,1)}, u32[]{:S(2)}) copy-start(bf16[32]{0:T(256)(128)(2,1)} %param.18) | copy-start | bytes 196
  0.7 12.1 %copy-start.42 = (bf16[32]{0:T(256)(128)(2,1)S(1)}, bf16[32]{0:T(256)(128)(2,1)}, u32[]{:S(2)}) copy-start(bf16[32]{0:T(256)(128)(2,1)} %param.19) | copy-start | bytes 196
  0.7 12.1 %copy-start.41 = (bf16[64]{0:T(256)(128)(2,1)S(1)}, bf16[64]{0:T(256)(128)(2,1)}, u32[]{:S(2)}) copy-start(bf16[64]{0:T(256)(128)(2,1)} %param.21) | copy-start | bytes 388
  0.7 12.0 %copy-start.40 = (bf16[32]{0:T(256)(128)(2,1)S(1)}, bf16[32]{0:T(256)(128)(2,1)}, u32[]{:S(2)}) copy-start(bf16[32]{0:T(256)(128)(2,1)} %param.23) | copy-start | bytes 196
  0.7 12.0 %copy-start.39 = (bf16[32]{0:T(256)(128)(2,1)S(1)}, bf16[32]{0:T(256)(128)(2,1)}, u32[]{:S(2)}) copy-start(bf16[32]{0:T(256)(128)(2,1)} %param.24) | copy-start | bytes 196
  0.7 11.9 %copy-start.38 = (bf16[32]{0:T(256)(128)(2,1)S(1)}, bf16[32]{0:T(256)(128)(2,1)}, u32[]{:S(2)}) copy-start(bf16[32]{0:T(256)(128)(2,1)} %param.25) | copy-start | bytes 196
  0.7 12.1 %copy-start.36 = (bf16[128]{0:T(256)(128)(2,1)S(1)}, bf16[128]{0:T(256)(128)(2,1)}, u32[]{:S(2)}) copy-start(bf16[128]{0:T(256)(128)(2,1)} %param.27) | copy-start | bytes 772
  0.7 11.9 %copy-start.37 = (bf16[32]{0:T(256)(128)(2,1)S(1)}, bf16[32]{0:T(256)(128)(2,1)}, u32[]{:S(2)}) copy-start(bf16[32]{0:T(256)(128)(2,1)} %param.29) | copy-start | bytes 196
  2.4 31.1 %collective-permute-start = (bf16[512,1024]{1,0:T(8,128)(2,1)}, bf16[512,1024]{1,0:T(8,128)(2,1)S(1)}, u32[]{:S(2)}, u32[]{:S(2)}) collective-permute-start(bf16[512,1024]{1,0:T(8,128)(2,1)} %bitcast.276), channel_id=1, source_target_pairs={{0,8},{8,0},{16,24},{24,16},{1,9},{9,1},{17,25},{25,17},{2,10},{10... | collective-permute-start | bytes 3145736 | tf_op jit(solution)/shard_map/ppermute | solution.py:331
  5.4 26.4 %collective-permute-start.1 = (bf16[512,1024]{1,0:T(8,128)(2,1)}, bf16[512,1024]{1,0:T(8,128)(2,1)S(1)}, u32[]{:S(2)}, u32[]{:S(2)}) collective-permute-start(bf16[512,1024]{1,0:T(8,128)(2,1)} %bitcast.277), channel_id=1, source_target_pairs={{0,16},{8,24},{16,0},{24,8},{1,17},{9,25},{17,1},{25,9},{2,18},{10... | collective-permute-start | bytes 3145736 | tf_op jit(solution)/shard_map/ppermute | solution.py:331
  8.7 16.8 %collective-permute-start.4 = (bf16[1,32,5120]{2,1,0:T(8,128)(2,1)S(1)}, bf16[1,32,5120]{2,1,0:T(8,128)(2,1)S(1)}, u32[]{:S(2)}, u32[]{:S(2)}) collective-permute-start(bf16[1,32,5120]{2,1,0:T(8,128)(2,1)S(1)} %bitcast.309), channel_id=1, source_target_pairs={{0,4},{2,6},{4,0},{6,2},{1,5},{3,7},{5,1},{7,3},{8,12},{10,14},{12... | collective-permute-start | bytes 983048 | tf_op jit(solution)/shard_map/ppermute | solution.py:331
  27.4 4.3 %collective-permute-start.5 = (bf16[1,40,768]{2,1,0:T(8,128)(2,1)S(1)}, bf16[1,40,768]{2,1,0:T(8,128)(2,1)S(1)}, u32[]{:S(2)}, u32[]{:S(2)}) collective-permute-start(bf16[1,40,768]{2,1,0:T(8,128)(2,1)S(1)} %get-tuple-element.142), channel_id=1, source_target_pairs={{0,8},{8,0},{16,24},{24,16},{1,9},{9,1},{17,25},{25,17},{2,10},{10... | collective-permute-start | bytes 184328 | tf_op jit(solution)/shard_map/ppermute | solution.py:331
  28.0 7.9 %collective-permute-start.6 = (bf16[1,40,768]{2,1,0:T(8,128)(2,1)S(1)}, bf16[1,40,768]{2,1,0:T(8,128)(2,1)S(1)}, u32[]{:S(2)}, u32[]{:S(2)}) collective-permute-start(bf16[1,40,768]{2,1,0:T(8,128)(2,1)S(1)} %get-tuple-element.141), channel_id=1, source_target_pairs={{0,16},{8,24},{16,0},{24,8},{1,17},{9,25},{17,1},{25,9},{2,18},{10... | collective-permute-start | bytes 184328 | tf_op jit(solution)/shard_map/ppermute | solution.py:331
  28.4 7.4 %collective-permute-start.7 = (bf16[1,40,768]{2,1,0:T(8,128)(2,1)S(1)}, bf16[1,40,768]{2,1,0:T(8,128)(2,1)S(1)}, u32[]{:S(2)}, u32[]{:S(2)}) collective-permute-start(bf16[1,40,768]{2,1,0:T(8,128)(2,1)S(1)} %get-tuple-element.140), channel_id=1, source_target_pairs={{0,24},{8,16},{16,8},{24,0},{1,25},{9,17},{17,9},{25,1},{2,26},{10... | collective-permute-start | bytes 184328 | tf_op jit(solution)/shard_map/ppermute | solution.py:331
  32.7 17.7 %collective-permute-start.2 = (bf16[256,1024]{1,0:T(8,128)(2,1)}, bf16[256,1024]{1,0:T(8,128)(2,1)S(1)}, u32[]{:S(2)}, u32[]{:S(2)}) collective-permute-start(bf16[256,1024]{1,0:T(8,128)(2,1)} %slice.311), channel_id=1, source_target_pairs={{0,8},{8,0},{16,24},{24,16},{1,9},{9,1},{17,25},{25,17},{2,10},{10... | collective-permute-start | bytes 1572872 | tf_op jit(solution)/shard_map/ppermute | solution.py:331
  34.5 15.9 %collective-permute-start.3 = (bf16[256,1024]{1,0:T(8,128)(2,1)}, bf16[256,1024]{1,0:T(8,128)(2,1)}, u32[]{:S(2)}, u32[]{:S(2)}) collective-permute-start(bf16[256,1024]{1,0:T(8,128)(2,1)} %slice.312), channel_id=1, source_target_pairs={{0,16},{8,24},{16,0},{24,8},{1,17},{9,25},{17,1},{25,9},{2,18},{10... | collective-permute-start | bytes 1572872 | tf_op jit(solution)/shard_map/ppermute | solution.py:331
  36.6 12.0 %collective-permute-start.8 = (bf16[1,4,40,768]{3,2,1,0:T(8,128)(2,1)}, bf16[1,4,40,768]{3,2,1,0:T(8,128)(2,1)S(1)}, u32[]{:S(2)}, u32[]{:S(2)}) collective-permute-start(bf16[1,4,40,768]{3,2,1,0:T(8,128)(2,1)} %bitcast.307), channel_id=1, source_target_pairs={{0,4},{2,6},{4,0},{6,2},{1,5},{3,7},{5,1},{7,3},{8,12},{10,14},{12... | collective-permute-start | bytes 737288 | tf_op jit(solution)/shard_map/ppermute | solution.py:331
  51.2 18.1 %copy-start.12 = (bf16[2,4,40,768]{3,2,1,0:T(8,128)(2,1)S(1)}, bf16[2,4,40,768]{3,2,1,0:T(8,128)(2,1)}, u32[]{:S(2)}) copy-start(bf16[2,4,40,768]{3,2,1,0:T(8,128)(2,1)} %after.17.refs_1_) | copy-start | bytes 1474564
  51.2 18.1 %collective-permute-start.9 = (bf16[2,4,40,768]{3,2,1,0:T(8,128)(2,1)}, bf16[2,4,40,768]{3,2,1,0:T(8,128)(2,1)S(1)}, u32[]{:S(2)}, u32[]{:S(2)}) collective-permute-start(bf16[2,4,40,768]{3,2,1,0:T(8,128)(2,1)} %after.17.refs_1_), channel_id=1, source_target_pairs={{0,2},{2,0},{4,6},{6,4},{1,3},{3,1},{5,7},{7,5},{8,10},{10,8},{12,... | collective-permute-start | bytes 1474568 | tf_op jit(solution)/shard_map/ppermute | solution.py:331
  52.0 20.7 %collective-permute-start.13 = (bf16[2,32,5120]{2,1,0:T(8,128)(2,1)}, bf16[2,32,5120]{2,1,0:T(8,128)(2,1)}, u32[]{:S(2)}, u32[]{:S(2)}) collective-permute-start(bf16[2,32,5120]{2,1,0:T(8,128)(2,1)} %after.19), channel_id=1, source_target_pairs={{0,8},{8,0},{16,24},{24,16},{1,9},{9,1},{17,25},{25,17},{2,10},{10... | collective-permute-start | bytes 1966088 | tf_op jit(solution)/shard_map/ppermute | solution.py:331
  52.5 30.2 %collective-permute-start.14 = (bf16[2,32,5120]{2,1,0:T(8,128)(2,1)}, bf16[2,32,5120]{2,1,0:T(8,128)(2,1)}, u32[]{:S(2)}, u32[]{:S(2)}) collective-permute-start(bf16[2,32,5120]{2,1,0:T(8,128)(2,1)} %after.19), channel_id=1, source_target_pairs={{0,16},{8,24},{16,0},{24,8},{1,17},{9,25},{17,1},{25,9},{2,18},{10... | collective-permute-start | bytes 1966088 | tf_op jit(solution)/shard_map/ppermute | solution.py:331
  53.0 29.7 %collective-permute-start.15 = (bf16[2,32,5120]{2,1,0:T(8,128)(2,1)}, bf16[2,32,5120]{2,1,0:T(8,128)(2,1)}, u32[]{:S(2)}, u32[]{:S(2)}) collective-permute-start(bf16[2,32,5120]{2,1,0:T(8,128)(2,1)} %after.19), channel_id=1, source_target_pairs={{0,24},{8,16},{16,8},{24,0},{1,25},{9,17},{17,9},{25,1},{2,26},{10... | collective-permute-start | bytes 1966088 | tf_op jit(solution)/shard_map/ppermute | solution.py:331
  55.4 14.1 %copy-start.22 = (bf16[1,128,1024]{2,1,0:T(8,128)(2,1)S(1)}, bf16[1,128,1024]{2,1,0:T(8,128)(2,1)}, u32[]{:S(2)}) copy-start(bf16[1,128,1024]{2,1,0:T(8,128)(2,1)} %after.18) | copy-start | bytes 786436
  55.5 14.1 %collective-permute-start.11 = (bf16[1,128,1024]{2,1,0:T(8,128)(2,1)}, bf16[1,128,1024]{2,1,0:T(8,128)(2,1)S(1)}, u32[]{:S(2)}, u32[]{:S(2)}) collective-permute-start(bf16[1,128,1024]{2,1,0:T(8,128)(2,1)} %after.18), channel_id=1, source_target_pairs={{0,4},{2,6},{4,0},{6,2},{1,5},{3,7},{5,1},{7,3},{8,12},{10,14},{12... | collective-permute-start | bytes 786440 | tf_op jit(solution)/shard_map/ppermute | solution.py:331
  69.4 13.3 %copy-start.9 = (bf16[2,32,5120]{2,1,0:T(8,128)(2,1)S(1)}, bf16[2,32,5120]{2,1,0:T(8,128)(2,1)}, u32[]{:S(2)}) copy-start(bf16[2,32,5120]{2,1,0:T(8,128)(2,1)} %after.19) | copy-start | bytes 1966084
  69.4 17.6 %collective-permute-start.10 = (bf16[4,4,40,768]{3,2,1,0:T(8,128)(2,1)S(1)}, bf16[4,4,40,768]{3,2,1,0:T(8,128)(2,1)S(1)}, u32[]{:S(2)}, u32[]{:S(2)}) collective-permute-start(bf16[4,4,40,768]{3,2,1,0:T(8,128)(2,1)S(1)} %bitcast.300), channel_id=1, source_target_pairs={{0,1},{1,0},{2,3},{3,2},{4,5},{5,4},{6,7},{7,6},{8,9},{9,8},{10,11... | collective-permute-start | bytes 2949128 | tf_op jit(solution)/shard_map/ppermute | solution.py:331
  69.6 16.3 %collective-permute-start.12 = (bf16[2,128,1024]{2,1,0:T(8,128)(2,1)S(1)}, bf16[2,128,1024]{2,1,0:T(8,128)(2,1)S(1)}, u32[]{:S(2)}, u32[]{:S(2)}) collective-permute-start(bf16[2,128,1024]{2,1,0:T(8,128)(2,1)S(1)} %get-tuple-element.136), channel_id=1, source_target_pairs={{0,2},{2,0},{4,6},{6,4},{1,3},{3,1},{5,7},{7,5},{8,10},{10,8},{12,... | collective-permute-start | bytes 1572872 | tf_op jit(solution)/shard_map/ppermute | solution.py:331
  88.6 31.5 %collective-permute-start.16 = (bf16[8,32,5120]{2,1,0:T(8,128)(2,1)}, bf16[8,32,5120]{2,1,0:T(8,128)(2,1)}, u32[]{:S(2)}, u32[]{:S(2)}) collective-permute-start(bf16[8,32,5120]{2,1,0:T(8,128)(2,1)} %after.21.refs_1_.refs_0_.refs_8_), channel_id=1, source_target_pairs={{0,1},{1,0},{2,3},{3,2},{4,5},{5,4},{6,7},{7,6},{8,9},{9,8},{10,11... | collective-permute-start | bytes 7864328 | tf_op jit(solution)/shard_map/ppermute | solution.py:331
  88.7 59.6 %collective-permute-start.17 = (bf16[8,32,5120]{2,1,0:T(8,128)(2,1)}, bf16[8,32,5120]{2,1,0:T(8,128)(2,1)}, u32[]{:S(2)}, u32[]{:S(2)}) collective-permute-start(bf16[8,32,5120]{2,1,0:T(8,128)(2,1)} %after.21.refs_1_.refs_0_.refs_8_), channel_id=1, source_target_pairs={{0,2},{2,0},{4,6},{6,4},{1,3},{3,1},{5,7},{7,5},{8,10},{10,8},{12,... | collective-permute-start | bytes 7864328 | tf_op jit(solution)/shard_map/ppermute | solution.py:331
  90.3 47.8 %collective-permute-start.18 = (bf16[4,128,1024]{2,1,0:T(8,128)(2,1)S(1)}, bf16[4,128,1024]{2,1,0:T(8,128)(2,1)S(1)}, u32[]{:S(2)}, u32[]{:S(2)}) collective-permute-start(bf16[4,128,1024]{2,1,0:T(8,128)(2,1)S(1)} %copy-done.1), channel_id=1, source_target_pairs={{0,8},{8,0},{16,24},{24,16},{1,9},{9,1},{17,25},{25,17},{2,10},{10... | collective-permute-start | bytes 3145736 | tf_op jit(solution)/shard_map/ppermute | solution.py:331
  91.9 47.6 %collective-permute-start.19 = (bf16[4,128,1024]{2,1,0:T(8,128)(2,1)S(1)}, bf16[4,128,1024]{2,1,0:T(8,128)(2,1)}, u32[]{:S(2)}, u32[]{:S(2)}) collective-permute-start(bf16[4,128,1024]{2,1,0:T(8,128)(2,1)S(1)} %copy-done.1), channel_id=1, source_target_pairs={{0,16},{8,24},{16,0},{24,8},{1,17},{9,25},{17,1},{25,9},{2,18},{10... | collective-permute-start | bytes 3145736 | tf_op jit(solution)/shard_map/ppermute | solution.py:331
  92.4 47.1 %collective-permute-start.20 = (bf16[4,128,1024]{2,1,0:T(8,128)(2,1)S(1)}, bf16[4,128,1024]{2,1,0:T(8,128)(2,1)}, u32[]{:S(2)}, u32[]{:S(2)}) collective-permute-start(bf16[4,128,1024]{2,1,0:T(8,128)(2,1)S(1)} %copy-done.1), channel_id=1, source_target_pairs={{0,24},{8,16},{16,8},{24,0},{1,25},{9,17},{17,9},{25,1},{2,26},{10... | collective-permute-start | bytes 3145736 | tf_op jit(solution)/shard_map/ppermute | solution.py:331
  120.1 11.8 %copy-start.33 = (bf16[2048,128]{1,0:T(8,128)(2,1)S(1)}, bf16[2048,128]{1,0:T(8,128)(2,1)}, u32[]{:S(2)}) copy-start(bf16[2048,128]{1,0:T(8,128)(2,1)} %get-tuple-element.68) | copy-start | bytes 1572868
  134.0 17.5 %all-to-all-start = ((bf16[4,512,256]{2,1,0:T(8,128)(2,1)}), bf16[4,512,256]{2,1,0:T(8,128)(2,1)S(1)}, u32[]{:S(2)}, u32[]{:S(2)}) async-start(bf16[4,512,256]{2,1,0:T(8,128)(2,1)} %bitcast.37), calls=%async_computation | async-start | bytes 2097152 | tf_op jit(solution)/shard_map/all_to_all | solution.py:1064
  138.1 15.5 %copy-start.43 = (s32[16]{0:T(128)S(1)}, s32[16]{0:T(128)}, u32[]{:S(2)}) copy-start(s32[16]{0:T(128)} %constant.105.clone) | copy-start | bytes 196
  138.1 13.4 %copy-start.17 = (bf16[4,128,1024]{2,1,0:T(8,128)(2,1)}, bf16[4,128,1024]{2,1,0:T(8,128)(2,1)S(1)}, u32[]{:S(2)}) copy-start(bf16[4,128,1024]{2,1,0:T(8,128)(2,1)S(1)} %collective-permute-done.18.refs_2_) | copy-start | bytes 3145732
  152.5 9.0 %collective-permute-start.21 = (bf16[8,32,5120]{2,1,0:T(8,128)(2,1)}, bf16[8,32,5120]{2,1,0:T(8,128)(2,1)}, u32[]{:S(2)}, u32[]{:S(2)}) collective-permute-start(bf16[8,32,5120]{2,1,0:T(8,128)(2,1)} %get-tuple-element.71.refs_1_.refs_9_), channel_id=1, source_target_pairs={{0,1},{1,0},{2,3},{3,2},{4,5},{5,4},{6,7},{7,6},{8,9},{9,8},{10,11... | collective-permute-start | bytes 7864328 | tf_op jit(solution)/shard_map/ppermute | solution.py:331
  152.5 14.7 %collective-permute-start.22 = (bf16[4,128,1024]{2,1,0:T(8,128)(2,1)}, bf16[4,128,1024]{2,1,0:T(8,128)(2,1)S(1)}, u32[]{:S(2)}, u32[]{:S(2)}) collective-permute-start(bf16[4,128,1024]{2,1,0:T(8,128)(2,1)} %get-tuple-element.74.refs_0_), channel_id=1, source_target_pairs={{0,1},{1,0},{2,3},{3,2},{4,5},{5,4},{6,7},{7,6},{8,9},{9,8},{10,11... | collective-permute-start | bytes 3145736 | tf_op jit(solution)/shard_map/ppermute | solution.py:331
  153.0 14.2 %collective-permute-start.23 = (bf16[4,128,1024]{2,1,0:T(8,128)(2,1)}, bf16[4,128,1024]{2,1,0:T(8,128)(2,1)S(1)}, u32[]{:S(2)}, u32[]{:S(2)}) collective-permute-start(bf16[4,128,1024]{2,1,0:T(8,128)(2,1)} %get-tuple-element.75.refs_1_), channel_id=1, source_target_pairs={{0,1},{1,0},{2,3},{3,2},{4,5},{5,4},{6,7},{7,6},{8,9},{9,8},{10,11... | collective-permute-start | bytes 3145736 | tf_op jit(solution)/shard_map/ppermute | solution.py:331
  153.0 14.3 %collective-permute-start.24 = (bf16[4,128,1024]{2,1,0:T(8,128)(2,1)}, bf16[4,128,1024]{2,1,0:T(8,128)(2,1)S(1)}, u32[]{:S(2)}, u32[]{:S(2)}) collective-permute-start(bf16[4,128,1024]{2,1,0:T(8,128)(2,1)} %get-tuple-element.76.refs_2_), channel_id=1, source_target_pairs={{0,1},{1,0},{2,3},{3,2},{4,5},{5,4},{6,7},{7,6},{8,9},{9,8},{10,11... | collective-permute-start | bytes 3145736 | tf_op jit(solution)/shard_map/ppermute | solution.py:331
  153.5 13.8 %collective-permute-start.25 = (bf16[4,128,1024]{2,1,0:T(8,128)(2,1)}, bf16[4,128,1024]{2,1,0:T(8,128)(2,1)}, u32[]{:S(2)}, u32[]{:S(2)}) collective-permute-start(bf16[4,128,1024]{2,1,0:T(8,128)(2,1)} %get-tuple-element.77.refs_3_), channel_id=1, source_target_pairs={{0,1},{1,0},{2,3},{3,2},{4,5},{5,4},{6,7},{7,6},{8,9},{9,8},{10,11... | collective-permute-start | bytes 3145736 | tf_op jit(solution)/shard_map/ppermute | solution.py:331
  210.0 14.9 %collective-permute-start.26 = (bf16[16,128,1024]{2,1,0:T(8,128)(2,1)}, bf16[16,128,1024]{2,1,0:T(8,128)(2,1)}, u32[]{:S(2)}, u32[]{:S(2)}) collective-permute-start(bf16[16,128,1024]{2,1,0:T(8,128)(2,1)} %get-tuple-element.84), channel_id=1, source_target_pairs={{0,1},{1,0},{2,3},{3,2},{4,5},{5,4},{6,7},{7,6},{8,9},{9,8},{10,11... | collective-permute-start | bytes 12582920 | tf_op jit(solution)/shard_map/ppermute | solution.py:331
  210.2 14.7 %collective-permute-start.28 = (bf16[16,32,4096]{2,1,0:T(8,128)(2,1)}, bf16[16,32,4096]{2,1,0:T(8,128)(2,1)}, u32[]{:S(2)}, u32[]{:S(2)}) collective-permute-start(bf16[16,32,4096]{2,1,0:T(8,128)(2,1)} %get-tuple-element.88), channel_id=1, source_target_pairs={{0,1},{1,0},{2,3},{3,2},{4,5},{5,4},{6,7},{7,6},{8,9},{9,8},{10,11... | collective-permute-start | bytes 12582920 | tf_op jit(solution)/shard_map/ppermute | solution.py:331
  220.2 4.7 %collective-permute-start.27 = (bf16[16,32,1024]{2,1,0:T(8,128)(2,1)}, bf16[16,32,1024]{2,1,0:T(8,128)(2,1)S(1)}, u32[]{:S(2)}, u32[]{:S(2)}) collective-permute-start(bf16[16,32,1024]{2,1,0:T(8,128)(2,1)} %get-tuple-element.86), channel_id=1, source_target_pairs={{0,1},{1,0},{2,3},{3,2},{4,5},{5,4},{6,7},{7,6},{8,9},{9,8},{10,11... | collective-permute-start | bytes 3145736 | tf_op jit(solution)/shard_map/ppermute | solution.py:331
  220.4 18.1 %all-to-all-start.1 = ((bf16[4,512,256]{2,1,0:T(8,128)(2,1)}), bf16[4,512,256]{2,1,0:T(8,128)(2,1)S(1)}, u32[]{:S(2)}, u32[]{:S(2)}) async-start(bf16[4,512,256]{2,1,0:T(8,128)(2,1)} %get-tuple-element.81), calls=%async_computation.1 | async-start | bytes 2097152 | tf_op jit(solution)/shard_map/all_to_all | solution.py:1064
  239.5 52.7 %collective-permute-start.32 = (bf16[8,32,4096]{2,1,0:T(8,128)(2,1)}, bf16[8,32,4096]{2,1,0:T(8,128)(2,1)S(1)}, u32[]{:S(2)}, u32[]{:S(2)}) collective-permute-start(bf16[8,32,4096]{2,1,0:T(8,128)(2,1)} %get-tuple-element.105), channel_id=1, source_target_pairs={{0,2},{2,0},{4,6},{6,4},{1,3},{3,1},{5,7},{7,5},{8,10},{10,8},{12,... | collective-permute-start | bytes 6291464 | tf_op jit(solution)/shard_map/ppermute | solution.py:331
  242.4 57.5 %collective-permute-start.29 = (bf16[4,160,1024]{2,1,0:T(8,128)(2,1)}, bf16[4,160,1024]{2,1,0:T(8,128)(2,1)}, u32[]{:S(2)}, u32[]{:S(2)}) collective-permute-start(bf16[4,160,1024]{2,1,0:T(8,128)(2,1)} %get-tuple-element.102), channel_id=1, source_target_pairs={{0,8},{8,0},{16,24},{24,16},{1,9},{9,1},{17,25},{25,17},{2,10},{10... | collective-permute-start | bytes 3932168 | tf_op jit(solution)/shard_map/ppermute | solution.py:331
  243.9 57.3 %collective-permute-start.30 = (bf16[4,160,1024]{2,1,0:T(8,128)(2,1)}, bf16[4,160,1024]{2,1,0:T(8,128)(2,1)}, u32[]{:S(2)}, u32[]{:S(2)}) collective-permute-start(bf16[4,160,1024]{2,1,0:T(8,128)(2,1)} %get-tuple-element.103), channel_id=1, source_target_pairs={{0,16},{8,24},{16,0},{24,8},{1,17},{9,25},{17,1},{25,9},{2,18},{10... | collective-permute-start | bytes 3932168 | tf_op jit(solution)/shard_map/ppermute | solution.py:331
  244.6 58.9 %collective-permute-start.31 = (bf16[4,160,1024]{2,1,0:T(8,128)(2,1)}, bf16[4,160,1024]{2,1,0:T(8,128)(2,1)}, u32[]{:S(2)}, u32[]{:S(2)}) collective-permute-start(bf16[4,160,1024]{2,1,0:T(8,128)(2,1)} %get-tuple-element.104), channel_id=1, source_target_pairs={{0,24},{8,16},{16,8},{24,0},{1,25},{9,17},{17,9},{25,1},{2,26},{10... | collective-permute-start | bytes 3932168 | tf_op jit(solution)/shard_map/ppermute | solution.py:331
  297.8 34.8 %collective-permute-start.34 = (bf16[2,32,4096]{2,1,0:T(8,128)(2,1)}, bf16[2,32,4096]{2,1,0:T(8,128)(2,1)}, u32[]{:S(2)}, u32[]{:S(2)}) collective-permute-start(bf16[2,32,4096]{2,1,0:T(8,128)(2,1)} %get-tuple-element.130), channel_id=1, source_target_pairs={{0,8},{8,0},{16,24},{24,16},{1,9},{9,1},{17,25},{25,17},{2,10},{10... | collective-permute-start | bytes 1572872 | tf_op jit(solution)/shard_map/ppermute | solution.py:331
  299.2 33.4 %collective-permute-start.35 = (bf16[2,32,4096]{2,1,0:T(8,128)(2,1)}, bf16[2,32,4096]{2,1,0:T(8,128)(2,1)}, u32[]{:S(2)}, u32[]{:S(2)}) collective-permute-start(bf16[2,32,4096]{2,1,0:T(8,128)(2,1)} %get-tuple-element.129), channel_id=1, source_target_pairs={{0,16},{8,24},{16,0},{24,8},{1,17},{9,25},{17,1},{25,9},{2,18},{10... | collective-permute-start | bytes 1572872 | tf_op jit(solution)/shard_map/ppermute | solution.py:331
  299.9 32.7 %collective-permute-start.36 = (bf16[2,32,4096]{2,1,0:T(8,128)(2,1)}, bf16[2,32,4096]{2,1,0:T(8,128)(2,1)}, u32[]{:S(2)}, u32[]{:S(2)}) collective-permute-start(bf16[2,32,4096]{2,1,0:T(8,128)(2,1)} %get-tuple-element.128), channel_id=1, source_target_pairs={{0,24},{8,16},{16,8},{24,0},{1,25},{9,17},{17,9},{25,1},{2,26},{10... | collective-permute-start | bytes 1572872 | tf_op jit(solution)/shard_map/ppermute | solution.py:331
  309.7 26.4 %collective-permute-start.37 = (bf16[2,160,1024]{2,1,0:T(8,128)(2,1)}, bf16[2,160,1024]{2,1,0:T(8,128)(2,1)}, u32[]{:S(2)}, u32[]{:S(2)}) collective-permute-start(bf16[2,160,1024]{2,1,0:T(8,128)(2,1)} %fusion.17), channel_id=1, source_target_pairs={{0,2},{2,0},{4,6},{6,4},{1,3},{3,1},{5,7},{7,5},{8,10},{10,8},{12,... | collective-permute-start | bytes 1966088 | tf_op jit(solution)/shard_map/ppermute | solution.py:331
  327.7 8.4 %collective-permute-start.33 = (bf16[4,4,40,768]{3,2,1,0:T(8,128)(2,1)}, bf16[4,4,40,768]{3,2,1,0:T(8,128)(2,1)}, u32[]{:S(2)}, u32[]{:S(2)}) collective-permute-start(bf16[4,4,40,768]{3,2,1,0:T(8,128)(2,1)} %fusion.12), channel_id=1, source_target_pairs={{0,1},{1,0},{2,3},{3,2},{4,5},{5,4},{6,7},{7,6},{8,9},{9,8},{10,11... | collective-permute-start | bytes 2949128 | tf_op jit(solution)/shard_map/ppermute | solution.py:331
  327.7 59.3 %all-to-all-start.2 = ((bf16[4,512,1024]{2,1,0:T(8,128)(2,1)}), bf16[4,512,1024]{2,1,0:T(8,128)(2,1)}, u32[]{:S(2)}, u32[]{:S(2)}) async-start(bf16[4,512,1024]{2,1,0:T(8,128)(2,1)} %bitcast.297), calls=%async_computation.2 | async-start | bytes 8388608 | tf_op jit(solution)/shard_map/all_to_all | solution.py:1064
  340.2 13.8 %collective-permute-start.38 = (bf16[2,4,40,768]{3,2,1,0:T(8,128)(2,1)}, bf16[2,4,40,768]{3,2,1,0:T(8,128)(2,1)S(1)}, u32[]{:S(2)}, u32[]{:S(2)}) collective-permute-start(bf16[2,4,40,768]{3,2,1,0:T(8,128)(2,1)} %fusion.20), channel_id=1, source_target_pairs={{0,2},{2,0},{4,6},{6,4},{1,3},{3,1},{5,7},{7,5},{8,10},{10,8},{12,... | collective-permute-start | bytes 1474568 | tf_op jit(solution)/shard_map/ppermute | solution.py:331
  344.3 9.7 %copy-start.8 = (f32[4,4,40,768]{3,2,1,0:T(8,128)S(1)}, f32[4,4,40,768]{3,2,1,0:T(8,128)}, u32[]{:S(2)}) copy-start(f32[4,4,40,768]{3,2,1,0:T(8,128)} %copy-done.7) | copy-start | bytes 5898244
  344.3 13.2 %copy-start.10 = (f32[512,1024]{1,0:T(8,128)S(1)}, f32[512,1024]{1,0:T(8,128)}, u32[]{:S(2)}) copy-start(f32[512,1024]{1,0:T(8,128)} %after.27) | copy-start | bytes 6291460
  354.1 14.6 %collective-permute-start.39 = (bf16[1,4,40,768]{3,2,1,0:T(8,128)(2,1)S(1)}, bf16[1,4,40,768]{3,2,1,0:T(8,128)(2,1)S(1)}, u32[]{:S(2)}, u32[]{:S(2)}) collective-permute-start(bf16[1,4,40,768]{3,2,1,0:T(8,128)(2,1)S(1)} %fusion.27), channel_id=1, source_target_pairs={{0,4},{2,6},{4,0},{6,2},{1,5},{3,7},{5,1},{7,3},{8,12},{10,14},{12... | collective-permute-start | bytes 737288 | tf_op jit(solution)/shard_map/ppermute | solution.py:331
  369.4 28.6 %collective-permute-start.43 = (bf16[160,1024]{1,0:T(8,128)(2,1)}, bf16[160,1024]{1,0:T(8,128)(2,1)S(1)}, u32[]{:S(2)}, u32[]{:S(2)}) collective-permute-start(bf16[160,1024]{1,0:T(8,128)(2,1)} %get-tuple-element.116), channel_id=1, source_target_pairs={{0,4},{2,6},{4,0},{6,2},{1,5},{3,7},{5,1},{7,3},{8,12},{10,14},{12... | collective-permute-start | bytes 983048 | tf_op jit(solution)/shard_map/ppermute | solution.py:331
  369.4 28.6 %collective-permute-start.44 = (bf16[32,4096]{1,0:T(8,128)(2,1)}, bf16[32,4096]{1,0:T(8,128)(2,1)S(1)}, u32[]{:S(2)}, u32[]{:S(2)}) collective-permute-start(bf16[32,4096]{1,0:T(8,128)(2,1)} %get-tuple-element.117), channel_id=1, source_target_pairs={{0,4},{2,6},{4,0},{6,2},{1,5},{3,7},{5,1},{7,3},{8,12},{10,14},{12... | collective-permute-start | bytes 786440 | tf_op jit(solution)/shard_map/ppermute | solution.py:331
  372.4 10.2 %collective-permute-start.40 = (bf16[1,40,768]{2,1,0:T(8,128)(2,1)S(1)}, bf16[1,40,768]{2,1,0:T(8,128)(2,1)S(1)}, u32[]{:S(2)}, u32[]{:S(2)}) collective-permute-start(bf16[1,40,768]{2,1,0:T(8,128)(2,1)S(1)} %get-tuple-element.139), channel_id=1, source_target_pairs={{0,8},{8,0},{16,24},{24,16},{1,9},{9,1},{17,25},{25,17},{2,10},{10... | collective-permute-start | bytes 184328 | tf_op jit(solution)/shard_map/ppermute | solution.py:331
  373.7 8.8 %collective-permute-start.41 = (bf16[1,40,768]{2,1,0:T(8,128)(2,1)S(1)}, bf16[1,40,768]{2,1,0:T(8,128)(2,1)S(1)}, u32[]{:S(2)}, u32[]{:S(2)}) collective-permute-start(bf16[1,40,768]{2,1,0:T(8,128)(2,1)S(1)} %get-tuple-element.138), channel_id=1, source_target_pairs={{0,16},{8,24},{16,0},{24,8},{1,17},{9,25},{17,1},{25,9},{2,18},{10... | collective-permute-start | bytes 184328 | tf_op jit(solution)/shard_map/ppermute | solution.py:331
  375.2 9.2 %collective-permute-start.42 = (bf16[1,40,768]{2,1,0:T(8,128)(2,1)S(1)}, bf16[1,40,768]{2,1,0:T(8,128)(2,1)S(1)}, u32[]{:S(2)}, u32[]{:S(2)}) collective-permute-start(bf16[1,40,768]{2,1,0:T(8,128)(2,1)S(1)} %get-tuple-element.137), channel_id=1, source_target_pairs={{0,24},{8,16},{16,8},{24,0},{1,25},{9,17},{17,9},{25,1},{2,26},{10... | collective-permute-start | bytes 184328 | tf_op jit(solution)/shard_map/ppermute | solution.py:331
  (29 other events, 58.0 us)

commit v4 on v3

--- a/solution.py
+++ b/solution.py
@@ -699,7 +699,7 @@
             refs[groups + group][...] = both(up_keep, up_came)
 
 
-def meet(down_keep, down_came, output_keep, output_came, up_keep, up_came, groups, up_groups, per=2):
+def meet(down_keep, down_came, output_keep, output_came, up_keep, up_came, groups, up_groups, per=4):
     chips, span, width = down_keep.shape
     owned, inner = up_keep.shape[1:]
     block = lambda rows, columns: pl.BlockSpec((per, rows, columns), lambda s: (s, 0, 0))

time: 407 us -> 407 us (level)
  no operation moved by 1% of the time
where the time goes in v4:
time: 407 us; the launch traced here: 403 us
  Pallas kernels  161 us (40%)
  waiting for transfers between devices  95.3 us (23%)
  starting transfers between devices  64.8 us (16%)
  local copies, waits for them, and re-layouts  42.7 us (10%)
  other arithmetic  37.5 us (9%)
    ppermute x45, waiting for transfers between devices, swap(): lax.ppermute(value, axis, [(i, i ^ bit) for i in range(lax.axis_size(axis...  90.1 us
    ppermute x45, starting transfers between devices, swap(): lax.ppermute(value, axis, [(i, i ^ bit) for i in range(lax.axis_size(axis...  52.2 us
    pallas_call x2, Pallas kernels, attend_backward(): pl.pallas_call(backward_kernel, grid=(2,), in_specs=[pl.BlockSpec(memory_...  46.2 us
    pallas_call x1, Pallas kernels, feed_forward(): pl.pallas_call(functools.partial(feed_forward_kernel, groups, per), grid_...  41 us
    pallas_call x2, Pallas kernels, attend_forward(): pl.pallas_call(forward_kernel, grid=(2,), in_specs=[pl.BlockSpec(memory_s...  23.6 us
    unnamed x123, local copies, waits for them, and re-layouts  18.5 us
    all_to_all x3, starting transfers between devices, exchange(): lax.all_to_all(value.reshape(ways, local, -1), 'seq', split_axis=0, conca...  12.6 us
    pallas_call x1, Pallas kernels, input_grad(): pl.pallas_call(input_grad_kernel, grid=(length // rows,), in_specs=[block...  12.6 us
  transfers between devices with their start and end apart: 48, of which 17 were waited for; matrix products, arithmetic and copies ran while one was open for 14% of the time, Pallas kernels for 30%

profile of v4, /device:TPU:0, one launch (start us, length us, event | category | flops | bytes accessed | tf_op | source)
XLA Modules:
  0.0 403.2 jit_solution(6194224866232082674)
XLA Ops:
  0.7 1.7 copy.194
  2.4 2.9 collective-permute-start
  5.4 1.5 collective-permute-start.1
  8.7 2.6 collective-permute-start.4
  13.5 12.0 %collective-permute-done.4 = bf16[1,32,5120]{2,1,0:T(8,128)(2,1)S(1)} collective-permute-done((bf16[1,32,5120]{2,1,0:T(8,128)(2,1)S(1)}, bf16[1,32,5120]{2,1,0:T(8,128)(2,1)S(1)}, u32[]{:S(2)}, u32[]{:S(2)}) %collective-permute-start.4) | collective-permute-done | bytes 327712 | tf_op jit(solution)/shard_map/ppermute | solution.py:331
  28.4 2.5 collective-permute-start.7
  34.5 1.4 collective-permute-start.3
  36.6 2.6 collective-permute-start.8
  39.2 9.4 %collective-permute-done.8 = bf16[1,4,40,768]{3,2,1,0:T(8,128)(2,1)S(1)} collective-permute-done((bf16[1,4,40,768]{3,2,1,0:T(8,128)(2,1)}, bf16[1,4,40,768]{3,2,1,0:T(8,128)(2,1)S(1)}, u32[]{:S(2)}, u32[]{:S(2)}) %collective-permute-start.8) | collective-permute-done | bytes 245792 | tf_op jit(solution)/shard_map/ppermute | solution.py:331
  48.6 1.8 maximum_bitcast_fusion.1.refs_0_
  53.0 2.4 collective-permute-start.15
  55.5 3.3 collective-permute-start.11
  58.7 10.5 %collective-permute-done.9 = bf16[2,4,40,768]{3,2,1,0:T(8,128)(2,1)S(1)} collective-permute-done((bf16[2,4,40,768]{3,2,1,0:T(8,128)(2,1)}, bf16[2,4,40,768]{3,2,1,0:T(8,128)(2,1)S(1)}, u32[]{:S(2)}, u32[]{:S(2)}) %collective-permute-start.9) | collective-permute-done | bytes 491552 | tf_op jit(solution)/shard_map/ppermute | solution.py:331
  69.6 3.1 collective-permute-start.12
  72.7 10.0 %collective-permute-done.14 = bf16[2,32,5120]{2,1,0:T(8,128)(2,1)} collective-permute-done((bf16[2,32,5120]{2,1,0:T(8,128)(2,1)}, bf16[2,32,5120]{2,1,0:T(8,128)(2,1)}, u32[]{:S(2)}, u32[]{:S(2)}) %collective-permute-start.14) | collective-permute-done | bytes 655392 | tf_op jit(solution)/shard_map/ppermute | solution.py:331
  82.7 3.2 pad_maximum_fusion.refs_1_.refs_0_
  87.2 1.4 copy.81
  90.3 1.6 collective-permute-start.18
  92.4 1.4 collective-permute-start.20
  96.9 11.4 %project.1 = (bf16[2048,768]{1,0:T(8,128)(2,1)}, bf16[2048,1024]{1,0:T(8,128)(2,1)}, bf16[2048,1024]{1,0:T(8,128)(2,1)}, bf16[1024,768]{1,0:T(8,128)(2,1)}) custom-call(s32[2]{0:T(128)} %pad_add_fusion.1.table_ref, bf16[512,1024]{1,0:T(8,128)(2,1)} %bitcast.278, bf16[512,1024]{1,0:T(8,128)(2,1)} %copy-done.13, bf16[512,1024]{1,0:T(8,128)(2,1)} %copy-done.14, ...), custom_call_target="tpu_custom_call" | custom-call | flops 900000000 | tf_op jit(solution)/shard_map/project/pallas_call | solution.py:478
  108.3 11.7 %attend_forward.2 = (bf16[2048,128]{1,0:T(8,128)(2,1)}, f32[128,2048]{1,0:T(8,128)}, f32[16,2048]{1,0:T(8,128)}) custom-call(f32[2]{0:T(128)} %get-tuple-element.160.slope_ref, bf16[2048,768]{1,0:T(8,128)(2,1)} %get-tuple-element.67.q_ref.k_ref.v_ref, bf16[2048,768]{1,0:T(8,128)(2,1)} %get-tuple-element.67.q_ref.k_ref.v_ref, ...), custom_call_target="tpu_custom_call" | custom-call | flops 1050000000 | tf_op jit(solution)/shard_map/attend_forward/pallas_call | solution.py:82
  120.1 11.8 %attend_forward.3 = (bf16[2048,128]{1,0:T(8,128)(2,1)}, f32[128,2048]{1,0:T(8,128)}, f32[16,2048]{1,0:T(8,128)}) custom-call(f32[2]{0:T(128)} %get-tuple-element.161.slope_ref, bf16[2048,768]{1,0:T(8,128)(2,1)} %get-tuple-element.67.q_ref.k_ref.v_ref, bf16[2048,768]{1,0:T(8,128)(2,1)} %get-tuple-element.67.q_ref.k_ref.v_ref, ...), custom_call_target="tpu_custom_call" | custom-call | flops 1050000000 | tf_op jit(solution)/shard_map/attend_forward/pallas_call | solution.py:82
  131.9 2.1 pad_maximum_fusion.4
  134.0 4.0 %all-to-all-start = ((bf16[4,512,256]{2,1,0:T(8,128)(2,1)}), bf16[4,512,256]{2,1,0:T(8,128)(2,1)S(1)}, u32[]{:S(2)}, u32[]{:S(2)}) async-start(bf16[4,512,256]{2,1,0:T(8,128)(2,1)} %bitcast.37), calls=%async_computation | async-start | bytes 2097152 | tf_op jit(solution)/shard_map/all_to_all | solution.py:1064
  138.1 1.4 collective-permute-done.19.refs_3_
  139.5 8.8 %collective-permute-done.17.refs_0_ = bf16[8,32,5120]{2,1,0:T(8,128)(2,1)} collective-permute-done((bf16[8,32,5120]{2,1,0:T(8,128)(2,1)}, bf16[8,32,5120]{2,1,0:T(8,128)(2,1)}, u32[]{:S(2)}, u32[]{:S(2)}) %collective-permute-start.17) | collective-permute-done | bytes 2621472 | tf_op jit(solution)/shard_map/ppermute | solution.py:331
  148.3 3.2 all-to-all-done.refs_5_.context_ref
  156.8 4.7 %collective-permute-done.21.refs_3_.refs_11_ = bf16[8,32,5120]{2,1,0:T(8,128)(2,1)} collective-permute-done((bf16[8,32,5120]{2,1,0:T(8,128)(2,1)}, bf16[8,32,5120]{2,1,0:T(8,128)(2,1)}, u32[]{:S(2)}, u32[]{:S(2)}) %collective-permute-start.21) | collective-permute-done | bytes 2621472 | tf_op jit(solution)/shard_map/ppermute | solution.py:331
  161.5 5.8 %project_output.1 = (f32[512,1024]{1,0:T(8,128)}, bf16[512,1024]{1,0:T(8,128)(2,1)}, bf16[1024,1024]{1,0:T(8,128)(2,1)}) custom-call(s32[33]{0:T(128)} %pad_add_fusion.table_ref, bf16[4,512,256]{2,1,0:T(8,128)(2,1)} %copy-done.6, bf16[512,1024]{1,0:T(8,128)(2,1)} %bitcast.279, f32[1,1024]{1,0:T(1,128)} %reshape.212.bias_ref, f32[1,1024]{1,0:T(1,128)} %reshape.213.gain_ref, ...), custom_call_target="tpu_custom_call" | custom-call | flops 500000000 | tf_op jit(solution)/shard_map/project_output/pallas_call | solution.py:594
  168.9 41.0 %feed_forward.1 = (f32[512,1024]{1,0:T(8,128)}, f32[512,1024]{1,0:T(8,128)}, bf16[16,128,1024]{2,1,0:T(8,128)(2,1)}, bf16[16,128,1024]{2,1,0:T(8,128)(2,1)}, bf1...) custom-call(s32[33]{0:T(128)} %pad_add_fusion.table_ref, ...), custom_call_target="tpu_custom_call" | custom-call | flops 4499999744 | tf_op jit(solution)/shard_map/feed_forward/pallas_call | solution.py:282
  210.5 9.7 %residual_grad.1 = (f32[512,1024]{1,0:T(8,128)}, bf16[4,512,256]{2,1,0:T(8,128)(2,1)}, bf16[16,32,1024]{2,1,0:T(8,128)(2,1)}, bf16[16,32,1024]{2,1,0:T(8,128)(2,1)}, f32[8,1024]{1,0:T(8,128)}) custom-call(s32[33]{0:T(128)} %pad_add_fusion.table_ref, f32[512,1024]{1,0:T(8,128)} %get-tuple-element.79.grad_ref, f32[512,1024]{1,0:T(8,128)} %get-tuple-element.72.residual_ref, ...), custom_call_target="tpu_custom_call" | custom-call | flops 700000000 | tf_op jit(solution)/shard_map/residual_grad/pallas_call | solution.py:658
  220.4 3.7 all-to-all-start.1
  225.9 10.7 %meet.1 = (bf16[4,160,1024]{2,1,0:T(8,128)(2,1)}, bf16[4,160,1024]{2,1,0:T(8,128)(2,1)}, bf16[4,160,1024]{2,1,0:T(8,128)(2,1)}, bf16[4,160,1024]{2,1,0:T(8,128)(...) custom-call(bf16[16,128,1024]{2,1,0:T(8,128)(2,1)} %get-tuple-element.83.down_keep, ...), custom_call_target="tpu_custom_call" | custom-call | flops 900000000 | tf_op jit(solution)/shard_map/meet/pallas_call | solution.py:710
  236.6 2.0 all-to-all-done.1
  239.5 1.7 collective-permute-start.32
  242.4 1.5 collective-permute-start.29
  244.5 1.5 collective-permute-start.31
  246.0 23.1 %attend_backward.2.refs_0_.low_ref = bf16[2048,384]{1,0:T(8,128)(2,1)} custom-call(f32[2]{0:T(128)} %get-tuple-element.160.slope_ref, bf16[2048,768]{1,0:T(8,128)(2,1)} %get-tuple-element.67.q_ref.k_ref.v_ref, bf16[2048,768]{1,0:T(8,128)(2,1)} %get-tuple-element.67.q_ref.k_ref.v_ref, bf16[2048,768]{1,0:T(8,128)(2,1)} %get-tuple-element.67.q_ref.k_ref.v_ref, ...), custom_call_target="tpu_custom_call" | custom-call | flops 2200000000 | tf_op jit(solution)/shard_map/attend_backward/pallas_call | solution.py:170
  269.0 23.1 %attend_backward.3.refs_1_.high_ref = bf16[2048,384]{1,0:T(8,128)(2,1)} custom-call(f32[2]{0:T(128)} %get-tuple-element.161.slope_ref, bf16[2048,768]{1,0:T(8,128)(2,1)} %get-tuple-element.67.q_ref.k_ref.v_ref, bf16[2048,768]{1,0:T(8,128)(2,1)} %get-tuple-element.67.q_ref.k_ref.v_ref, bf16[2048,768]{1,0:T(8,128)(2,1)} %get-tuple-element.67.q_ref.k_ref.v_ref, ...), custom_call_target="tpu_custom_call" | custom-call | flops 2200000000 | tf_op jit(solution)/shard_map/attend_backward/pallas_call | solution.py:170
  293.5 3.0 add_convert_fusion
  297.8 1.4 collective-permute-start.34
  299.8 1.5 collective-permute-start.36
  301.3 2.3 collective-permute-done.31.refs_2_
  303.6 3.6 convert_add_fusion.refs_0_
  307.2 1.6 copy-done.3
  310.9 12.6 %input_grad.1 = (bf16[2048,1024]{1,0:T(8,128)(2,1)}, bf16[1024,768]{1,0:T(8,128)(2,1)}, f32[8,1024]{1,0:T(8,128)}, f32[8,768]{1,0:T(8,128)}) custom-call(bf16[2048,384]{1,0:T(8,128)(2,1)} %attend_backward.2.refs_0_.low_ref, bf16[2048,384]{1,0:T(8,128)(2,1)} %attend_backward.3.refs_1_.high_ref, bf16[1024,768]{1,0:T(8,128)(2,1)} %get-tuple-element.99.w_ref, ...), custom_call_target="tpu_custom_call" | custom-call | flops 1000000000 | tf_op jit(solution)/shard_map/input_grad/pallas_call | solution.py:535
  325.5 2.2 fusion.12
  327.7 4.8 %all-to-all-start.2 = ((bf16[4,512,1024]{2,1,0:T(8,128)(2,1)}), bf16[4,512,1024]{2,1,0:T(8,128)(2,1)}, u32[]{:S(2)}, u32[]{:S(2)}) async-start(bf16[4,512,1024]{2,1,0:T(8,128)(2,1)} %bitcast.297), calls=%async_computation.2 | async-start | bytes 8388608 | tf_op jit(solution)/shard_map/all_to_all | solution.py:1064
  332.6 1.8 convert_add_fusion.2
  336.1 1.4 copy-done.15
  337.5 1.4 convert_add_fusion.1
  341.8 1.3 fusion.9
  344.3 9.7 %collective-permute-done.38 = bf16[2,4,40,768]{3,2,1,0:T(8,128)(2,1)S(1)} collective-permute-done((bf16[2,4,40,768]{3,2,1,0:T(8,128)(2,1)}, bf16[2,4,40,768]{3,2,1,0:T(8,128)(2,1)S(1)}, u32[]{:S(2)}, u32[]{:S(2)}) %collective-permute-start.38) | collective-permute-done | bytes 491552 | tf_op jit(solution)/shard_map/ppermute | solution.py:331
  354.1 3.3 collective-permute-start.39
  357.5 3.1 fusion.10
  360.5 8.2 %collective-permute-done.39 = bf16[1,4,40,768]{3,2,1,0:T(8,128)(2,1)S(1)} collective-permute-done((bf16[1,4,40,768]{3,2,1,0:T(8,128)(2,1)S(1)}, bf16[1,4,40,768]{3,2,1,0:T(8,128)(2,1)S(1)}, u32[]{:S(2)}, u32[]{:S(2)}) %collective-permute-start.39) | collective-permute-done | bytes 245792 | tf_op jit(solution)/shard_map/ppermute | solution.py:331
  369.4 2.9 collective-permute-start.44
  372.4 1.4 collective-permute-start.40
  373.7 1.5 collective-permute-start.41
  376.7 5.8 %collective-permute-done.40 = bf16[1,40,768]{2,1,0:T(8,128)(2,1)S(1)} collective-permute-done((bf16[1,40,768]{2,1,0:T(8,128)(2,1)S(1)}, bf16[1,40,768]{2,1,0:T(8,128)(2,1)S(1)}, u32[]{:S(2)}, u32[]{:S(2)}) %collective-permute-start.40) | collective-permute-done | bytes 61472 | tf_op jit(solution)/shard_map/ppermute | solution.py:331
  382.6 1.8 collective-permute-done.42
  387.0 3.4 convert_reduce_fusion
  392.0 2.0 fusion.7.refs_2_
  394.1 4.0 collective-permute-done.44.refs_1_
  (294 shorter events, 57.3 us)
Async XLA Ops:
  0.6 12.1 %copy-start.44 = (bf16[32]{0:T(256)(128)(2,1)S(1)}, bf16[32]{0:T(256)(128)(2,1)}, u32[]{:S(2)}) copy-start(bf16[32]{0:T(256)(128)(2,1)} %param.18) | copy-start | bytes 196
  0.7 12.1 %copy-start.42 = (bf16[32]{0:T(256)(128)(2,1)S(1)}, bf16[32]{0:T(256)(128)(2,1)}, u32[]{:S(2)}) copy-start(bf16[32]{0:T(256)(128)(2,1)} %param.19) | copy-start | bytes 196
  0.7 12.1 %copy-start.41 = (bf16[64]{0:T(256)(128)(2,1)S(1)}, bf16[64]{0:T(256)(128)(2,1)}, u32[]{:S(2)}) copy-start(bf16[64]{0:T(256)(128)(2,1)} %param.21) | copy-start | bytes 388
  0.7 12.0 %copy-start.40 = (bf16[32]{0:T(256)(128)(2,1)S(1)}, bf16[32]{0:T(256)(128)(2,1)}, u32[]{:S(2)}) copy-start(bf16[32]{0:T(256)(128)(2,1)} %param.23) | copy-start | bytes 196
  0.7 12.0 %copy-start.39 = (bf16[32]{0:T(256)(128)(2,1)S(1)}, bf16[32]{0:T(256)(128)(2,1)}, u32[]{:S(2)}) copy-start(bf16[32]{0:T(256)(128)(2,1)} %param.24) | copy-start | bytes 196
  0.7 11.9 %copy-start.38 = (bf16[32]{0:T(256)(128)(2,1)S(1)}, bf16[32]{0:T(256)(128)(2,1)}, u32[]{:S(2)}) copy-start(bf16[32]{0:T(256)(128)(2,1)} %param.25) | copy-start | bytes 196
  0.7 12.1 %copy-start.36 = (bf16[128]{0:T(256)(128)(2,1)S(1)}, bf16[128]{0:T(256)(128)(2,1)}, u32[]{:S(2)}) copy-start(bf16[128]{0:T(256)(128)(2,1)} %param.27) | copy-start | bytes 772
  0.7 11.9 %copy-start.37 = (bf16[32]{0:T(256)(128)(2,1)S(1)}, bf16[32]{0:T(256)(128)(2,1)}, u32[]{:S(2)}) copy-start(bf16[32]{0:T(256)(128)(2,1)} %param.29) | copy-start | bytes 196
  2.4 31.1 %collective-permute-start = (bf16[512,1024]{1,0:T(8,128)(2,1)}, bf16[512,1024]{1,0:T(8,128)(2,1)S(1)}, u32[]{:S(2)}, u32[]{:S(2)}) collective-permute-start(bf16[512,1024]{1,0:T(8,128)(2,1)} %bitcast.276), channel_id=1, source_target_pairs={{0,8},{8,0},{16,24},{24,16},{1,9},{9,1},{17,25},{25,17},{2,10},{10... | collective-permute-start | bytes 3145736 | tf_op jit(solution)/shard_map/ppermute | solution.py:331
  5.4 26.4 %collective-permute-start.1 = (bf16[512,1024]{1,0:T(8,128)(2,1)}, bf16[512,1024]{1,0:T(8,128)(2,1)S(1)}, u32[]{:S(2)}, u32[]{:S(2)}) collective-permute-start(bf16[512,1024]{1,0:T(8,128)(2,1)} %bitcast.277), channel_id=1, source_target_pairs={{0,16},{8,24},{16,0},{24,8},{1,17},{9,25},{17,1},{25,9},{2,18},{10... | collective-permute-start | bytes 3145736 | tf_op jit(solution)/shard_map/ppermute | solution.py:331
  8.7 16.8 %collective-permute-start.4 = (bf16[1,32,5120]{2,1,0:T(8,128)(2,1)S(1)}, bf16[1,32,5120]{2,1,0:T(8,128)(2,1)S(1)}, u32[]{:S(2)}, u32[]{:S(2)}) collective-permute-start(bf16[1,32,5120]{2,1,0:T(8,128)(2,1)S(1)} %bitcast.309), channel_id=1, source_target_pairs={{0,4},{2,6},{4,0},{6,2},{1,5},{3,7},{5,1},{7,3},{8,12},{10,14},{12... | collective-permute-start | bytes 983048 | tf_op jit(solution)/shard_map/ppermute | solution.py:331
  27.4 4.3 %collective-permute-start.5 = (bf16[1,40,768]{2,1,0:T(8,128)(2,1)S(1)}, bf16[1,40,768]{2,1,0:T(8,128)(2,1)S(1)}, u32[]{:S(2)}, u32[]{:S(2)}) collective-permute-start(bf16[1,40,768]{2,1,0:T(8,128)(2,1)S(1)} %get-tuple-element.142), channel_id=1, source_target_pairs={{0,8},{8,0},{16,24},{24,16},{1,9},{9,1},{17,25},{25,17},{2,10},{10... | collective-permute-start | bytes 184328 | tf_op jit(solution)/shard_map/ppermute | solution.py:331
  28.0 7.9 %collective-permute-start.6 = (bf16[1,40,768]{2,1,0:T(8,128)(2,1)S(1)}, bf16[1,40,768]{2,1,0:T(8,128)(2,1)S(1)}, u32[]{:S(2)}, u32[]{:S(2)}) collective-permute-start(bf16[1,40,768]{2,1,0:T(8,128)(2,1)S(1)} %get-tuple-element.141), channel_id=1, source_target_pairs={{0,16},{8,24},{16,0},{24,8},{1,17},{9,25},{17,1},{25,9},{2,18},{10... | collective-permute-start | bytes 184328 | tf_op jit(solution)/shard_map/ppermute | solution.py:331
  28.4 7.4 %collective-permute-start.7 = (bf16[1,40,768]{2,1,0:T(8,128)(2,1)S(1)}, bf16[1,40,768]{2,1,0:T(8,128)(2,1)S(1)}, u32[]{:S(2)}, u32[]{:S(2)}) collective-permute-start(bf16[1,40,768]{2,1,0:T(8,128)(2,1)S(1)} %get-tuple-element.140), channel_id=1, source_target_pairs={{0,24},{8,16},{16,8},{24,0},{1,25},{9,17},{17,9},{25,1},{2,26},{10... | collective-permute-start | bytes 184328 | tf_op jit(solution)/shard_map/ppermute | solution.py:331
  32.7 17.7 %collective-permute-start.2 = (bf16[256,1024]{1,0:T(8,128)(2,1)}, bf16[256,1024]{1,0:T(8,128)(2,1)S(1)}, u32[]{:S(2)}, u32[]{:S(2)}) collective-permute-start(bf16[256,1024]{1,0:T(8,128)(2,1)} %slice.311), channel_id=1, source_target_pairs={{0,8},{8,0},{16,24},{24,16},{1,9},{9,1},{17,25},{25,17},{2,10},{10... | collective-permute-start | bytes 1572872 | tf_op jit(solution)/shard_map/ppermute | solution.py:331
  34.5 15.9 %collective-permute-start.3 = (bf16[256,1024]{1,0:T(8,128)(2,1)}, bf16[256,1024]{1,0:T(8,128)(2,1)}, u32[]{:S(2)}, u32[]{:S(2)}) collective-permute-start(bf16[256,1024]{1,0:T(8,128)(2,1)} %slice.312), channel_id=1, source_target_pairs={{0,16},{8,24},{16,0},{24,8},{1,17},{9,25},{17,1},{25,9},{2,18},{10... | collective-permute-start | bytes 1572872 | tf_op jit(solution)/shard_map/ppermute | solution.py:331
  36.6 12.0 %collective-permute-start.8 = (bf16[1,4,40,768]{3,2,1,0:T(8,128)(2,1)}, bf16[1,4,40,768]{3,2,1,0:T(8,128)(2,1)S(1)}, u32[]{:S(2)}, u32[]{:S(2)}) collective-permute-start(bf16[1,4,40,768]{3,2,1,0:T(8,128)(2,1)} %bitcast.307), channel_id=1, source_target_pairs={{0,4},{2,6},{4,0},{6,2},{1,5},{3,7},{5,1},{7,3},{8,12},{10,14},{12... | collective-permute-start | bytes 737288 | tf_op jit(solution)/shard_map/ppermute | solution.py:331
  51.2 18.1 %copy-start.12 = (bf16[2,4,40,768]{3,2,1,0:T(8,128)(2,1)S(1)}, bf16[2,4,40,768]{3,2,1,0:T(8,128)(2,1)}, u32[]{:S(2)}) copy-start(bf16[2,4,40,768]{3,2,1,0:T(8,128)(2,1)} %after.17.refs_1_) | copy-start | bytes 1474564
  51.2 18.1 %collective-permute-start.9 = (bf16[2,4,40,768]{3,2,1,0:T(8,128)(2,1)}, bf16[2,4,40,768]{3,2,1,0:T(8,128)(2,1)S(1)}, u32[]{:S(2)}, u32[]{:S(2)}) collective-permute-start(bf16[2,4,40,768]{3,2,1,0:T(8,128)(2,1)} %after.17.refs_1_), channel_id=1, source_target_pairs={{0,2},{2,0},{4,6},{6,4},{1,3},{3,1},{5,7},{7,5},{8,10},{10,8},{12,... | collective-permute-start | bytes 1474568 | tf_op jit(solution)/shard_map/ppermute | solution.py:331
  52.0 20.7 %collective-permute-start.13 = (bf16[2,32,5120]{2,1,0:T(8,128)(2,1)}, bf16[2,32,5120]{2,1,0:T(8,128)(2,1)}, u32[]{:S(2)}, u32[]{:S(2)}) collective-permute-start(bf16[2,32,5120]{2,1,0:T(8,128)(2,1)} %after.19), channel_id=1, source_target_pairs={{0,8},{8,0},{16,24},{24,16},{1,9},{9,1},{17,25},{25,17},{2,10},{10... | collective-permute-start | bytes 1966088 | tf_op jit(solution)/shard_map/ppermute | solution.py:331
  52.5 30.2 %collective-permute-start.14 = (bf16[2,32,5120]{2,1,0:T(8,128)(2,1)}, bf16[2,32,5120]{2,1,0:T(8,128)(2,1)}, u32[]{:S(2)}, u32[]{:S(2)}) collective-permute-start(bf16[2,32,5120]{2,1,0:T(8,128)(2,1)} %after.19), channel_id=1, source_target_pairs={{0,16},{8,24},{16,0},{24,8},{1,17},{9,25},{17,1},{25,9},{2,18},{10... | collective-permute-start | bytes 1966088 | tf_op jit(solution)/shard_map/ppermute | solution.py:331
  53.0 29.7 %collective-permute-start.15 = (bf16[2,32,5120]{2,1,0:T(8,128)(2,1)}, bf16[2,32,5120]{2,1,0:T(8,128)(2,1)}, u32[]{:S(2)}, u32[]{:S(2)}) collective-permute-start(bf16[2,32,5120]{2,1,0:T(8,128)(2,1)} %after.19), channel_id=1, source_target_pairs={{0,24},{8,16},{16,8},{24,0},{1,25},{9,17},{17,9},{25,1},{2,26},{10... | collective-permute-start | bytes 1966088 | tf_op jit(solution)/shard_map/ppermute | solution.py:331
  55.4 14.1 %copy-start.22 = (bf16[1,128,1024]{2,1,0:T(8,128)(2,1)S(1)}, bf16[1,128,1024]{2,1,0:T(8,128)(2,1)}, u32[]{:S(2)}) copy-start(bf16[1,128,1024]{2,1,0:T(8,128)(2,1)} %after.18) | copy-start | bytes 786436
  55.5 14.1 %collective-permute-start.11 = (bf16[1,128,1024]{2,1,0:T(8,128)(2,1)}, bf16[1,128,1024]{2,1,0:T(8,128)(2,1)S(1)}, u32[]{:S(2)}, u32[]{:S(2)}) collective-permute-start(bf16[1,128,1024]{2,1,0:T(8,128)(2,1)} %after.18), channel_id=1, source_target_pairs={{0,4},{2,6},{4,0},{6,2},{1,5},{3,7},{5,1},{7,3},{8,12},{10,14},{12... | collective-permute-start | bytes 786440 | tf_op jit(solution)/shard_map/ppermute | solution.py:331
  69.4 13.3 %copy-start.9 = (bf16[2,32,5120]{2,1,0:T(8,128)(2,1)S(1)}, bf16[2,32,5120]{2,1,0:T(8,128)(2,1)}, u32[]{:S(2)}) copy-start(bf16[2,32,5120]{2,1,0:T(8,128)(2,1)} %after.19) | copy-start | bytes 1966084
  69.4 17.6 %collective-permute-start.10 = (bf16[4,4,40,768]{3,2,1,0:T(8,128)(2,1)S(1)}, bf16[4,4,40,768]{3,2,1,0:T(8,128)(2,1)S(1)}, u32[]{:S(2)}, u32[]{:S(2)}) collective-permute-start(bf16[4,4,40,768]{3,2,1,0:T(8,128)(2,1)S(1)} %bitcast.300), channel_id=1, source_target_pairs={{0,1},{1,0},{2,3},{3,2},{4,5},{5,4},{6,7},{7,6},{8,9},{9,8},{10,11... | collective-permute-start | bytes 2949128 | tf_op jit(solution)/shard_map/ppermute | solution.py:331
  69.6 16.3 %collective-permute-start.12 = (bf16[2,128,1024]{2,1,0:T(8,128)(2,1)S(1)}, bf16[2,128,1024]{2,1,0:T(8,128)(2,1)S(1)}, u32[]{:S(2)}, u32[]{:S(2)}) collective-permute-start(bf16[2,128,1024]{2,1,0:T(8,128)(2,1)S(1)} %get-tuple-element.136), channel_id=1, source_target_pairs={{0,2},{2,0},{4,6},{6,4},{1,3},{3,1},{5,7},{7,5},{8,10},{10,8},{12,... | collective-permute-start | bytes 1572872 | tf_op jit(solution)/shard_map/ppermute | solution.py:331
  88.6 31.5 %collective-permute-start.16 = (bf16[8,32,5120]{2,1,0:T(8,128)(2,1)}, bf16[8,32,5120]{2,1,0:T(8,128)(2,1)}, u32[]{:S(2)}, u32[]{:S(2)}) collective-permute-start(bf16[8,32,5120]{2,1,0:T(8,128)(2,1)} %after.21.refs_1_.refs_0_.refs_8_), channel_id=1, source_target_pairs={{0,1},{1,0},{2,3},{3,2},{4,5},{5,4},{6,7},{7,6},{8,9},{9,8},{10,11... | collective-permute-start | bytes 7864328 | tf_op jit(solution)/shard_map/ppermute | solution.py:331
  88.7 59.6 %collective-permute-start.17 = (bf16[8,32,5120]{2,1,0:T(8,128)(2,1)}, bf16[8,32,5120]{2,1,0:T(8,128)(2,1)}, u32[]{:S(2)}, u32[]{:S(2)}) collective-permute-start(bf16[8,32,5120]{2,1,0:T(8,128)(2,1)} %after.21.refs_1_.refs_0_.refs_8_), channel_id=1, source_target_pairs={{0,2},{2,0},{4,6},{6,4},{1,3},{3,1},{5,7},{7,5},{8,10},{10,8},{12,... | collective-permute-start | bytes 7864328 | tf_op jit(solution)/shard_map/ppermute | solution.py:331
  90.3 47.8 %collective-permute-start.18 = (bf16[4,128,1024]{2,1,0:T(8,128)(2,1)S(1)}, bf16[4,128,1024]{2,1,0:T(8,128)(2,1)S(1)}, u32[]{:S(2)}, u32[]{:S(2)}) collective-permute-start(bf16[4,128,1024]{2,1,0:T(8,128)(2,1)S(1)} %copy-done.1), channel_id=1, source_target_pairs={{0,8},{8,0},{16,24},{24,16},{1,9},{9,1},{17,25},{25,17},{2,10},{10... | collective-permute-start | bytes 3145736 | tf_op jit(solution)/shard_map/ppermute | solution.py:331
  91.9 47.6 %collective-permute-start.19 = (bf16[4,128,1024]{2,1,0:T(8,128)(2,1)S(1)}, bf16[4,128,1024]{2,1,0:T(8,128)(2,1)}, u32[]{:S(2)}, u32[]{:S(2)}) collective-permute-start(bf16[4,128,1024]{2,1,0:T(8,128)(2,1)S(1)} %copy-done.1), channel_id=1, source_target_pairs={{0,16},{8,24},{16,0},{24,8},{1,17},{9,25},{17,1},{25,9},{2,18},{10... | collective-permute-start | bytes 3145736 | tf_op jit(solution)/shard_map/ppermute | solution.py:331
  92.4 47.1 %collective-permute-start.20 = (bf16[4,128,1024]{2,1,0:T(8,128)(2,1)S(1)}, bf16[4,128,1024]{2,1,0:T(8,128)(2,1)}, u32[]{:S(2)}, u32[]{:S(2)}) collective-permute-start(bf16[4,128,1024]{2,1,0:T(8,128)(2,1)S(1)} %copy-done.1), channel_id=1, source_target_pairs={{0,24},{8,16},{16,8},{24,0},{1,25},{9,17},{17,9},{25,1},{2,26},{10... | collective-permute-start | bytes 3145736 | tf_op jit(solution)/shard_map/ppermute | solution.py:331
  120.1 11.8 %copy-start.33 = (bf16[2048,128]{1,0:T(8,128)(2,1)S(1)}, bf16[2048,128]{1,0:T(8,128)(2,1)}, u32[]{:S(2)}) copy-start(bf16[2048,128]{1,0:T(8,128)(2,1)} %get-tuple-element.68) | copy-start | bytes 1572868
  134.0 17.5 %all-to-all-start = ((bf16[4,512,256]{2,1,0:T(8,128)(2,1)}), bf16[4,512,256]{2,1,0:T(8,128)(2,1)S(1)}, u32[]{:S(2)}, u32[]{:S(2)}) async-start(bf16[4,512,256]{2,1,0:T(8,128)(2,1)} %bitcast.37), calls=%async_computation | async-start | bytes 2097152 | tf_op jit(solution)/shard_map/all_to_all | solution.py:1064
  138.1 15.5 %copy-start.43 = (s32[16]{0:T(128)S(1)}, s32[16]{0:T(128)}, u32[]{:S(2)}) copy-start(s32[16]{0:T(128)} %constant.105.clone) | copy-start | bytes 196
  138.1 13.4 %copy-start.17 = (bf16[4,128,1024]{2,1,0:T(8,128)(2,1)}, bf16[4,128,1024]{2,1,0:T(8,128)(2,1)S(1)}, u32[]{:S(2)}) copy-start(bf16[4,128,1024]{2,1,0:T(8,128)(2,1)S(1)} %collective-permute-done.18.refs_2_) | copy-start | bytes 3145732
  152.5 9.0 %collective-permute-start.21 = (bf16[8,32,5120]{2,1,0:T(8,128)(2,1)}, bf16[8,32,5120]{2,1,0:T(8,128)(2,1)}, u32[]{:S(2)}, u32[]{:S(2)}) collective-permute-start(bf16[8,32,5120]{2,1,0:T(8,128)(2,1)} %get-tuple-element.71.refs_1_.refs_9_), channel_id=1, source_target_pairs={{0,1},{1,0},{2,3},{3,2},{4,5},{5,4},{6,7},{7,6},{8,9},{9,8},{10,11... | collective-permute-start | bytes 7864328 | tf_op jit(solution)/shard_map/ppermute | solution.py:331
  152.5 14.7 %collective-permute-start.22 = (bf16[4,128,1024]{2,1,0:T(8,128)(2,1)}, bf16[4,128,1024]{2,1,0:T(8,128)(2,1)S(1)}, u32[]{:S(2)}, u32[]{:S(2)}) collective-permute-start(bf16[4,128,1024]{2,1,0:T(8,128)(2,1)} %get-tuple-element.74.refs_0_), channel_id=1, source_target_pairs={{0,1},{1,0},{2,3},{3,2},{4,5},{5,4},{6,7},{7,6},{8,9},{9,8},{10,11... | collective-permute-start | bytes 3145736 | tf_op jit(solution)/shard_map/ppermute | solution.py:331
  153.0 14.2 %collective-permute-start.23 = (bf16[4,128,1024]{2,1,0:T(8,128)(2,1)}, bf16[4,128,1024]{2,1,0:T(8,128)(2,1)S(1)}, u32[]{:S(2)}, u32[]{:S(2)}) collective-permute-start(bf16[4,128,1024]{2,1,0:T(8,128)(2,1)} %get-tuple-element.75.refs_1_), channel_id=1, source_target_pairs={{0,1},{1,0},{2,3},{3,2},{4,5},{5,4},{6,7},{7,6},{8,9},{9,8},{10,11... | collective-permute-start | bytes 3145736 | tf_op jit(solution)/shard_map/ppermute | solution.py:331
  153.0 14.3 %collective-permute-start.24 = (bf16[4,128,1024]{2,1,0:T(8,128)(2,1)}, bf16[4,128,1024]{2,1,0:T(8,128)(2,1)S(1)}, u32[]{:S(2)}, u32[]{:S(2)}) collective-permute-start(bf16[4,128,1024]{2,1,0:T(8,128)(2,1)} %get-tuple-element.76.refs_2_), channel_id=1, source_target_pairs={{0,1},{1,0},{2,3},{3,2},{4,5},{5,4},{6,7},{7,6},{8,9},{9,8},{10,11... | collective-permute-start | bytes 3145736 | tf_op jit(solution)/shard_map/ppermute | solution.py:331
  153.5 13.8 %collective-permute-start.25 = (bf16[4,128,1024]{2,1,0:T(8,128)(2,1)}, bf16[4,128,1024]{2,1,0:T(8,128)(2,1)}, u32[]{:S(2)}, u32[]{:S(2)}) collective-permute-start(bf16[4,128,1024]{2,1,0:T(8,128)(2,1)} %get-tuple-element.77.refs_3_), channel_id=1, source_target_pairs={{0,1},{1,0},{2,3},{3,2},{4,5},{5,4},{6,7},{7,6},{8,9},{9,8},{10,11... | collective-permute-start | bytes 3145736 | tf_op jit(solution)/shard_map/ppermute | solution.py:331
  210.0 14.9 %collective-permute-start.26 = (bf16[16,128,1024]{2,1,0:T(8,128)(2,1)}, bf16[16,128,1024]{2,1,0:T(8,128)(2,1)}, u32[]{:S(2)}, u32[]{:S(2)}) collective-permute-start(bf16[16,128,1024]{2,1,0:T(8,128)(2,1)} %get-tuple-element.84), channel_id=1, source_target_pairs={{0,1},{1,0},{2,3},{3,2},{4,5},{5,4},{6,7},{7,6},{8,9},{9,8},{10,11... | collective-permute-start | bytes 12582920 | tf_op jit(solution)/shard_map/ppermute | solution.py:331
  210.2 14.7 %collective-permute-start.28 = (bf16[16,32,4096]{2,1,0:T(8,128)(2,1)}, bf16[16,32,4096]{2,1,0:T(8,128)(2,1)}, u32[]{:S(2)}, u32[]{:S(2)}) collective-permute-start(bf16[16,32,4096]{2,1,0:T(8,128)(2,1)} %get-tuple-element.88), channel_id=1, source_target_pairs={{0,1},{1,0},{2,3},{3,2},{4,5},{5,4},{6,7},{7,6},{8,9},{9,8},{10,11... | collective-permute-start | bytes 12582920 | tf_op jit(solution)/shard_map/ppermute | solution.py:331
  220.2 4.7 %collective-permute-start.27 = (bf16[16,32,1024]{2,1,0:T(8,128)(2,1)}, bf16[16,32,1024]{2,1,0:T(8,128)(2,1)S(1)}, u32[]{:S(2)}, u32[]{:S(2)}) collective-permute-start(bf16[16,32,1024]{2,1,0:T(8,128)(2,1)} %get-tuple-element.86), channel_id=1, source_target_pairs={{0,1},{1,0},{2,3},{3,2},{4,5},{5,4},{6,7},{7,6},{8,9},{9,8},{10,11... | collective-permute-start | bytes 3145736 | tf_op jit(solution)/shard_map/ppermute | solution.py:331
  220.4 18.1 %all-to-all-start.1 = ((bf16[4,512,256]{2,1,0:T(8,128)(2,1)}), bf16[4,512,256]{2,1,0:T(8,128)(2,1)S(1)}, u32[]{:S(2)}, u32[]{:S(2)}) async-start(bf16[4,512,256]{2,1,0:T(8,128)(2,1)} %get-tuple-element.81), calls=%async_computation.1 | async-start | bytes 2097152 | tf_op jit(solution)/shard_map/all_to_all | solution.py:1064
  239.5 52.7 %collective-permute-start.32 = (bf16[8,32,4096]{2,1,0:T(8,128)(2,1)}, bf16[8,32,4096]{2,1,0:T(8,128)(2,1)S(1)}, u32[]{:S(2)}, u32[]{:S(2)}) collective-permute-start(bf16[8,32,4096]{2,1,0:T(8,128)(2,1)} %get-tuple-element.105), channel_id=1, source_target_pairs={{0,2},{2,0},{4,6},{6,4},{1,3},{3,1},{5,7},{7,5},{8,10},{10,8},{12,... | collective-permute-start | bytes 6291464 | tf_op jit(solution)/shard_map/ppermute | solution.py:331
  242.4 57.3 %collective-permute-start.29 = (bf16[4,160,1024]{2,1,0:T(8,128)(2,1)}, bf16[4,160,1024]{2,1,0:T(8,128)(2,1)}, u32[]{:S(2)}, u32[]{:S(2)}) collective-permute-start(bf16[4,160,1024]{2,1,0:T(8,128)(2,1)} %get-tuple-element.102), channel_id=1, source_target_pairs={{0,8},{8,0},{16,24},{24,16},{1,9},{9,1},{17,25},{25,17},{2,10},{10... | collective-permute-start | bytes 3932168 | tf_op jit(solution)/shard_map/ppermute | solution.py:331
  243.9 57.3 %collective-permute-start.30 = (bf16[4,160,1024]{2,1,0:T(8,128)(2,1)}, bf16[4,160,1024]{2,1,0:T(8,128)(2,1)}, u32[]{:S(2)}, u32[]{:S(2)}) collective-permute-start(bf16[4,160,1024]{2,1,0:T(8,128)(2,1)} %get-tuple-element.103), channel_id=1, source_target_pairs={{0,16},{8,24},{16,0},{24,8},{1,17},{9,25},{17,1},{25,9},{2,18},{10... | collective-permute-start | bytes 3932168 | tf_op jit(solution)/shard_map/ppermute | solution.py:331
  244.5 59.1 %collective-permute-start.31 = (bf16[4,160,1024]{2,1,0:T(8,128)(2,1)}, bf16[4,160,1024]{2,1,0:T(8,128)(2,1)}, u32[]{:S(2)}, u32[]{:S(2)}) collective-permute-start(bf16[4,160,1024]{2,1,0:T(8,128)(2,1)} %get-tuple-element.104), channel_id=1, source_target_pairs={{0,24},{8,16},{16,8},{24,0},{1,25},{9,17},{17,9},{25,1},{2,26},{10... | collective-permute-start | bytes 3932168 | tf_op jit(solution)/shard_map/ppermute | solution.py:331
  297.8 34.8 %collective-permute-start.34 = (bf16[2,32,4096]{2,1,0:T(8,128)(2,1)}, bf16[2,32,4096]{2,1,0:T(8,128)(2,1)}, u32[]{:S(2)}, u32[]{:S(2)}) collective-permute-start(bf16[2,32,4096]{2,1,0:T(8,128)(2,1)} %get-tuple-element.130), channel_id=1, source_target_pairs={{0,8},{8,0},{16,24},{24,16},{1,9},{9,1},{17,25},{25,17},{2,10},{10... | collective-permute-start | bytes 1572872 | tf_op jit(solution)/shard_map/ppermute | solution.py:331
  299.2 33.4 %collective-permute-start.35 = (bf16[2,32,4096]{2,1,0:T(8,128)(2,1)}, bf16[2,32,4096]{2,1,0:T(8,128)(2,1)}, u32[]{:S(2)}, u32[]{:S(2)}) collective-permute-start(bf16[2,32,4096]{2,1,0:T(8,128)(2,1)} %get-tuple-element.129), channel_id=1, source_target_pairs={{0,16},{8,24},{16,0},{24,8},{1,17},{9,25},{17,1},{25,9},{2,18},{10... | collective-permute-start | bytes 1572872 | tf_op jit(solution)/shard_map/ppermute | solution.py:331
  299.8 32.8 %collective-permute-start.36 = (bf16[2,32,4096]{2,1,0:T(8,128)(2,1)}, bf16[2,32,4096]{2,1,0:T(8,128)(2,1)}, u32[]{:S(2)}, u32[]{:S(2)}) collective-permute-start(bf16[2,32,4096]{2,1,0:T(8,128)(2,1)} %get-tuple-element.128), channel_id=1, source_target_pairs={{0,24},{8,16},{16,8},{24,0},{1,25},{9,17},{17,9},{25,1},{2,26},{10... | collective-permute-start | bytes 1572872 | tf_op jit(solution)/shard_map/ppermute | solution.py:331
  309.7 26.4 %collective-permute-start.37 = (bf16[2,160,1024]{2,1,0:T(8,128)(2,1)}, bf16[2,160,1024]{2,1,0:T(8,128)(2,1)}, u32[]{:S(2)}, u32[]{:S(2)}) collective-permute-start(bf16[2,160,1024]{2,1,0:T(8,128)(2,1)} %fusion.17), channel_id=1, source_target_pairs={{0,2},{2,0},{4,6},{6,4},{1,3},{3,1},{5,7},{7,5},{8,10},{10,8},{12,... | collective-permute-start | bytes 1966088 | tf_op jit(solution)/shard_map/ppermute | solution.py:331
  327.7 8.4 %collective-permute-start.33 = (bf16[4,4,40,768]{3,2,1,0:T(8,128)(2,1)}, bf16[4,4,40,768]{3,2,1,0:T(8,128)(2,1)}, u32[]{:S(2)}, u32[]{:S(2)}) collective-permute-start(bf16[4,4,40,768]{3,2,1,0:T(8,128)(2,1)} %fusion.12), channel_id=1, source_target_pairs={{0,1},{1,0},{2,3},{3,2},{4,5},{5,4},{6,7},{7,6},{8,9},{9,8},{10,11... | collective-permute-start | bytes 2949128 | tf_op jit(solution)/shard_map/ppermute | solution.py:331
  327.7 59.3 %all-to-all-start.2 = ((bf16[4,512,1024]{2,1,0:T(8,128)(2,1)}), bf16[4,512,1024]{2,1,0:T(8,128)(2,1)}, u32[]{:S(2)}, u32[]{:S(2)}) async-start(bf16[4,512,1024]{2,1,0:T(8,128)(2,1)} %bitcast.297), calls=%async_computation.2 | async-start | bytes 8388608 | tf_op jit(solution)/shard_map/all_to_all | solution.py:1064
  340.2 13.8 %collective-permute-start.38 = (bf16[2,4,40,768]{3,2,1,0:T(8,128)(2,1)}, bf16[2,4,40,768]{3,2,1,0:T(8,128)(2,1)S(1)}, u32[]{:S(2)}, u32[]{:S(2)}) collective-permute-start(bf16[2,4,40,768]{3,2,1,0:T(8,128)(2,1)} %fusion.20), channel_id=1, source_target_pairs={{0,2},{2,0},{4,6},{6,4},{1,3},{3,1},{5,7},{7,5},{8,10},{10,8},{12,... | collective-permute-start | bytes 1474568 | tf_op jit(solution)/shard_map/ppermute | solution.py:331
  344.3 9.7 %copy-start.8 = (f32[4,4,40,768]{3,2,1,0:T(8,128)S(1)}, f32[4,4,40,768]{3,2,1,0:T(8,128)}, u32[]{:S(2)}) copy-start(f32[4,4,40,768]{3,2,1,0:T(8,128)} %copy-done.7) | copy-start | bytes 5898244
  344.3 13.2 %copy-start.10 = (f32[512,1024]{1,0:T(8,128)S(1)}, f32[512,1024]{1,0:T(8,128)}, u32[]{:S(2)}) copy-start(f32[512,1024]{1,0:T(8,128)} %after.27) | copy-start | bytes 6291460
  354.1 14.6 %collective-permute-start.39 = (bf16[1,4,40,768]{3,2,1,0:T(8,128)(2,1)S(1)}, bf16[1,4,40,768]{3,2,1,0:T(8,128)(2,1)S(1)}, u32[]{:S(2)}, u32[]{:S(2)}) collective-permute-start(bf16[1,4,40,768]{3,2,1,0:T(8,128)(2,1)S(1)} %fusion.27), channel_id=1, source_target_pairs={{0,4},{2,6},{4,0},{6,2},{1,5},{3,7},{5,1},{7,3},{8,12},{10,14},{12... | collective-permute-start | bytes 737288 | tf_op jit(solution)/shard_map/ppermute | solution.py:331
  369.4 28.6 %collective-permute-start.43 = (bf16[160,1024]{1,0:T(8,128)(2,1)}, bf16[160,1024]{1,0:T(8,128)(2,1)S(1)}, u32[]{:S(2)}, u32[]{:S(2)}) collective-permute-start(bf16[160,1024]{1,0:T(8,128)(2,1)} %get-tuple-element.116), channel_id=1, source_target_pairs={{0,4},{2,6},{4,0},{6,2},{1,5},{3,7},{5,1},{7,3},{8,12},{10,14},{12... | collective-permute-start | bytes 983048 | tf_op jit(solution)/shard_map/ppermute | solution.py:331
  369.4 28.6 %collective-permute-start.44 = (bf16[32,4096]{1,0:T(8,128)(2,1)}, bf16[32,4096]{1,0:T(8,128)(2,1)S(1)}, u32[]{:S(2)}, u32[]{:S(2)}) collective-permute-start(bf16[32,4096]{1,0:T(8,128)(2,1)} %get-tuple-element.117), channel_id=1, source_target_pairs={{0,4},{2,6},{4,0},{6,2},{1,5},{3,7},{5,1},{7,3},{8,12},{10,14},{12... | collective-permute-start | bytes 786440 | tf_op jit(solution)/shard_map/ppermute | solution.py:331
  372.4 10.2 %collective-permute-start.40 = (bf16[1,40,768]{2,1,0:T(8,128)(2,1)S(1)}, bf16[1,40,768]{2,1,0:T(8,128)(2,1)S(1)}, u32[]{:S(2)}, u32[]{:S(2)}) collective-permute-start(bf16[1,40,768]{2,1,0:T(8,128)(2,1)S(1)} %get-tuple-element.139), channel_id=1, source_target_pairs={{0,8},{8,0},{16,24},{24,16},{1,9},{9,1},{17,25},{25,17},{2,10},{10... | collective-permute-start | bytes 184328 | tf_op jit(solution)/shard_map/ppermute | solution.py:331
  373.7 8.8 %collective-permute-start.41 = (bf16[1,40,768]{2,1,0:T(8,128)(2,1)S(1)}, bf16[1,40,768]{2,1,0:T(8,128)(2,1)S(1)}, u32[]{:S(2)}, u32[]{:S(2)}) collective-permute-start(bf16[1,40,768]{2,1,0:T(8,128)(2,1)S(1)} %get-tuple-element.138), channel_id=1, source_target_pairs={{0,16},{8,24},{16,0},{24,8},{1,17},{9,25},{17,1},{25,9},{2,18},{10... | collective-permute-start | bytes 184328 | tf_op jit(solution)/shard_map/ppermute | solution.py:331
  375.2 9.2 %collective-permute-start.42 = (bf16[1,40,768]{2,1,0:T(8,128)(2,1)S(1)}, bf16[1,40,768]{2,1,0:T(8,128)(2,1)S(1)}, u32[]{:S(2)}, u32[]{:S(2)}) collective-permute-start(bf16[1,40,768]{2,1,0:T(8,128)(2,1)S(1)} %get-tuple-element.137), channel_id=1, source_target_pairs={{0,24},{8,16},{16,8},{24,0},{1,25},{9,17},{17,9},{25,1},{2,26},{10... | collective-permute-start | bytes 184328 | tf_op jit(solution)/shard_map/ppermute | solution.py:331
  (29 other events, 58.0 us)
